TPU v7x, 512 devices: a whole 4x8x8 slice. The times are simulated.
512 devices in a mesh: dp: 32 (over z_hi, y), tensor: 16 (over x, z_lo, core).
Axes of the slice: x: 4, y: 8, z: 8 (z_hi: 4, z_lo: 2; z = z_hi * 2 + z_lo), core: 2. Of those that a mesh axis runs over, the one named last changes fastest.
Arguments:
- hidden: bfloat16 [6144, 14336], P('dp', 'tensor'), may hold values from -6 to 6
- down_rotated: bfloat16 [14336, 4096], P('tensor', 'dp'), may hold values from -0.09375 to 0.09375
- out_gradient: bfloat16 [6144, 4096], P('dp', 'tensor'), may hold values from -6 to 6
- sign_bits: int32 [14336], P('tensor'), may hold values from 0 to 1
- act_exponent: int32 [6144], P('dp'), may hold values from -7 to -3
- grad_exponent: int32 [6144], P('dp'), may hold values from -7 to -3
Outputs:
- mixed: bfloat16 [6144, 4096], P('dp', 'tensor')
- grad_hidden: bfloat16 [6144, 14336], P('dp', 'tensor')
Inputs may be any that keep to these rules, and one draw needn't show every extreme that they name: `sign_bits`: 0 means the sign +1, 1 means -1.
All inputs are finite; a program needn't handle non-finite values.
Results may differ from a plain program's by a relative error of at most 0.028.
Values may be sent and summed in bfloat16 or wider, within the bound.
No kernel may reach another device: no remote copies, remote signals or barrier semaphores. Data moves between devices by JAX's collectives and lax.ppermute only.
A program may use at most 64 MiB of HBM per device.

v0:
```python
import jax
import jax.numpy as jnp
from jax import lax
from jax.sharding import PartitionSpec as P

BLK = 128


def from_partner(value, axis, apart):
    return lax.ppermute(value, axis, [(i, i ^ 1 << apart) for i in range(lax.axis_size(axis))])


def hadamard(order):
    index = jnp.arange(order, dtype=jnp.int32)
    intersection_bits = index[:, None] & index[None, :]
    parity = jnp.zeros((order, order), jnp.int32)
    for bit_number in range(order.bit_length() - 1):
        parity = parity ^ intersection_bits >> bit_number & 1
    return (1 - 2 * parity).astype(jnp.float32)


def local_mix(values):
    count, width = values.shape
    shaped = values.reshape(count, width // BLK, BLK)
    shaped = jnp.einsum("rbk,kj->rbj", shaped, hadamard(BLK), precision=lax.Precision.HIGHEST)
    return shaped.reshape(count, width)


def cross_mix(values):
    groups = lax.axis_size("tensor")
    factor = 1.0 / float(groups * BLK) ** 0.5
    position = lax.axis_index("tensor")
    for bit_number in range(groups.bit_length() - 1):
        partner = from_partner(values.astype(jnp.bfloat16), "tensor", bit_number).astype(
            values.dtype
        )
        is_upper = position >> bit_number & 1 == 1
        values = jnp.where(is_upper, partner - values, values + partner)
    return values * factor


def local(hidden, down_rotated, out_gradient, sign_bits, act_exponent, grad_exponent):
    flips = (1 - 2 * sign_bits).astype(jnp.float32)
    rotated = cross_mix(local_mix(hidden.astype(jnp.float32) * flips[None, :]))
    act_factor = jnp.exp2(act_exponent.astype(jnp.float32))[:, None]
    act_grid = jnp.clip(rotated / act_factor, -127.0, 127.0).astype(jnp.bfloat16)
    grad_factor = jnp.exp2(grad_exponent.astype(jnp.float32))[:, None]
    grad_local = jnp.clip(out_gradient.astype(jnp.float32) / grad_factor, -127.0, 127.0).astype(
        jnp.bfloat16
    )
    grad_grid = lax.all_gather(grad_local, "tensor", axis=1, tiled=True)
    shard_piece = lax.all_gather(down_rotated, "dp", axis=1, tiled=True)
    columns = jnp.dot(act_grid, shard_piece, preferred_element_type=jnp.float32)
    partials = columns
    product = lax.dot_general(
        grad_grid, shard_piece, (((1,), (1,)), ((), ())), preferred_element_type=jnp.float32
    )
    partials, grad_rot = (partials, product)
    terms = lax.optimization_barrier(partials.astype(jnp.bfloat16)).astype(jnp.float32)
    summed = lax.psum_scatter(
        terms.astype(jnp.bfloat16), "tensor", scatter_dimension=1, tiled=True
    ).astype(jnp.float32)
    mixed = (summed * act_factor).astype(jnp.bfloat16)
    grad_rot = grad_rot * grad_factor
    grad_hidden = (local_mix(cross_mix(grad_rot)) * flips[None, :]).astype(jnp.bfloat16)
    return (mixed, grad_hidden)


def solution(mesh):
    in_specs = (
        P("dp", "tensor"),
        P("tensor", "dp"),
        P("dp", "tensor"),
        P("tensor"),
        P("dp"),
        P("dp"),
    )
    out_specs = (P("dp", "tensor"), P("dp", "tensor"))
    return jax.shard_map(local, mesh=mesh, in_specs=in_specs, out_specs=out_specs, check_vma=False)
```

profile of v0, /device:TPU:8, one launch (start us, length us, event | category | flops | bytes accessed | tf_op | source)
XLA Modules:
  0.0 363.9 jit_solution(3895170771111517336)
XLA Ops:
  7.2 0.7 multiply_exponential_fusion
  7.9 1.6 clamp_convert_fusion
  9.6 0.7 all-gather.3.cloned.1.call-update
  10.4 46.0 %all-gather.5.cloned.1.call-done = bf16[192,4096]{1,0:T(8,128)(2,1)} async-done(((bf16[192,256]{1,0:T(8,128)(2,1)}), bf16[192,4096]{1,0:T(8,128)(2,1)}) %all-gather.5.cloned.1.call-update) | async-done | bytes 1572880 | tf_op jit(solution)/shard_map/all_gather | solution.py:51
  56.3 142.8 %all-gather.3.cloned.1.call-done = bf16[896,4096]{1,0:T(8,128)(2,1)} async-done(((bf16[896,128]{1,0:T(8,128)(2,1)}), bf16[896,4096]{1,0:T(8,128)(2,1)}) %all-gather.3.cloned.1.call-update) | async-done | bytes 7340048 | tf_op jit(solution)/shard_map/all_gather | solution.py:52
  199.2 6.1 %fusion.55 = (bf16[192,896]{1,0:T(8,128)(2,1)S(1)}, f32[192,896]{1,0:T(8,128)S(1)}) fusion(f32[192]{0:T(256)S(1)} %multiply_exponential_fusion, bf16[192,4096]{1,0:T(8,128)(2,1)} %all-gather.5.cloned.1.call-done, bf16[896,4096]{1,0:T(8,128)(2,1)} %all-gather.3.cloned.1.call-done), kind=kOutput, calls=%fused_computation.81 | convolution fusion | flops 1409630208 | bytes 9945856 | tf_op jit(solution)/shard_map/dot_general | solution.py:55
  205.3 1.9 collective-permute-start.4
  207.3 1.6 collective-permute-done.4
  208.9 0.1 fusion.20
  209.0 1.9 collective-permute-start.5
  210.9 10.1 %collective-permute-done.5 = bf16[192,896]{1,0:T(8,128)(2,1)S(1)} collective-permute-done((bf16[192,896]{1,0:T(8,128)(2,1)S(1)}, bf16[192,896]{1,0:T(8,128)(2,1)S(1)}, u32[]{:S(2)}, u32[]{:S(2)}) %collective-permute-start.5) | collective-permute-done | bytes 344096 | tf_op jit(solution)/shard_map/ppermute | solution.py:10
  221.0 0.2 fusion.51
  221.2 3.4 collective-permute-start.6
  224.6 7.8 %collective-permute-done.6 = bf16[192,896]{1,0:T(8,128)(2,1)S(1)} collective-permute-done((bf16[192,896]{1,0:T(8,128)(2,1)S(1)}, bf16[192,896]{1,0:T(8,128)(2,1)S(1)}, u32[]{:S(2)}, u32[]{:S(2)}) %collective-permute-start.6) | collective-permute-done | bytes 344096 | tf_op jit(solution)/shard_map/ppermute | solution.py:10
  232.4 4.9 %collective-permute-start.7 = (bf16[192,896]{1,0:T(8,128)(2,1)S(1)}, bf16[192,896]{1,0:T(8,128)(2,1)S(1)}, u32[]{:S(2)}, u32[]{:S(2)}) collective-permute-start(bf16[192,896]{1,0:T(8,128)(2,1)S(1)} %fusion.19), channel_id=1, source_target_pairs={{0,8},{1,9},{2,10},{3,11},{4,12},{5,13},{6,14},{7,15},{8,0},{9,1},... | collective-permute-start | bytes 1032200 | tf_op jit(solution)/shard_map/ppermute | solution.py:10
  237.4 6.8 %collective-permute-done.7 = bf16[192,896]{1,0:T(8,128)(2,1)S(1)} collective-permute-done((bf16[192,896]{1,0:T(8,128)(2,1)S(1)}, bf16[192,896]{1,0:T(8,128)(2,1)S(1)}, u32[]{:S(2)}, u32[]{:S(2)}) %collective-permute-start.7) | collective-permute-done | bytes 344096 | tf_op jit(solution)/shard_map/ppermute | solution.py:10
  244.2 0.9 convolution_bitcast_fusion
  245.1 0.8 fusion.13
  245.9 0.7 convolution_bitcast_fusion.1
  246.7 1.9 collective-permute-start
  248.6 1.6 collective-permute-done
  250.2 0.1 fusion.22
  250.4 2.9 collective-permute-start.1
  253.2 9.1 %collective-permute-done.1 = bf16[192,896]{1,0:T(8,128)(2,1)S(1)} collective-permute-done((bf16[192,896]{1,0:T(8,128)(2,1)S(1)}, bf16[192,896]{1,0:T(8,128)(2,1)S(1)}, u32[]{:S(2)}, u32[]{:S(2)}) %collective-permute-start.1) | collective-permute-done | bytes 344096 | tf_op jit(solution)/shard_map/ppermute | solution.py:10
  262.4 0.2 fusion.53
  262.6 3.4 collective-permute-start.2
  265.9 7.8 %collective-permute-done.2 = bf16[192,896]{1,0:T(8,128)(2,1)S(1)} collective-permute-done((bf16[192,896]{1,0:T(8,128)(2,1)S(1)}, bf16[192,896]{1,0:T(8,128)(2,1)S(1)}, u32[]{:S(2)}, u32[]{:S(2)}) %collective-permute-start.2) | collective-permute-done | bytes 344096 | tf_op jit(solution)/shard_map/ppermute | solution.py:10
  273.8 4.9 %collective-permute-start.3 = (bf16[192,896]{1,0:T(8,128)(2,1)S(1)}, bf16[192,896]{1,0:T(8,128)(2,1)S(1)}, u32[]{:S(2)}, u32[]{:S(2)}) collective-permute-start(bf16[192,896]{1,0:T(8,128)(2,1)S(1)} %fusion.21), channel_id=1, source_target_pairs={{0,8},{1,9},{2,10},{3,11},{4,12},{5,13},{6,14},{7,15},{8,0},{9,1},... | collective-permute-start | bytes 1032200 | tf_op jit(solution)/shard_map/ppermute | solution.py:10
  278.7 6.8 %collective-permute-done.3 = bf16[192,896]{1,0:T(8,128)(2,1)S(1)} collective-permute-done((bf16[192,896]{1,0:T(8,128)(2,1)S(1)}, bf16[192,896]{1,0:T(8,128)(2,1)S(1)}, u32[]{:S(2)}, u32[]{:S(2)}) %collective-permute-start.3) | collective-permute-done | bytes 344096 | tf_op jit(solution)/shard_map/ppermute | solution.py:10
  285.6 6.3 %convolution_convert_fusion = bf16[192,4096]{1,0:T(8,128)(2,1)} fusion(bf16[896,4096]{1,0:T(8,128)(2,1)} %all-gather.3.cloned.1.call-done, bf16[192,896]{1,0:T(8,128)(2,1)S(1)} %collective-permute-done.3, f32[192,896]{1,0:T(8,128)S(1)} %get-tuple-element.5, bf16[192,896]{1,0:T(8,128)(2,1)S(1)} %collective-permute-done.2, ...), kind=kOutput, calls=%fused_computation | convolution fusion | flops 1412136960 | bytes 10289922 | tf_op jit(solution)/shard_map/dot_general | solution.py:53
  291.9 63.8 %reduce-scatter.2.cloned.1.call-done = bf16[192,256]{1,0:T(8,128)(2,1)} async-done(((bf16[192,4096]{1,0:T(8,128)(2,1)}), bf16[192,256]{1,0:T(8,128)(2,1)}) %reduce-scatter.2.cloned.1.call-update) | async-done | bytes 98320 | tf_op jit(solution)/shard_map/reduce_scatter | solution.py:60
  355.7 1.6 multiply_convert_fusion
  (16 shorter events, 0.4 us)
Async XLA Ops:
  7.2 49.2 %all-gather.5.cloned.1.call-start = ((), (), s32[]{:S(2)}) async-start(), calls=%async_computation.3 | async-start | bytes 1671168 | tf_op jit(solution)/shard_map/all_gather | solution.py:51
  9.6 189.6 %all-gather.3.cloned.1.call-start = ((), (), s32[]{:S(2)}) async-start(), calls=%async_computation.1 | async-start | bytes 7569408 | tf_op jit(solution)/shard_map/all_gather | solution.py:52
  10.3 227.0 %copy-start.1 = (s32[896]{0:T(1024)S(1)}, s32[896]{0:T(1024)}, u32[]{:S(2)}) copy-start(s32[896]{0:T(1024)} %param.9) | copy-start | bytes 10756
  10.3 234.7 %copy-start = (bf16[192,896]{1,0:T(8,128)(2,1)S(1)}, bf16[192,896]{1,0:T(8,128)(2,1)}, u32[]{:S(2)}) copy-start(bf16[192,896]{1,0:T(8,128)(2,1)} %param.6) | copy-start | bytes 1032196
  10.3 345.4 %reduce-scatter.2.cloned.1.call-start = ((), (), s32[]{:S(2)}) async-start(), calls=%async_computation.2 | async-start | bytes 1671168 | tf_op jit(solution)/shard_map/reduce_scatter | solution.py:60
  205.3 3.5 collective-permute-start.4
  209.0 12.0 %collective-permute-start.5 = (bf16[192,896]{1,0:T(8,128)(2,1)S(1)}, bf16[192,896]{1,0:T(8,128)(2,1)S(1)}, u32[]{:S(2)}, u32[]{:S(2)}) collective-permute-start(bf16[192,896]{1,0:T(8,128)(2,1)S(1)} %fusion.20), channel_id=1, source_target_pairs={{0,2},{1,3},{2,0},{3,1},{4,6},{5,7},{6,4},{7,5},{8,10},{9,11},{10,... | collective-permute-start | bytes 1032200 | tf_op jit(solution)/shard_map/ppermute | solution.py:10
  210.9 67.8 %copy-start.2 = (s32[192]{0:T(256)S(1)}, s32[192]{0:T(256)}, u32[]{:S(2)}) copy-start(s32[192]{0:T(256)} %param.10) | copy-start | bytes 2308
  221.2 11.2 %collective-permute-start.6 = (bf16[192,896]{1,0:T(8,128)(2,1)S(1)}, bf16[192,896]{1,0:T(8,128)(2,1)S(1)}, u32[]{:S(2)}, u32[]{:S(2)}) collective-permute-start(bf16[192,896]{1,0:T(8,128)(2,1)S(1)} %get-tuple-element.2), channel_id=1, source_target_pairs={{0,4},{1,5},{2,6},{3,7},{4,0},{5,1},{6,2},{7,3},{8,12},{9,13},{10,... | collective-permute-start | bytes 1032200 | tf_op jit(solution)/shard_map/ppermute | solution.py:10
  232.4 11.8 %collective-permute-start.7 = (bf16[192,896]{1,0:T(8,128)(2,1)S(1)}, bf16[192,896]{1,0:T(8,128)(2,1)S(1)}, u32[]{:S(2)}, u32[]{:S(2)}) collective-permute-start(bf16[192,896]{1,0:T(8,128)(2,1)S(1)} %fusion.19), channel_id=1, source_target_pairs={{0,8},{1,9},{2,10},{3,11},{4,12},{5,13},{6,14},{7,15},{8,0},{9,1},... | collective-permute-start | bytes 1032200 | tf_op jit(solution)/shard_map/ppermute | solution.py:10
  246.7 3.5 collective-permute-start
  250.4 12.0 %collective-permute-start.1 = (bf16[192,896]{1,0:T(8,128)(2,1)S(1)}, bf16[192,896]{1,0:T(8,128)(2,1)S(1)}, u32[]{:S(2)}, u32[]{:S(2)}) collective-permute-start(bf16[192,896]{1,0:T(8,128)(2,1)S(1)} %fusion.22), channel_id=1, source_target_pairs={{0,2},{1,3},{2,0},{3,1},{4,6},{5,7},{6,4},{7,5},{8,10},{9,11},{10,... | collective-permute-start | bytes 1032200 | tf_op jit(solution)/shard_map/ppermute | solution.py:10
  262.6 11.2 %collective-permute-start.2 = (bf16[192,896]{1,0:T(8,128)(2,1)S(1)}, bf16[192,896]{1,0:T(8,128)(2,1)S(1)}, u32[]{:S(2)}, u32[]{:S(2)}) collective-permute-start(bf16[192,896]{1,0:T(8,128)(2,1)S(1)} %get-tuple-element.4), channel_id=1, source_target_pairs={{0,4},{1,5},{2,6},{3,7},{4,0},{5,1},{6,2},{7,3},{8,12},{9,13},{10,... | collective-permute-start | bytes 1032200 | tf_op jit(solution)/shard_map/ppermute | solution.py:10
  273.8 11.8 %collective-permute-start.3 = (bf16[192,896]{1,0:T(8,128)(2,1)S(1)}, bf16[192,896]{1,0:T(8,128)(2,1)S(1)}, u32[]{:S(2)}, u32[]{:S(2)}) collective-permute-start(bf16[192,896]{1,0:T(8,128)(2,1)S(1)} %fusion.21), channel_id=1, source_target_pairs={{0,8},{1,9},{2,10},{3,11},{4,12},{5,13},{6,14},{7,15},{8,0},{9,1},... | collective-permute-start | bytes 1032200 | tf_op jit(solution)/shard_map/ppermute | solution.py:10
Sparse Core Ops, SparseCore 0:
  10.6 45.6 all-gather.4
  59.4 139.7 all-gather.2
  292.0 63.6 reduce-scatter.1
where the time goes:
time: 364 us
  waiting for transfers between devices  305 us (84%)
  starting transfers between devices  25.3 us (7%)
  matrix products  14 us (4%)
  between operations  13.9 us (4%)
  other arithmetic  5.59 us (2%)
    all_gather x1, waiting for transfers between devices, local(): shard_piece = lax.all_gather(down_rotated, 'dp', axis=1, tiled=True)  143 us
    reduce_scatter x1, waiting for transfers between devices, local(): lax.psum_scatter(terms.astype(jnp.bfloat16), 'tensor', scatter_dimension=...  63.8 us
    ppermute x8, waiting for transfers between devices, from_partner(): lax.ppermute(value, axis, [(i, i ^ 1 << apart) for i in range(lax.axis_si...  51.6 us
    all_gather x1, waiting for transfers between devices, local(): grad_grid = lax.all_gather(grad_local, 'tensor', axis=1, tiled=True)  46 us
    ppermute x8, starting transfers between devices, from_partner(): lax.ppermute(value, axis, [(i, i ^ 1 << apart) for i in range(lax.axis_si...  25.2 us
  transfers between devices with their start and end apart: 11, of which 11 were waited for; matrix products, arithmetic and copies ran while one was open for 0% of the time, Pallas kernels for 0%

commit v1 on v0

v1 whole, which is shorter than its diff:
```python
import functools

import jax
import jax.numpy as jnp
import numpy as np
from jax import lax
from jax.experimental import pallas as pl
from jax.experimental.pallas import tpu as pltpu
from jax.sharding import Mesh, PartitionSpec as P

BLK = 128
TENSOR = ("x", "zl", "core")
DP = ("zh", "y")
BF = jnp.bfloat16
F32 = jnp.float32
SC_ROWS = 448


def sylvester(order):
    index = np.arange(order)
    bits = index[:, None] & index[None, :]
    parity = np.zeros((order, order), np.int64)
    for bit in range(order.bit_length() - 1):
        parity ^= (bits >> bit) & 1
    return 1.0 - 2.0 * parity


def shifted(value, axis, step):
    size = lax.axis_size(axis)
    return lax.ppermute(value, axis, [(i, (i + step) % size) for i in range(size)])


def exchange(value):
    return lax.all_to_all(value, TENSOR, 0, 0)


def hadamard_kernel(limit, table_ref, x_ref, out_ref, mixed_ref):
    parts, rows, _ = x_ref.shape
    for n in range(parts):
        mixed_ref[n] = jnp.dot(x_ref[n], table_ref[...], preferred_element_type=F32)
    factor = 1.0 / float(parts * BLK) ** 0.5
    for r in range(rows // 16):
        at = pl.ds(r * 16, 16)
        values = [mixed_ref[n, at, :] for n in range(parts)]
        apart = 1
        while apart < parts:
            values = [
                values[n ^ apart] - values[n] if n & apart else values[n] + values[n ^ apart]
                for n in range(parts)
            ]
            apart *= 2
        for n in range(parts):
            done = values[n] * factor
            if limit is not None:
                done = jnp.clip(done, -limit, limit)
            out_ref[n, at, :] = done.astype(BF)


def both_factors(values, limit=None):
    vmem = pl.BlockSpec(memory_space=pltpu.VMEM)
    return pl.pallas_call(
        functools.partial(hadamard_kernel, limit),
        out_shape=jax.ShapeDtypeStruct(values.shape, BF),
        in_specs=[vmem, vmem],
        out_specs=vmem,
        scratch_shapes=[pltpu.VMEM(values.shape, F32)],
        compiler_params=pltpu.CompilerParams(vmem_limit_bytes=16 * 2**20),
        cost_estimate=pl.CostEstimate(flops=2 * values.size * BLK, bytes_accessed=2_000_000, transcendentals=0),
    )(jnp.asarray(sylvester(BLK), BF), values)


def to_groups(values, parts):
    rows, width = values.shape
    out = values.reshape(2, rows // 2, width // BLK, BLK).transpose(2, 0, 1, 3).reshape(-1, rows // 2, BLK)
    return jnp.pad(out, ((0, parts - out.shape[0]), (0, 0), (0, 0)))


def from_groups(values, width):
    groups = 2 * (width // BLK)
    rows = values.shape[1]
    out = values[:groups].reshape(width // BLK, 2, rows, BLK).transpose(1, 2, 0, 3)
    return out.reshape(2 * rows, width)


def dots_kernel(place_ref, groups_ref, grad_ref, scale_ref, sc_ref, *refs):
    ring = refs[:9]
    partial_ref, rot_ref, total_ref, act_ref = refs[9:]
    zh, y = place_ref[0], place_ref[1]
    n_sc = sc_ref.shape[1]
    n_ring = ring[0].shape[1]
    rows, width = act_ref.shape
    each = rows // 2
    used = 2 * (width // BLK)
    for g in range(used):
        act_ref[(g % 2) * each : (g % 2 + 1) * each, (g // 2) * BLK : (g // 2 + 1) * BLK] = groups_ref[g]
    act_sc = act_ref[:, :n_sc]
    act_ring = act_ref[:, n_sc:]
    dims = (((1,), (1,)), ((), ()))
    for k in range(8):
        shift = (0, -1, 1, -2, 2, -3, 3, 4)[k]
        at = lax.rem(y + shift + 8, 8)
        lanes = pl.multiple_of(lax.rem(at, 2) * BLK, BLK)
        for pair in range(2):
            blocks_sc, blocks_ring, grads, dests = [], [], [], []
            for j in range(2):
                slot = 2 * pair + j
                z = lax.rem(zh + (0, 3, 1, 2)[slot], 4)
                blocks_sc.append(sc_ref[z * 8 + at])
                if k < 7:
                    blocks_ring.append(ring[k][slot])
                else:
                    blocks_ring.append(jnp.concatenate([ring[7][slot], ring[8][slot]], 0))
                dest = z * 4 + lax.div(at, 2)
                dests.append(dest)
                grads.append(grad_ref[dest, :, pl.ds(lanes, BLK)])
            w_sc = jnp.concatenate(blocks_sc, 1)
            w_ring = jnp.concatenate(blocks_ring, 1)
            g = jnp.concatenate(grads, 1)
            part = jnp.dot(act_sc, w_sc, preferred_element_type=F32)
            part += jnp.dot(act_ring, w_ring, preferred_element_type=F32)
            for j in range(2):
                partial_ref[dests[j], :, pl.ds(lanes, BLK)] = part[:, j * BLK : (j + 1) * BLK].astype(BF)
            one = lax.dot_general(g, w_sc, dims, preferred_element_type=F32)
            two = lax.dot_general(g, w_ring, dims, preferred_element_type=F32)
            if k == 0 and pair == 0:
                total_ref[:, :n_sc] = one
                total_ref[:, n_sc:] = two
            else:
                total_ref[:, :n_sc] += one
                total_ref[:, n_sc:] += two
    for g in range(rot_ref.shape[0]):
        if g < used:
            at = slice((g % 2) * each, (g % 2 + 1) * each)
            rot_ref[g] = (total_ref[at, (g // 2) * BLK : (g // 2 + 1) * BLK] * scale_ref[at, :]).astype(BF)
        else:
            rot_ref[g] = jnp.zeros((each, BLK), BF)


def local(hidden, down_rotated, out_gradient, sign_bits, act_exponent, grad_exponent):
    rows, width = hidden.shape
    parts = 16
    cols = out_gradient.shape[1]
    flips = (1 - 2 * sign_bits).astype(F32)
    act_factor = jnp.exp2(act_exponent.astype(F32))[:, None]
    grad_factor = jnp.exp2(grad_exponent.astype(F32))[:, None]

    by_sc = lax.all_gather(down_rotated[:SC_ROWS], DP, axis=0)
    mine = down_rotated[SC_ROWS:]
    own = jnp.stack([mine, shifted(mine, "zh", 1), shifted(mine, "zh", -1), shifted(mine, "zh", 2)])

    signed = (hidden.astype(F32) * flips[None, :] / act_factor).astype(BF)
    act = exchange(both_factors(exchange(to_groups(signed, parts)), 127.0))

    up = down = own
    ring = [own]
    for _ in range(3):
        up, down = shifted(up, "y", 1), shifted(down, "y", -1)
        ring += [up, down]
    half = mine.shape[0] // 2
    ring += [shifted(up[:, :half], "y", 1), shifted(down[:, half:], "y", -1)]

    grad_local = jnp.clip(out_gradient.astype(F32) / grad_factor, -127.0, 127.0).astype(BF)
    grads = exchange(jnp.broadcast_to(grad_local[None], (parts, rows, cols)))

    place = jnp.stack([lax.axis_index("zh"), lax.axis_index("y")]).astype(jnp.int32)
    vmem = pl.BlockSpec(memory_space=pltpu.VMEM)
    partial, rot = pl.pallas_call(
        dots_kernel,
        out_shape=(
            jax.ShapeDtypeStruct((parts, rows, cols), BF),
            jax.ShapeDtypeStruct((parts, rows // 2, BLK), BF),
        ),
        in_specs=[pl.BlockSpec(memory_space=pltpu.SMEM)] + [vmem] * 13,
        out_specs=(vmem, vmem),
        scratch_shapes=[pltpu.VMEM((rows, width), F32), pltpu.VMEM((rows, width), BF)],
        compiler_params=pltpu.CompilerParams(vmem_limit_bytes=40 * 2**20),
        cost_estimate=pl.CostEstimate(flops=4 * rows * width * 4096, bytes_accessed=12_000_000, transcendentals=0),
    )(place, act, grads, grad_factor, by_sc, *ring)

    summed = jnp.sum(exchange(partial).astype(F32), 0)
    mixed = (summed * act_factor).astype(BF)

    back = exchange(both_factors(exchange(rot)))
    grad_hidden = from_groups(back, width).astype(F32) * flips[None, :]
    return mixed, grad_hidden.astype(BF)


def solution(mesh):
    fine = Mesh(mesh.devices.reshape(4, 8, 4, 2, 2), DP + TENSOR)
    in_specs = (P(DP, TENSOR), P(TENSOR, DP), P(DP, TENSOR), P(TENSOR), P(DP), P(DP))
    out_specs = (P(DP, TENSOR), P(DP, TENSOR))
    return jax.shard_map(local, mesh=fine, in_specs=in_specs, out_specs=out_specs, check_vma=False)
```

time: 364 us -> 239 us (0.66)
  the two profiles are of different devices: /device:TPU:8 before, /device:TPU:128 now
where the time goes in v1:
time: 239 us; the launch traced here: 238 us
  waiting for transfers between devices  100 us (42%)
  starting transfers between devices  57.5 us (24%)
  blocking collectives  39.6 us (17%)
  between operations  14.3 us (6%)
  local copies, waits for them, and re-layouts  13.7 us (6%)
  Pallas kernels  7.7 us (3%)
  other arithmetic  4.52 us (2%)
    ppermute x11, waiting for transfers between devices, shifted(): lax.ppermute(value, axis, [(i, (i + step) % size) for i in range(size)])  68.3 us
    ppermute x11, starting transfers between devices, shifted(): lax.ppermute(value, axis, [(i, (i + step) % size) for i in range(size)])  46.5 us
    all_to_all x3, blocking collectives, exchange(): return lax.all_to_all(value, TENSOR, 0, 0)  39.6 us
    all_to_all x3, waiting for transfers between devices, exchange(): return lax.all_to_all(value, TENSOR, 0, 0)  32 us
    all_to_all x3, starting transfers between devices, exchange(): return lax.all_to_all(value, TENSOR, 0, 0)  11 us
    unnamed x24, local copies, waits for them, and re-layouts  8.46 us
    pallas_call x1, Pallas kernels, local(): pl.pallas_call(dots_kernel, out_shape=(jax.ShapeDtypeStruct((parts, rows,...  6.19 us
  transfers between devices with their start and end apart: 15, of which 9 were waited for; matrix products, arithmetic and copies ran while one was open for 3% of the time, Pallas kernels for 0%

profile of v1, /device:TPU:128, one launch (start us, length us, event | category | flops | bytes accessed | tf_op | source)
XLA Modules:
  0.0 237.6 jit_solution(8913506473700346396)
XLA Ops:
  7.2 1.7 slice_bitcast_fusion
  10.3 1.1 divide_convert_fusion
  11.9 15.5 %all_to_all.30.x_ref = bf16[16,96,128]{2,1,0:T(8,128)(2,1)S(1)} all-to-all(bf16[16,96,128]{2,1,0:T(8,128)(2,1)S(1)} %pad.4), channel_id=1, replica_groups=mesh['zh'=4,'y'=8,'x'=4,'zl'=2,'core'=2] {'x','zl','core'}, dimensions={0} | all-to-all | bytes 786432 | tf_op jit(solution)/shard_map/all_to_all | solution.py:34
  27.4 1.1 shard_map.95
  28.5 3.6 %all-to-all-start.1 = ((bf16[16,96,128]{2,1,0:T(8,128)(2,1)}), bf16[16,96,128]{2,1,0:T(8,128)(2,1)S(1)}, u32[]{:S(2)}, u32[]{:S(2)}) async-start(bf16[16,96,128]{2,1,0:T(8,128)(2,1)} %shard_map.95), calls=%async_computation.1 | async-start | bytes 786432 | tf_op jit(solution)/shard_map/all_to_all | solution.py:34
  32.2 10.8 %all-to-all-done.1.groups_ref = bf16[16,96,128]{2,1,0:T(8,128)(2,1)S(1)} async-done(((bf16[16,96,128]{2,1,0:T(8,128)(2,1)}), bf16[16,96,128]{2,1,0:T(8,128)(2,1)S(1)}, u32[]{:S(2)}, u32[]{:S(2)}) %all-to-all-start.1) | async-done | bytes 393248 | tf_op jit(solution)/shard_map/all_to_all | solution.py:34
  43.1 1.3 broadcast_in_dim.4
  44.4 3.7 %all-to-all-start.2 = ((bf16[16,192,256]{2,1,0:T(8,128)(2,1)}), bf16[16,192,256]{2,1,0:T(8,128)(2,1)S(1)}, u32[]{:S(2)}, u32[]{:S(2)}) async-start(bf16[16,192,256]{2,1,0:T(8,128)(2,1)} %broadcast_in_dim.4), calls=%async_computation.2 | async-start | bytes 3145728 | tf_op jit(solution)/shard_map/all_to_all | solution.py:34
  48.1 2.3 collective-permute-start.1
  50.4 5.7 %collective-permute-start = (bf16[448,128]{1,0:T(8,128)(2,1)S(1)}, bf16[448,128]{1,0:T(8,128)(2,1)S(1)}, u32[]{:S(2)}, u32[]{:S(2)}) collective-permute-start(bf16[448,128]{1,0:T(8,128)(2,1)S(1)} %get-tuple-element.7), channel_id=1, source_target_pairs={{0,128},{128,256},{256,384},{384,0},{1,129},{129,257},{257,385},{3... | collective-permute-start | bytes 344072 | tf_op jit(solution)/shard_map/ppermute | solution.py:30
  56.1 7.4 %collective-permute-start.2 = (bf16[448,128]{1,0:T(8,128)(2,1)S(1)}, bf16[448,128]{1,0:T(8,128)(2,1)S(1)}, u32[]{:S(2)}, u32[]{:S(2)}) collective-permute-start(bf16[448,128]{1,0:T(8,128)(2,1)S(1)} %get-tuple-element.7), channel_id=1, source_target_pairs={{0,256},{128,384},{256,0},{384,128},{1,257},{129,385},{257,1},{385... | collective-permute-start | bytes 344072 | tf_op jit(solution)/shard_map/ppermute | solution.py:30
  63.5 20.0 %collective-permute-done = bf16[448,128]{1,0:T(8,128)(2,1)S(1)} collective-permute-done((bf16[448,128]{1,0:T(8,128)(2,1)S(1)}, bf16[448,128]{1,0:T(8,128)(2,1)S(1)}, u32[]{:S(2)}, u32[]{:S(2)}) %collective-permute-start) | collective-permute-done | bytes 114720 | tf_op jit(solution)/shard_map/ppermute | solution.py:30
  83.5 14.6 %collective-permute-done.2 = bf16[448,128]{1,0:T(8,128)(2,1)S(1)} collective-permute-done((bf16[448,128]{1,0:T(8,128)(2,1)S(1)}, bf16[448,128]{1,0:T(8,128)(2,1)S(1)}, u32[]{:S(2)}, u32[]{:S(2)}) %collective-permute-start.2) | collective-permute-done | bytes 114720 | tf_op jit(solution)/shard_map/ppermute | solution.py:30
  98.2 7.4 %collective-permute-start.4 = (bf16[4,448,128]{2,1,0:T(8,128)(2,1)S(1)}, bf16[4,448,128]{2,1,0:T(8,128)(2,1)S(1)}, u32[]{:S(2)}, u32[]{:S(2)}) collective-permute-start(bf16[4,448,128]{2,1,0:T(8,128)(2,1)S(1)} %pad_maximum_fusion.refs_0_), channel_id=1, source_target_pairs={{0,112},{16,0},{32,16},{48,32},{64,48},{80,64},{96,80},{112,96},{1... | collective-permute-start | bytes 1376264 | tf_op jit(solution)/shard_map/ppermute | solution.py:30
  105.6 2.0 collective-permute-start.3
  107.6 15.0 %collective-permute-done.4.refs_2_ = bf16[4,448,128]{2,1,0:T(8,128)(2,1)S(1)} collective-permute-done((bf16[4,448,128]{2,1,0:T(8,128)(2,1)S(1)}, bf16[4,448,128]{2,1,0:T(8,128)(2,1)S(1)}, u32[]{:S(2)}, u32[]{:S(2)}) %collective-permute-start.4) | collective-permute-done | bytes 458784 | tf_op jit(solution)/shard_map/ppermute | solution.py:30
  122.6 4.8 %collective-permute-start.6 = (bf16[4,448,128]{2,1,0:T(8,128)(2,1)S(1)}, bf16[4,448,128]{2,1,0:T(8,128)(2,1)S(1)}, u32[]{:S(2)}, u32[]{:S(2)}) collective-permute-start(bf16[4,448,128]{2,1,0:T(8,128)(2,1)S(1)} %collective-permute-done.4.refs_2_), channel_id=1, source_target_pairs={{0,112},{16,0},{32,16},{48,32},{64,48},{80,64},{96,80},{112,96},{1... | collective-permute-start | bytes 1376264 | tf_op jit(solution)/shard_map/ppermute | solution.py:30
  128.3 1.9 collective-permute-start.5
  130.9 5.7 %collective-permute-done.6.refs_4_ = bf16[4,448,128]{2,1,0:T(8,128)(2,1)S(1)} collective-permute-done((bf16[4,448,128]{2,1,0:T(8,128)(2,1)S(1)}, bf16[4,448,128]{2,1,0:T(8,128)(2,1)S(1)}, u32[]{:S(2)}, u32[]{:S(2)}) %collective-permute-start.6) | collective-permute-done | bytes 458784 | tf_op jit(solution)/shard_map/ppermute | solution.py:30
  136.7 5.6 %collective-permute-start.8 = (bf16[4,448,128]{2,1,0:T(8,128)(2,1)S(1)}, bf16[4,448,128]{2,1,0:T(8,128)(2,1)S(1)}, u32[]{:S(2)}, u32[]{:S(2)}) collective-permute-start(bf16[4,448,128]{2,1,0:T(8,128)(2,1)S(1)} %collective-permute-done.6.refs_4_), channel_id=1, source_target_pairs={{0,112},{16,0},{32,16},{48,32},{64,48},{80,64},{96,80},{112,96},{1... | collective-permute-start | bytes 1376264 | tf_op jit(solution)/shard_map/ppermute | solution.py:30
  143.0 1.9 collective-permute-start.7
  145.0 5.6 %collective-permute-done.8.refs_6_ = bf16[4,448,128]{2,1,0:T(8,128)(2,1)S(1)} collective-permute-done((bf16[4,448,128]{2,1,0:T(8,128)(2,1)S(1)}, bf16[4,448,128]{2,1,0:T(8,128)(2,1)S(1)}, u32[]{:S(2)}, u32[]{:S(2)}) %collective-permute-start.8) | collective-permute-done | bytes 458784 | tf_op jit(solution)/shard_map/ppermute | solution.py:30
  151.3 5.6 %collective-permute-start.10 = (bf16[4,224,128]{2,1,0:T(8,128)(2,1)}, bf16[4,224,128]{2,1,0:T(8,128)(2,1)}, u32[]{:S(2)}, u32[]{:S(2)}) collective-permute-start(bf16[4,224,128]{2,1,0:T(8,128)(2,1)} %slice.21), channel_id=1, source_target_pairs={{0,112},{16,0},{32,16},{48,32},{64,48},{80,64},{96,80},{112,96},{1... | collective-permute-start | bytes 688136 | tf_op jit(solution)/shard_map/ppermute | solution.py:30
  157.6 1.9 collective-permute-start.9
  160.7 6.3 %collective-permute-done.9.refs_7_ = bf16[4,224,128]{2,1,0:T(8,128)(2,1)} collective-permute-done((bf16[4,224,128]{2,1,0:T(8,128)(2,1)}, bf16[4,224,128]{2,1,0:T(8,128)(2,1)}, u32[]{:S(2)}, u32[]{:S(2)}) %collective-permute-start.9) | collective-permute-done | bytes 229408 | tf_op jit(solution)/shard_map/ppermute | solution.py:30
  167.0 2.0 copy-done.1
  169.1 1.0 copy-done.3
  173.1 6.2 %shard_map.96 = (bf16[16,192,256]{2,1,0:T(8,128)(2,1)}, bf16[16,96,128]{2,1,0:T(8,128)(2,1)S(1)}) custom-call(s32[2]{0:T(128)S(1)} %pad_add_fusion.place_ref, bf16[16,96,128]{2,1,0:T(8,128)(2,1)S(1)} %all-to-all-done.1.groups_ref, bf16[16,192,256]{2,1,0:T(8,128)(2,1)S(1)} %all-to-all-done.2.grad_ref, f32[192,1]{1,0:T(8,128)S(1)} %copy.13.scale_ref, ...), custom_call_target="tpu_custom_call" | custom-call | flops 2818572288 | bytes 12000000 | tf_op jit(solution)/shard_map/pallas_call | solution.py:167
  179.3 12.1 %all_to_all.31.x_ref = bf16[16,96,128]{2,1,0:T(8,128)(2,1)S(1)} all-to-all(bf16[16,96,128]{2,1,0:T(8,128)(2,1)S(1)} %get-tuple-element.5), channel_id=1, replica_groups=mesh['zh'=4,'y'=8,'x'=4,'zl'=2,'core'=2] {'x','zl','core'}, dimensions={0} | all-to-all | bytes 786432 | tf_op jit(solution)/shard_map/all_to_all | solution.py:34
  191.7 12.1 %all_to_all.32 = bf16[16,96,128]{2,1,0:T(8,128)(2,1)S(1)} all-to-all(bf16[16,96,128]{2,1,0:T(8,128)(2,1)S(1)} %shard_map.97), channel_id=1, replica_groups=mesh['zh'=4,'y'=8,'x'=4,'zl'=2,'core'=2] {'x','zl','core'}, dimensions={0} | all-to-all | bytes 786432 | tf_op jit(solution)/shard_map/all_to_all | solution.py:34
  203.8 3.7 %all-to-all-start.3 = ((bf16[16,192,256]{2,1,0:T(8,128)(2,1)}), bf16[16,192,256]{2,1,0:T(8,128)(2,1)S(1)}, u32[]{:S(2)}, u32[]{:S(2)}) async-start(bf16[16,192,256]{2,1,0:T(8,128)(2,1)} %get-tuple-element.4), calls=%async_computation.3 | async-start | bytes 3145728 | tf_op jit(solution)/shard_map/all_to_all | solution.py:34
  208.6 21.1 %all-to-all-done.3 = bf16[16,192,256]{2,1,0:T(8,128)(2,1)S(1)} async-done(((bf16[16,192,256]{2,1,0:T(8,128)(2,1)}), bf16[16,192,256]{2,1,0:T(8,128)(2,1)S(1)}, u32[]{:S(2)}, u32[]{:S(2)}) %all-to-all-start.3) | async-done | bytes 1572896 | tf_op jit(solution)/shard_map/all_to_all | solution.py:34
  (49 shorter events, 12.5 us)
Async XLA Ops:
  7.2 159.8 %all-gather.3.cloned.1.call-start = ((), (), s32[]{:S(2)}) async-start(), calls=%async_computation.6 | async-start | bytes 3784704 | tf_op jit(solution)/shard_map/all_gather | solution.py:147
  11.4 16.0 %copy-start = (bf16[128,128]{1,0:T(8,128)(2,1)S(1)}, bf16[128,128]{1,0:T(8,128)(2,1)}, u32[]{:S(2)}) copy-start(bf16[128,128]{1,0:T(8,128)(2,1)} %constant.28.clone.table_ref) | copy-start | bytes 98308
  11.9 20.2 %copy-start.11 = (s32[192]{0:T(256)S(1)}, s32[192]{0:T(256)}, u32[]{:S(2)}) copy-start(s32[192]{0:T(256)} %param.13) | copy-start | bytes 2308
  11.9 20.2 %copy-start.10 = (bf16[192,256]{1,0:T(8,128)(2,1)S(1)}, bf16[192,256]{1,0:T(8,128)(2,1)}, u32[]{:S(2)}) copy-start(bf16[192,256]{1,0:T(8,128)(2,1)} %param.10) | copy-start | bytes 294916
  28.5 14.5 %all-to-all-start.1 = ((bf16[16,96,128]{2,1,0:T(8,128)(2,1)}), bf16[16,96,128]{2,1,0:T(8,128)(2,1)S(1)}, u32[]{:S(2)}, u32[]{:S(2)}) async-start(bf16[16,96,128]{2,1,0:T(8,128)(2,1)} %shard_map.95), calls=%async_computation.1 | async-start | bytes 786432 | tf_op jit(solution)/shard_map/all_to_all | solution.py:34
  44.4 122.6 %all-to-all-start.2 = ((bf16[16,192,256]{2,1,0:T(8,128)(2,1)}), bf16[16,192,256]{2,1,0:T(8,128)(2,1)S(1)}, u32[]{:S(2)}, u32[]{:S(2)}) async-start(bf16[16,192,256]{2,1,0:T(8,128)(2,1)} %broadcast_in_dim.4), calls=%async_computation.2 | async-start | bytes 3145728 | tf_op jit(solution)/shard_map/all_to_all | solution.py:34
  48.1 15.4 %collective-permute-start.1 = (bf16[448,128]{1,0:T(8,128)(2,1)S(1)}, bf16[448,128]{1,0:T(8,128)(2,1)S(1)}, u32[]{:S(2)}, u32[]{:S(2)}) collective-permute-start(bf16[448,128]{1,0:T(8,128)(2,1)S(1)} %get-tuple-element.7), channel_id=1, source_target_pairs={{0,384},{128,0},{256,128},{384,256},{1,385},{129,1},{257,129},{385... | collective-permute-start | bytes 344072 | tf_op jit(solution)/shard_map/ppermute | solution.py:30
  50.4 33.1 %collective-permute-start = (bf16[448,128]{1,0:T(8,128)(2,1)S(1)}, bf16[448,128]{1,0:T(8,128)(2,1)S(1)}, u32[]{:S(2)}, u32[]{:S(2)}) collective-permute-start(bf16[448,128]{1,0:T(8,128)(2,1)S(1)} %get-tuple-element.7), channel_id=1, source_target_pairs={{0,128},{128,256},{256,384},{384,0},{1,129},{129,257},{257,385},{3... | collective-permute-start | bytes 344072 | tf_op jit(solution)/shard_map/ppermute | solution.py:30
  56.1 42.0 %collective-permute-start.2 = (bf16[448,128]{1,0:T(8,128)(2,1)S(1)}, bf16[448,128]{1,0:T(8,128)(2,1)S(1)}, u32[]{:S(2)}, u32[]{:S(2)}) collective-permute-start(bf16[448,128]{1,0:T(8,128)(2,1)S(1)} %get-tuple-element.7), channel_id=1, source_target_pairs={{0,256},{128,384},{256,0},{384,128},{1,257},{129,385},{257,1},{385... | collective-permute-start | bytes 344072 | tf_op jit(solution)/shard_map/ppermute | solution.py:30
  98.2 24.4 %collective-permute-start.4 = (bf16[4,448,128]{2,1,0:T(8,128)(2,1)S(1)}, bf16[4,448,128]{2,1,0:T(8,128)(2,1)S(1)}, u32[]{:S(2)}, u32[]{:S(2)}) collective-permute-start(bf16[4,448,128]{2,1,0:T(8,128)(2,1)S(1)} %pad_maximum_fusion.refs_0_), channel_id=1, source_target_pairs={{0,112},{16,0},{32,16},{48,32},{64,48},{80,64},{96,80},{112,96},{1... | collective-permute-start | bytes 1376264 | tf_op jit(solution)/shard_map/ppermute | solution.py:30
  105.6 22.7 %collective-permute-start.3 = (bf16[4,448,128]{2,1,0:T(8,128)(2,1)S(1)}, bf16[4,448,128]{2,1,0:T(8,128)(2,1)S(1)}, u32[]{:S(2)}, u32[]{:S(2)}) collective-permute-start(bf16[4,448,128]{2,1,0:T(8,128)(2,1)S(1)} %pad_maximum_fusion.refs_0_), channel_id=1, source_target_pairs={{0,16},{16,32},{32,48},{48,64},{64,80},{80,96},{96,112},{112,0},{1... | collective-permute-start | bytes 1376264 | tf_op jit(solution)/shard_map/ppermute | solution.py:30
  122.6 14.0 %collective-permute-start.6 = (bf16[4,448,128]{2,1,0:T(8,128)(2,1)S(1)}, bf16[4,448,128]{2,1,0:T(8,128)(2,1)S(1)}, u32[]{:S(2)}, u32[]{:S(2)}) collective-permute-start(bf16[4,448,128]{2,1,0:T(8,128)(2,1)S(1)} %collective-permute-done.4.refs_2_), channel_id=1, source_target_pairs={{0,112},{16,0},{32,16},{48,32},{64,48},{80,64},{96,80},{112,96},{1... | collective-permute-start | bytes 1376264 | tf_op jit(solution)/shard_map/ppermute | solution.py:30
  127.4 0.8 copy-start.2
  128.3 14.8 %collective-permute-start.5 = (bf16[4,448,128]{2,1,0:T(8,128)(2,1)S(1)}, bf16[4,448,128]{2,1,0:T(8,128)(2,1)S(1)}, u32[]{:S(2)}, u32[]{:S(2)}) collective-permute-start(bf16[4,448,128]{2,1,0:T(8,128)(2,1)S(1)} %collective-permute-done.3.refs_1_), channel_id=1, source_target_pairs={{0,16},{16,32},{32,48},{48,64},{64,80},{80,96},{96,112},{112,0},{1... | collective-permute-start | bytes 1376264 | tf_op jit(solution)/shard_map/ppermute | solution.py:30
  130.2 0.8 copy-start.4
  136.7 13.9 %collective-permute-start.8 = (bf16[4,448,128]{2,1,0:T(8,128)(2,1)S(1)}, bf16[4,448,128]{2,1,0:T(8,128)(2,1)S(1)}, u32[]{:S(2)}, u32[]{:S(2)}) collective-permute-start(bf16[4,448,128]{2,1,0:T(8,128)(2,1)S(1)} %collective-permute-done.6.refs_4_), channel_id=1, source_target_pairs={{0,112},{16,0},{32,16},{48,32},{64,48},{80,64},{96,80},{112,96},{1... | collective-permute-start | bytes 1376264 | tf_op jit(solution)/shard_map/ppermute | solution.py:30
  142.3 0.8 copy-start.6
  143.0 13.8 %copy-start.8 = (bf16[4,448,128]{2,1,0:T(8,128)(2,1)}, bf16[4,448,128]{2,1,0:T(8,128)(2,1)S(1)}, u32[]{:S(2)}) copy-start(bf16[4,448,128]{2,1,0:T(8,128)(2,1)S(1)} %collective-permute-done.5.refs_3_) | copy-start | bytes 1376260
  143.0 13.8 %collective-permute-start.7 = (bf16[4,448,128]{2,1,0:T(8,128)(2,1)S(1)}, bf16[4,448,128]{2,1,0:T(8,128)(2,1)S(1)}, u32[]{:S(2)}, u32[]{:S(2)}) collective-permute-start(bf16[4,448,128]{2,1,0:T(8,128)(2,1)S(1)} %collective-permute-done.5.refs_3_), channel_id=1, source_target_pairs={{0,16},{16,32},{32,48},{48,64},{64,80},{80,96},{96,112},{112,0},{1... | collective-permute-start | bytes 1376264 | tf_op jit(solution)/shard_map/ppermute | solution.py:30
  151.3 9.4 %collective-permute-start.10 = (bf16[4,224,128]{2,1,0:T(8,128)(2,1)}, bf16[4,224,128]{2,1,0:T(8,128)(2,1)}, u32[]{:S(2)}, u32[]{:S(2)}) collective-permute-start(bf16[4,224,128]{2,1,0:T(8,128)(2,1)} %slice.21), channel_id=1, source_target_pairs={{0,112},{16,0},{32,16},{48,32},{64,48},{80,64},{96,80},{112,96},{1... | collective-permute-start | bytes 688136 | tf_op jit(solution)/shard_map/ppermute | solution.py:30
  157.6 9.4 %collective-permute-start.9 = (bf16[4,224,128]{2,1,0:T(8,128)(2,1)}, bf16[4,224,128]{2,1,0:T(8,128)(2,1)}, u32[]{:S(2)}, u32[]{:S(2)}) collective-permute-start(bf16[4,224,128]{2,1,0:T(8,128)(2,1)} %slice.20), channel_id=1, source_target_pairs={{0,16},{16,32},{32,48},{48,64},{64,80},{80,96},{96,112},{112,0},{1... | collective-permute-start | bytes 688136 | tf_op jit(solution)/shard_map/ppermute | solution.py:30
  167.0 2.0 copy-start.1
  169.1 1.0 copy-start.3
  170.1 1.0 copy-start.5
  171.1 1.0 copy-start.7
  172.1 1.0 copy-start.9
  203.8 26.0 %all-to-all-start.3 = ((bf16[16,192,256]{2,1,0:T(8,128)(2,1)}), bf16[16,192,256]{2,1,0:T(8,128)(2,1)S(1)}, u32[]{:S(2)}, u32[]{:S(2)}) async-start(bf16[16,192,256]{2,1,0:T(8,128)(2,1)} %get-tuple-element.4), calls=%async_computation.3 | async-start | bytes 3145728 | tf_op jit(solution)/shard_map/all_to_all | solution.py:34
Sparse Core Ops, SparseCore 0:
  11.2 112.2 all-gather.2

commit v2 on v1

--- a/solution.py
+++ b/solution.py
@@ -84,7 +84,7 @@
 
 def dots_kernel(place_ref, groups_ref, grad_ref, scale_ref, sc_ref, *refs):
     ring = refs[:9]
-    partial_ref, rot_ref, total_ref, act_ref = refs[9:]
+    sent_ref, total_ref, act_ref = refs[9:]
     zh, y = place_ref[0], place_ref[1]
     n_sc = sc_ref.shape[1]
     n_ring = ring[0].shape[1]
@@ -100,6 +100,7 @@
         shift = (0, -1, 1, -2, 2, -3, 3, 4)[k]
         at = lax.rem(y + shift + 8, 8)
         lanes = pl.multiple_of(lax.rem(at, 2) * BLK, BLK)
+        lines = pl.multiple_of(lax.rem(at, 2) * rows, rows)
         for pair in range(2):
             blocks_sc, blocks_ring, grads, dests = [], [], [], []
             for j in range(2):
@@ -119,7 +120,7 @@
             part = jnp.dot(act_sc, w_sc, preferred_element_type=F32)
             part += jnp.dot(act_ring, w_ring, preferred_element_type=F32)
             for j in range(2):
-                partial_ref[dests[j], :, pl.ds(lanes, BLK)] = part[:, j * BLK : (j + 1) * BLK].astype(BF)
+                sent_ref[dests[j], pl.ds(lines, rows), :] = part[:, j * BLK : (j + 1) * BLK].astype(BF)
             one = lax.dot_general(g, w_sc, dims, preferred_element_type=F32)
             two = lax.dot_general(g, w_ring, dims, preferred_element_type=F32)
             if k == 0 and pair == 0:
@@ -128,12 +129,12 @@
             else:
                 total_ref[:, :n_sc] += one
                 total_ref[:, n_sc:] += two
-    for g in range(rot_ref.shape[0]):
+    for g in range(sent_ref.shape[0]):
         if g < used:
             at = slice((g % 2) * each, (g % 2 + 1) * each)
-            rot_ref[g] = (total_ref[at, (g // 2) * BLK : (g // 2 + 1) * BLK] * scale_ref[at, :]).astype(BF)
+            sent_ref[g, 2 * rows :, :] = (total_ref[at, (g // 2) * BLK : (g // 2 + 1) * BLK] * scale_ref[at, :]).astype(BF)
         else:
-            rot_ref[g] = jnp.zeros((each, BLK), BF)
+            sent_ref[g, 2 * rows :, :] = jnp.zeros((each, BLK), BF)
 
 
 def local(hidden, down_rotated, out_gradient, sign_bits, act_exponent, grad_exponent):
@@ -148,39 +149,43 @@
     mine = down_rotated[SC_ROWS:]
     own = jnp.stack([mine, shifted(mine, "zh", 1), shifted(mine, "zh", -1), shifted(mine, "zh", 2)])
 
-    signed = (hidden.astype(F32) * flips[None, :] / act_factor).astype(BF)
-    act = exchange(both_factors(exchange(to_groups(signed, parts)), 127.0))
+    signed = to_groups((hidden.astype(F32) * flips[None, :] / act_factor).astype(BF), parts)
+    grad_local = jnp.clip(out_gradient.astype(F32) / grad_factor, -127.0, 127.0).astype(BF)
+    grad_copies = jnp.broadcast_to(grad_local[None], (parts, rows, cols))
 
-    up = down = own
-    ring = [own]
-    for _ in range(3):
-        up, down = shifted(up, "y", 1), shifted(down, "y", -1)
-        ring += [up, down]
+    own, signed = lax.optimization_barrier((own, signed))
+    up, down = shifted(own, "y", 1), shifted(own, "y", -1)
+    ring = [own, up, down]
+    grid = both_factors(exchange(signed), 127.0)
+    up, down, grid = lax.optimization_barrier((up, down, grid))
+    up, down = shifted(up, "y", 1), shifted(down, "y", -1)
+    ring += [up, down]
+    act = exchange(grid)
+    up, down, grad_copies = lax.optimization_barrier((up, down, grad_copies))
+    up, down = shifted(up, "y", 1), shifted(down, "y", -1)
+    ring += [up, down]
+    grads = exchange(grad_copies)
     half = mine.shape[0] // 2
     ring += [shifted(up[:, :half], "y", 1), shifted(down[:, half:], "y", -1)]
 
-    grad_local = jnp.clip(out_gradient.astype(F32) / grad_factor, -127.0, 127.0).astype(BF)
-    grads = exchange(jnp.broadcast_to(grad_local[None], (parts, rows, cols)))
-
     place = jnp.stack([lax.axis_index("zh"), lax.axis_index("y")]).astype(jnp.int32)
     vmem = pl.BlockSpec(memory_space=pltpu.VMEM)
-    partial, rot = pl.pallas_call(
+    sent = pl.pallas_call(
         dots_kernel,
-        out_shape=(
-            jax.ShapeDtypeStruct((parts, rows, cols), BF),
-            jax.ShapeDtypeStruct((parts, rows // 2, BLK), BF),
-        ),
+        out_shape=jax.ShapeDtypeStruct((parts, 2 * rows + rows // 2, BLK), BF),
         in_specs=[pl.BlockSpec(memory_space=pltpu.SMEM)] + [vmem] * 13,
-        out_specs=(vmem, vmem),
+        out_specs=vmem,
         scratch_shapes=[pltpu.VMEM((rows, width), F32), pltpu.VMEM((rows, width), BF)],
         compiler_params=pltpu.CompilerParams(vmem_limit_bytes=40 * 2**20),
         cost_estimate=pl.CostEstimate(flops=4 * rows * width * 4096, bytes_accessed=12_000_000, transcendentals=0),
     )(place, act, grads, grad_factor, by_sc, *ring)
 
-    summed = jnp.sum(exchange(partial).astype(F32), 0)
+    arrived = exchange(sent)
+    back = exchange(both_factors(arrived[:, 2 * rows :]))
+    summed = jnp.sum(arrived[:, : 2 * rows].astype(F32), 0)
+    summed = jnp.concatenate([summed[:rows], summed[rows:]], 1)
     mixed = (summed * act_factor).astype(BF)
 
-    back = exchange(both_factors(exchange(rot)))
     grad_hidden = from_groups(back, width).astype(F32) * flips[None, :]
     return mixed, grad_hidden.astype(BF)
 

time: 239 us -> 194 us (0.81)
  the two profiles are of different devices: /device:TPU:128 before, /device:TPU:24 now
where the time goes in v2:
time: 194 us; the launch traced here: 193 us
  starting transfers between devices  64 us (33%)
  waiting for transfers between devices  61.6 us (32%)
  blocking collectives  30.8 us (16%)
  between operations  14.3 us (7%)
  local copies, waits for them, and re-layouts  10.1 us (5%)
  Pallas kernels  7.65 us (4%)
  other arithmetic  4.53 us (2%)
    ppermute x11, waiting for transfers between devices, shifted(): lax.ppermute(value, axis, [(i, (i + step) % size) for i in range(size)])  49.8 us
    ppermute x11, starting transfers between devices, shifted(): lax.ppermute(value, axis, [(i, (i + step) % size) for i in range(size)])  44.8 us
    all_to_all x1, blocking collectives, exchange(): return lax.all_to_all(value, TENSOR, 0, 0)  30.8 us
    all_to_all x4, starting transfers between devices, exchange(): return lax.all_to_all(value, TENSOR, 0, 0)  19.2 us
    all_to_all x4, waiting for transfers between devices, exchange(): return lax.all_to_all(value, TENSOR, 0, 0)  11.7 us
    pallas_call x1, Pallas kernels, local(): pl.pallas_call(dots_kernel, out_shape=jax.ShapeDtypeStruct((parts, 2 * ro...  5.41 us
    unnamed x16, local copies, waits for them, and re-layouts  4.1 us
  transfers between devices with their start and end apart: 16, of which 10 were waited for; matrix products, arithmetic and copies ran while one was open for 4% of the time, Pallas kernels for 1%

profile of v2, /device:TPU:24, one launch (start us, length us, event | category | flops | bytes accessed | tf_op | source)
XLA Modules:
  0.0 193.0 jit_solution(13663589062394261990)
XLA Ops:
  7.2 1.6 fusion.2
  8.9 10.9 %collective-permute-start.1 = (bf16[448,128]{1,0:T(8,128)(2,1)S(1)}, bf16[448,128]{1,0:T(8,128)(2,1)S(1)}, u32[]{:S(2)}, u32[]{:S(2)}) collective-permute-start(bf16[448,128]{1,0:T(8,128)(2,1)S(1)} %get-tuple-element.20), channel_id=1, source_target_pairs={{0,384},{128,0},{256,128},{384,256},{1,385},{129,1},{257,129},{385... | collective-permute-start | bytes 344072 | tf_op jit(solution)/shard_map/ppermute | solution.py:30
  19.8 1.9 collective-permute-start
  21.8 4.8 %collective-permute-start.2 = (bf16[448,128]{1,0:T(8,128)(2,1)S(1)}, bf16[448,128]{1,0:T(8,128)(2,1)S(1)}, u32[]{:S(2)}, u32[]{:S(2)}) collective-permute-start(bf16[448,128]{1,0:T(8,128)(2,1)S(1)} %get-tuple-element.20), channel_id=1, source_target_pairs={{0,256},{128,384},{256,0},{384,128},{1,257},{129,385},{257,1},{385... | collective-permute-start | bytes 344072 | tf_op jit(solution)/shard_map/ppermute | solution.py:30
  27.9 1.1 divide_convert_fusion
  30.3 4.1 %collective-permute-done = bf16[448,128]{1,0:T(8,128)(2,1)S(1)} collective-permute-done((bf16[448,128]{1,0:T(8,128)(2,1)S(1)}, bf16[448,128]{1,0:T(8,128)(2,1)S(1)}, u32[]{:S(2)}, u32[]{:S(2)}) %collective-permute-start) | collective-permute-done | bytes 114720 | tf_op jit(solution)/shard_map/ppermute | solution.py:30
  34.5 5.5 %all-to-all-start = ((bf16[16,96,128]{2,1,0:T(8,128)(2,1)}), bf16[16,96,128]{2,1,0:T(8,128)(2,1)S(1)}, u32[]{:S(2)}, u32[]{:S(2)}) async-start(bf16[16,96,128]{2,1,0:T(8,128)(2,1)} %pad.4), calls=%async_computation | async-start | bytes 786432 | tf_op jit(solution)/shard_map/all_to_all | solution.py:34
  40.0 2.3 %collective-permute-start.4 = (bf16[4,448,128]{2,1,0:T(8,128)(2,1)S(1)}, bf16[4,448,128]{2,1,0:T(8,128)(2,1)S(1)}, u32[]{:S(2)}, u32[]{:S(2)}) collective-permute-start(bf16[4,448,128]{2,1,0:T(8,128)(2,1)S(1)} %pad_maximum_fusion.refs_0_), channel_id=1, source_target_pairs={{0,112},{16,0},{32,16},{48,32},{64,48},{80,64},{96,80},{112,96},{1... | collective-permute-start | bytes 1376264 | tf_op jit(solution)/shard_map/ppermute | solution.py:30
  42.3 4.7 %collective-permute-start.3 = (bf16[4,448,128]{2,1,0:T(8,128)(2,1)S(1)}, bf16[4,448,128]{2,1,0:T(8,128)(2,1)S(1)}, u32[]{:S(2)}, u32[]{:S(2)}) collective-permute-start(bf16[4,448,128]{2,1,0:T(8,128)(2,1)S(1)} %pad_maximum_fusion.refs_0_), channel_id=1, source_target_pairs={{0,16},{16,32},{32,48},{48,64},{64,80},{80,96},{96,112},{112,0},{1... | collective-permute-start | bytes 1376264 | tf_op jit(solution)/shard_map/ppermute | solution.py:30
  47.0 3.3 %all-to-all-done.x_ref = bf16[16,96,128]{2,1,0:T(8,128)(2,1)S(1)} async-done(((bf16[16,96,128]{2,1,0:T(8,128)(2,1)}), bf16[16,96,128]{2,1,0:T(8,128)(2,1)S(1)}, u32[]{:S(2)}, u32[]{:S(2)}) %all-to-all-start) | async-done | bytes 393248 | tf_op jit(solution)/shard_map/all_to_all | solution.py:34
  50.3 1.1 shard_map.95
  51.5 6.5 %collective-permute-done.4.refs_2_ = bf16[4,448,128]{2,1,0:T(8,128)(2,1)S(1)} collective-permute-done((bf16[4,448,128]{2,1,0:T(8,128)(2,1)S(1)}, bf16[4,448,128]{2,1,0:T(8,128)(2,1)S(1)}, u32[]{:S(2)}, u32[]{:S(2)}) %collective-permute-start.4) | collective-permute-done | bytes 458784 | tf_op jit(solution)/shard_map/ppermute | solution.py:30
  58.6 5.2 %all-to-all-start.1 = ((bf16[16,96,128]{2,1,0:T(8,128)(2,1)}), bf16[16,96,128]{2,1,0:T(8,128)(2,1)S(1)}, u32[]{:S(2)}, u32[]{:S(2)}) async-start(bf16[16,96,128]{2,1,0:T(8,128)(2,1)} %shard_map.95), calls=%async_computation.1 | async-start | bytes 786432 | tf_op jit(solution)/shard_map/all_to_all | solution.py:34
  63.8 5.5 %collective-permute-start.5 = (bf16[4,448,128]{2,1,0:T(8,128)(2,1)S(1)}, bf16[4,448,128]{2,1,0:T(8,128)(2,1)}, u32[]{:S(2)}, u32[]{:S(2)}) collective-permute-start(bf16[4,448,128]{2,1,0:T(8,128)(2,1)S(1)} %collective-permute-done.3.refs_1_), channel_id=1, source_target_pairs={{0,16},{16,32},{32,48},{48,64},{64,80},{80,96},{96,112},{112,0},{1... | collective-permute-start | bytes 1376264 | tf_op jit(solution)/shard_map/ppermute | solution.py:30
  69.4 1.9 collective-permute-start.6
  71.4 12.0 %collective-permute-done.5.refs_3_ = bf16[4,448,128]{2,1,0:T(8,128)(2,1)} collective-permute-done((bf16[4,448,128]{2,1,0:T(8,128)(2,1)S(1)}, bf16[4,448,128]{2,1,0:T(8,128)(2,1)}, u32[]{:S(2)}, u32[]{:S(2)}) %collective-permute-start.5) | collective-permute-done | bytes 458784 | tf_op jit(solution)/shard_map/ppermute | solution.py:30
  83.4 4.6 %collective-permute-done.6.refs_4_ = bf16[4,448,128]{2,1,0:T(8,128)(2,1)} collective-permute-done((bf16[4,448,128]{2,1,0:T(8,128)(2,1)S(1)}, bf16[4,448,128]{2,1,0:T(8,128)(2,1)}, u32[]{:S(2)}, u32[]{:S(2)}) %collective-permute-start.6) | collective-permute-done | bytes 458784 | tf_op jit(solution)/shard_map/ppermute | solution.py:30
  88.0 1.3 broadcast_in_dim.4
  89.3 5.0 %all-to-all-start.2 = ((bf16[16,192,256]{2,1,0:T(8,128)(2,1)}), bf16[16,192,256]{2,1,0:T(8,128)(2,1)S(1)}, u32[]{:S(2)}, u32[]{:S(2)}) async-start(bf16[16,192,256]{2,1,0:T(8,128)(2,1)} %broadcast_in_dim.4), calls=%async_computation.2 | async-start | bytes 3145728 | tf_op jit(solution)/shard_map/all_to_all | solution.py:34
  94.3 2.2 %collective-permute-start.7 = (bf16[4,448,128]{2,1,0:T(8,128)(2,1)}, bf16[4,448,128]{2,1,0:T(8,128)(2,1)S(1)}, u32[]{:S(2)}, u32[]{:S(2)}) collective-permute-start(bf16[4,448,128]{2,1,0:T(8,128)(2,1)} %collective-permute-done.5.refs_3_), channel_id=1, source_target_pairs={{0,16},{16,32},{32,48},{48,64},{64,80},{80,96},{96,112},{112,0},{1... | collective-permute-start | bytes 1376264 | tf_op jit(solution)/shard_map/ppermute | solution.py:30
  96.5 3.7 %collective-permute-start.8 = (bf16[4,448,128]{2,1,0:T(8,128)(2,1)}, bf16[4,448,128]{2,1,0:T(8,128)(2,1)S(1)}, u32[]{:S(2)}, u32[]{:S(2)}) collective-permute-start(bf16[4,448,128]{2,1,0:T(8,128)(2,1)} %collective-permute-done.6.refs_4_), channel_id=1, source_target_pairs={{0,112},{16,0},{32,16},{48,32},{64,48},{80,64},{96,80},{112,96},{1... | collective-permute-start | bytes 1376264 | tf_op jit(solution)/shard_map/ppermute | solution.py:30
  100.2 13.6 %collective-permute-done.7.refs_5_ = bf16[4,448,128]{2,1,0:T(8,128)(2,1)S(1)} collective-permute-done((bf16[4,448,128]{2,1,0:T(8,128)(2,1)}, bf16[4,448,128]{2,1,0:T(8,128)(2,1)S(1)}, u32[]{:S(2)}, u32[]{:S(2)}) %collective-permute-start.7) | collective-permute-done | bytes 458784 | tf_op jit(solution)/shard_map/ppermute | solution.py:30
  114.5 4.9 %collective-permute-start.9 = (bf16[4,224,128]{2,1,0:T(8,128)(2,1)}, bf16[4,224,128]{2,1,0:T(8,128)(2,1)}, u32[]{:S(2)}, u32[]{:S(2)}) collective-permute-start(bf16[4,224,128]{2,1,0:T(8,128)(2,1)} %slice.36), channel_id=1, source_target_pairs={{0,16},{16,32},{32,48},{48,64},{64,80},{80,96},{96,112},{112,0},{1... | collective-permute-start | bytes 688136 | tf_op jit(solution)/shard_map/ppermute | solution.py:30
  120.0 1.9 collective-permute-start.10
  122.2 2.4 %collective-permute-done.9.refs_7_ = bf16[4,224,128]{2,1,0:T(8,128)(2,1)} collective-permute-done((bf16[4,224,128]{2,1,0:T(8,128)(2,1)}, bf16[4,224,128]{2,1,0:T(8,128)(2,1)}, u32[]{:S(2)}, u32[]{:S(2)}) %collective-permute-start.9) | collective-permute-done | bytes 229408 | tf_op jit(solution)/shard_map/ppermute | solution.py:30
  124.6 6.0 %collective-permute-done.10.refs_8_ = bf16[4,224,128]{2,1,0:T(8,128)(2,1)} collective-permute-done((bf16[4,224,128]{2,1,0:T(8,128)(2,1)}, bf16[4,224,128]{2,1,0:T(8,128)(2,1)}, u32[]{:S(2)}, u32[]{:S(2)}) %collective-permute-start.10) | collective-permute-done | bytes 229408 | tf_op jit(solution)/shard_map/ppermute | solution.py:30
  130.6 2.0 %copy-done = bf16[14336,128]{1,0:T(8,128)(2,1)S(1)} copy-done((bf16[14336,128]{1,0:T(8,128)(2,1)S(1)}, bf16[14336,128]{1,0:T(8,128)(2,1)}, u32[]{:S(2)}) %copy-start) | copy-done | bytes 3670040
  134.7 5.4 %shard_map.96 = bf16[16,480,128]{2,1,0:T(8,128)(2,1)S(1)} custom-call(s32[2]{0:T(128)S(1)} %pad_add_fusion.place_ref, bf16[16,96,128]{2,1,0:T(8,128)(2,1)S(1)} %all-to-all-done.1.groups_ref, bf16[16,192,256]{2,1,0:T(8,128)(2,1)S(1)} %all-to-all-done.2.grad_ref, f32[192,1]{1,0:T(8,128)S(1)} %copy.13.scale_ref, bf16[32,448,128]{2,1,0:T(8,128)(2,1)S(1)} %bitcast.20, ...), custom_call_target="tpu_custom_call" | custom-call | flops 2818572288 | bytes 12000000 | tf_op jit(solution)/shard_map/pallas_call | solution.py:173
  140.1 30.8 %all_to_all.25 = bf16[16,480,128]{2,1,0:T(8,128)(2,1)S(1)} all-to-all(bf16[16,480,128]{2,1,0:T(8,128)(2,1)S(1)} %shard_map.96), channel_id=1, replica_groups=mesh['zh'=4,'y'=8,'x'=4,'zl'=2,'core'=2] {'x','zl','core'}, dimensions={0} | all-to-all | bytes 3932160 | tf_op jit(solution)/shard_map/all_to_all | solution.py:34
  171.0 1.1 shard_map.97
  172.1 3.6 %all-to-all-start.4 = ((bf16[16,96,128]{2,1,0:T(8,128)(2,1)}), bf16[16,96,128]{2,1,0:T(8,128)(2,1)S(1)}, u32[]{:S(2)}, u32[]{:S(2)}) async-start(bf16[16,96,128]{2,1,0:T(8,128)(2,1)} %shard_map.97), calls=%async_computation.4 | async-start | bytes 786432 | tf_op jit(solution)/shard_map/all_to_all | solution.py:34
  176.6 8.4 %all-to-all-done.4 = bf16[16,96,128]{2,1,0:T(8,128)(2,1)S(1)} async-done(((bf16[16,96,128]{2,1,0:T(8,128)(2,1)}), bf16[16,96,128]{2,1,0:T(8,128)(2,1)S(1)}, u32[]{:S(2)}, u32[]{:S(2)}) %all-to-all-start.4) | async-done | bytes 393248 | tf_op jit(solution)/shard_map/all_to_all | solution.py:34
  (43 shorter events, 9.2 us)
Async XLA Ops:
  7.2 123.4 %all-gather.3.cloned.1.call-start = ((), (), s32[]{:S(2)}) async-start(), calls=%async_computation.5 | async-start | bytes 3784704 | tf_op jit(solution)/shard_map/all_gather | solution.py:148
  8.9 21.4 %collective-permute-start.1 = (bf16[448,128]{1,0:T(8,128)(2,1)S(1)}, bf16[448,128]{1,0:T(8,128)(2,1)S(1)}, u32[]{:S(2)}, u32[]{:S(2)}) collective-permute-start(bf16[448,128]{1,0:T(8,128)(2,1)S(1)} %get-tuple-element.20), channel_id=1, source_target_pairs={{0,384},{128,0},{256,128},{384,256},{1,385},{129,1},{257,129},{385... | collective-permute-start | bytes 344072 | tf_op jit(solution)/shard_map/ppermute | solution.py:30
  19.8 14.6 %collective-permute-start = (bf16[448,128]{1,0:T(8,128)(2,1)S(1)}, bf16[448,128]{1,0:T(8,128)(2,1)S(1)}, u32[]{:S(2)}, u32[]{:S(2)}) collective-permute-start(bf16[448,128]{1,0:T(8,128)(2,1)S(1)} %get-tuple-element.20), channel_id=1, source_target_pairs={{0,128},{128,256},{256,384},{384,0},{1,129},{129,257},{257,385},{3... | collective-permute-start | bytes 344072 | tf_op jit(solution)/shard_map/ppermute | solution.py:30
  21.8 12.7 %collective-permute-start.2 = (bf16[448,128]{1,0:T(8,128)(2,1)S(1)}, bf16[448,128]{1,0:T(8,128)(2,1)S(1)}, u32[]{:S(2)}, u32[]{:S(2)}) collective-permute-start(bf16[448,128]{1,0:T(8,128)(2,1)S(1)} %get-tuple-element.20), channel_id=1, source_target_pairs={{0,256},{128,384},{256,0},{384,128},{1,257},{129,385},{257,1},{385... | collective-permute-start | bytes 344072 | tf_op jit(solution)/shard_map/ppermute | solution.py:30
  29.0 21.3 %copy-start.5 = (bf16[128,128]{1,0:T(8,128)(2,1)S(1)}, bf16[128,128]{1,0:T(8,128)(2,1)}, u32[]{:S(2)}) copy-start(bf16[128,128]{1,0:T(8,128)(2,1)} %constant.28.clone.table_ref) | copy-start | bytes 98308
  29.5 41.8 %copy-start.7 = (s32[192]{0:T(256)S(1)}, s32[192]{0:T(256)}, u32[]{:S(2)}) copy-start(s32[192]{0:T(256)} %param.13) | copy-start | bytes 2308
  29.5 41.8 %copy-start.6 = (bf16[192,256]{1,0:T(8,128)(2,1)S(1)}, bf16[192,256]{1,0:T(8,128)(2,1)}, u32[]{:S(2)}) copy-start(bf16[192,256]{1,0:T(8,128)(2,1)} %param.10) | copy-start | bytes 294916
  34.5 15.8 %all-to-all-start = ((bf16[16,96,128]{2,1,0:T(8,128)(2,1)}), bf16[16,96,128]{2,1,0:T(8,128)(2,1)S(1)}, u32[]{:S(2)}, u32[]{:S(2)}) async-start(bf16[16,96,128]{2,1,0:T(8,128)(2,1)} %pad.4), calls=%async_computation | async-start | bytes 786432 | tf_op jit(solution)/shard_map/all_to_all | solution.py:34
  40.0 18.0 %collective-permute-start.4 = (bf16[4,448,128]{2,1,0:T(8,128)(2,1)S(1)}, bf16[4,448,128]{2,1,0:T(8,128)(2,1)S(1)}, u32[]{:S(2)}, u32[]{:S(2)}) collective-permute-start(bf16[4,448,128]{2,1,0:T(8,128)(2,1)S(1)} %pad_maximum_fusion.refs_0_), channel_id=1, source_target_pairs={{0,112},{16,0},{32,16},{48,32},{64,48},{80,64},{96,80},{112,96},{1... | collective-permute-start | bytes 1376264 | tf_op jit(solution)/shard_map/ppermute | solution.py:30
  42.3 16.3 %collective-permute-start.3 = (bf16[4,448,128]{2,1,0:T(8,128)(2,1)S(1)}, bf16[4,448,128]{2,1,0:T(8,128)(2,1)S(1)}, u32[]{:S(2)}, u32[]{:S(2)}) collective-permute-start(bf16[4,448,128]{2,1,0:T(8,128)(2,1)S(1)} %pad_maximum_fusion.refs_0_), channel_id=1, source_target_pairs={{0,16},{16,32},{32,48},{48,64},{64,80},{80,96},{96,112},{112,0},{1... | collective-permute-start | bytes 1376264 | tf_op jit(solution)/shard_map/ppermute | solution.py:30
  58.0 31.3 %copy-start.1 = (bf16[4,448,128]{2,1,0:T(8,128)(2,1)}, bf16[4,448,128]{2,1,0:T(8,128)(2,1)S(1)}, u32[]{:S(2)}) copy-start(bf16[4,448,128]{2,1,0:T(8,128)(2,1)S(1)} %collective-permute-done.4.refs_2_) | copy-start | bytes 1376260
  58.6 30.7 %copy-start.3 = (bf16[4,448,128]{2,1,0:T(8,128)(2,1)}, bf16[4,448,128]{2,1,0:T(8,128)(2,1)S(1)}, u32[]{:S(2)}) copy-start(bf16[4,448,128]{2,1,0:T(8,128)(2,1)S(1)} %collective-permute-done.3.refs_1_) | copy-start | bytes 1376260
  58.6 30.7 %all-to-all-start.1 = ((bf16[16,96,128]{2,1,0:T(8,128)(2,1)}), bf16[16,96,128]{2,1,0:T(8,128)(2,1)S(1)}, u32[]{:S(2)}, u32[]{:S(2)}) async-start(bf16[16,96,128]{2,1,0:T(8,128)(2,1)} %shard_map.95), calls=%async_computation.1 | async-start | bytes 786432 | tf_op jit(solution)/shard_map/all_to_all | solution.py:34
  63.8 19.6 %collective-permute-start.5 = (bf16[4,448,128]{2,1,0:T(8,128)(2,1)S(1)}, bf16[4,448,128]{2,1,0:T(8,128)(2,1)}, u32[]{:S(2)}, u32[]{:S(2)}) collective-permute-start(bf16[4,448,128]{2,1,0:T(8,128)(2,1)S(1)} %collective-permute-done.3.refs_1_), channel_id=1, source_target_pairs={{0,16},{16,32},{32,48},{48,64},{64,80},{80,96},{96,112},{112,0},{1... | collective-permute-start | bytes 1376264 | tf_op jit(solution)/shard_map/ppermute | solution.py:30
  69.4 18.6 %collective-permute-start.6 = (bf16[4,448,128]{2,1,0:T(8,128)(2,1)S(1)}, bf16[4,448,128]{2,1,0:T(8,128)(2,1)}, u32[]{:S(2)}, u32[]{:S(2)}) collective-permute-start(bf16[4,448,128]{2,1,0:T(8,128)(2,1)S(1)} %collective-permute-done.4.refs_2_), channel_id=1, source_target_pairs={{0,112},{16,0},{32,16},{48,32},{64,48},{80,64},{96,80},{112,96},{1... | collective-permute-start | bytes 1376264 | tf_op jit(solution)/shard_map/ppermute | solution.py:30
  89.3 41.3 %all-to-all-start.2 = ((bf16[16,192,256]{2,1,0:T(8,128)(2,1)}), bf16[16,192,256]{2,1,0:T(8,128)(2,1)S(1)}, u32[]{:S(2)}, u32[]{:S(2)}) async-start(bf16[16,192,256]{2,1,0:T(8,128)(2,1)} %broadcast_in_dim.4), calls=%async_computation.2 | async-start | bytes 3145728 | tf_op jit(solution)/shard_map/all_to_all | solution.py:34
  94.3 19.4 %collective-permute-start.7 = (bf16[4,448,128]{2,1,0:T(8,128)(2,1)}, bf16[4,448,128]{2,1,0:T(8,128)(2,1)S(1)}, u32[]{:S(2)}, u32[]{:S(2)}) collective-permute-start(bf16[4,448,128]{2,1,0:T(8,128)(2,1)} %collective-permute-done.5.refs_3_), channel_id=1, source_target_pairs={{0,16},{16,32},{32,48},{48,64},{64,80},{80,96},{96,112},{112,0},{1... | collective-permute-start | bytes 1376264 | tf_op jit(solution)/shard_map/ppermute | solution.py:30
  96.5 22.8 %collective-permute-start.8 = (bf16[4,448,128]{2,1,0:T(8,128)(2,1)}, bf16[4,448,128]{2,1,0:T(8,128)(2,1)S(1)}, u32[]{:S(2)}, u32[]{:S(2)}) collective-permute-start(bf16[4,448,128]{2,1,0:T(8,128)(2,1)} %collective-permute-done.6.refs_4_), channel_id=1, source_target_pairs={{0,112},{16,0},{32,16},{48,32},{64,48},{80,64},{96,80},{112,96},{1... | collective-permute-start | bytes 1376264 | tf_op jit(solution)/shard_map/ppermute | solution.py:30
  114.5 10.1 %collective-permute-start.9 = (bf16[4,224,128]{2,1,0:T(8,128)(2,1)}, bf16[4,224,128]{2,1,0:T(8,128)(2,1)}, u32[]{:S(2)}, u32[]{:S(2)}) collective-permute-start(bf16[4,224,128]{2,1,0:T(8,128)(2,1)} %slice.36), channel_id=1, source_target_pairs={{0,16},{16,32},{32,48},{48,64},{64,80},{80,96},{96,112},{112,0},{1... | collective-permute-start | bytes 688136 | tf_op jit(solution)/shard_map/ppermute | solution.py:30
  120.0 10.6 %collective-permute-start.10 = (bf16[4,224,128]{2,1,0:T(8,128)(2,1)}, bf16[4,224,128]{2,1,0:T(8,128)(2,1)}, u32[]{:S(2)}, u32[]{:S(2)}) collective-permute-start(bf16[4,224,128]{2,1,0:T(8,128)(2,1)} %slice.37), channel_id=1, source_target_pairs={{0,112},{16,0},{32,16},{48,32},{64,48},{80,64},{96,80},{112,96},{1... | collective-permute-start | bytes 688136 | tf_op jit(solution)/shard_map/ppermute | solution.py:30
  130.6 2.0 %copy-start = (bf16[14336,128]{1,0:T(8,128)(2,1)S(1)}, bf16[14336,128]{1,0:T(8,128)(2,1)}, u32[]{:S(2)}) copy-start(bf16[14336,128]{1,0:T(8,128)(2,1)} %all-gather.3.cloned.1.call-done) | copy-start | bytes 11010052
  132.7 1.0 copy-start.2
  133.7 1.0 copy-start.4
  172.1 13.0 %all-to-all-start.4 = ((bf16[16,96,128]{2,1,0:T(8,128)(2,1)}), bf16[16,96,128]{2,1,0:T(8,128)(2,1)S(1)}, u32[]{:S(2)}, u32[]{:S(2)}) async-start(bf16[16,96,128]{2,1,0:T(8,128)(2,1)} %shard_map.97), calls=%async_computation.4 | async-start | bytes 786432 | tf_op jit(solution)/shard_map/all_to_all | solution.py:34
Sparse Core Ops, SparseCore 0:
  11.2 107.2 all-gather.2

commit v3 on v0

v3 whole, which is shorter than its diff:
```python
import functools

import jax
import jax.numpy as jnp
import numpy as np
from jax import lax
from jax.experimental import pallas as pl
from jax.experimental.pallas import tpu as pltpu
from jax.sharding import Mesh, PartitionSpec as P

BLK = 128
TENSOR = ("x", "zl", "core")
DP = ("zh", "y")
BF = jnp.bfloat16
F32 = jnp.float32


def sylvester(order):
    index = np.arange(order)
    bits = index[:, None] & index[None, :]
    parity = np.zeros((order, order), np.int64)
    for bit in range(order.bit_length() - 1):
        parity ^= (bits >> bit) & 1
    return 1.0 - 2.0 * parity


def shifted(value, axis, step):
    size = lax.axis_size(axis)
    return lax.ppermute(value, axis, [(i, (i + step) % size) for i in range(size)])


def turned(value):
    return lax.ppermute(value, ("zh", "x"), [(a * 4 + b, b * 4 + a) for a in range(4) for b in range(4)])


def exchange(value, axes=TENSOR):
    return lax.all_to_all(value, axes, 0, 0)


def to_other_core(value):
    return lax.ppermute(value, "core", [(0, 1), (1, 0)])


def two_to(exponents):
    up = jnp.left_shift(1, jnp.maximum(exponents, 0)).astype(F32)
    down = jnp.left_shift(1, jnp.maximum(exponents, -7) + 7).astype(F32) * (1.0 / 128.0)
    return jnp.where(exponents > 0, up, down)


def groups_of(width, rows):
    half = rows // 2
    for g in range(2 * (width // BLK)):
        yield g, slice((g % 2) * half, (g % 2 + 1) * half), slice((g // 2) * BLK, (g // 2 + 1) * BLK)


def call(kernel, out, arguments, flops, scratch=(), limit=12):
    vmem = pl.BlockSpec(memory_space=pltpu.VMEM)
    smem = pl.BlockSpec(memory_space=pltpu.SMEM)
    return pl.pallas_call(
        kernel,
        out_shape=out,
        in_specs=[smem if a.ndim == 1 else vmem for a in arguments],
        out_specs=jax.tree.map(lambda _: vmem, out),
        scratch_shapes=list(scratch),
        compiler_params=pltpu.CompilerParams(vmem_limit_bytes=limit * 2**20),
        cost_estimate=pl.CostEstimate(flops=flops, bytes_accessed=2_000_000, transcendentals=0),
    )(*arguments)


def spread_kernel(hidden_ref, weight_ref, sign_ref, exponent_ref, out_ref):
    rows, width = hidden_ref.shape
    flips = (1 - 2 * sign_ref[...]).astype(F32)
    scale = two_to(-exponent_ref[...])
    for g, at, units in groups_of(width, rows):
        signed = hidden_ref[at, units].astype(F32) * flips[:, units] * scale[at, :]
        out_ref[g, : rows // 2, :] = signed.astype(BF)
    for b in range(width // BLK):
        block = jnp.transpose(weight_ref[b * BLK : (b + 1) * BLK, :].astype(F32)).astype(BF)
        for h in range(2):
            out_ref[2 * b + h, rows // 2 :, :] = block[h * (BLK // 2) : (h + 1) * (BLK // 2), :]
    for g in range(2 * (width // BLK), out_ref.shape[0]):
        out_ref[g] = jnp.zeros(out_ref.shape[1:], BF)


def hadamard_kernel(clipped, limit, table_ref, x_ref, out_ref, mixed_ref):
    parts, rows, _ = x_ref.shape
    for n in range(parts):
        mixed_ref[n] = jnp.dot(x_ref[n], table_ref[...], preferred_element_type=F32)
    factor = 1.0 / float(parts * BLK) ** 0.5
    for r in range(rows // 16):
        at = pl.ds(r * 16, 16)
        values = [mixed_ref[n, at, :] for n in range(parts)]
        apart = 1
        while apart < parts:
            values = [
                values[n ^ apart] - values[n] if n & apart else values[n] + values[n ^ apart]
                for n in range(parts)
            ]
            apart *= 2
        for n in range(parts):
            done = values[n] * factor
            if r * 16 < clipped:
                done = jnp.clip(done, -limit, limit)
            out_ref[n, at, :] = done.astype(BF)


def forward_kernel(place_ref, weight_ref, own_ref, prev_ref, next_ref, first_ref, second_ref, keep_ref, give_ref, act_ref):
    _, rows, width = act_ref.shape
    split = first_ref.shape[0]
    for g, at, units in groups_of(width, rows):
        act_ref[0, at, units] = own_ref[g]
        act_ref[1, at, units] = prev_ref[g]
        act_ref[2, at, units] = next_ref[g]
        act_ref[3, at, units] = first_ref[g] if g < split else second_ref[g - split]
    core = place_ref[1]
    for out_ref, column in ((give_ref, 1 - core), (keep_ref, core)):
        for zl in range(2):
            at = 2 * (2 * zl + column)
            w = jnp.concatenate([weight_ref[at], weight_ref[at + 1]], 1)
            for k, away in enumerate((0, 3, 1, 2)):
                block = lax.rem(place_ref[0] + away, 4)
                part = jnp.dot(act_ref[k], w, preferred_element_type=F32)
                out_ref[block * 2 + zl] = part.astype(BF)


def back_kernel(place_ref, grad_ref, cross_ref, groups_ref, far_ref, next_ref, prev_ref, kept_ref, weight_ref):
    each, width = groups_ref.shape[2], weight_ref.shape[1]
    for y in range(groups_ref.shape[0]):
        for g in range(groups_ref.shape[1]):
            top = (2 * y + g % 2) * each
            weight_ref[top : top + each, (g // 2) * BLK : (g // 2 + 1) * BLK] = groups_ref[y, g]
    cols = grad_ref.shape[2]
    for out_ref, away in ((far_ref, 2), (next_ref, 1), (prev_ref, 3), (kept_ref, 0)):
        block = lax.rem(place_ref[0] + away, 4)
        total = None
        for from_ref, column in ((grad_ref, place_ref[1]), (cross_ref, 1 - place_ref[1])):
            for zl in range(2):
                w = weight_ref[pl.ds(pl.multiple_of((2 * zl + column) * cols, cols), cols), :]
                term = jnp.dot(from_ref[block * 2 + zl], w, preferred_element_type=F32)
                total = term if total is None else total + term
        out_ref[...] = total.astype(out_ref.dtype)


def local(hidden, down_rotated, out_gradient, sign_bits, act_exponent, grad_exponent):
    rows, width = hidden.shape
    parts = 16
    cols = out_gradient.shape[1]
    half = rows // 2
    used = 2 * (width // BLK)
    lines = half + BLK // 2

    weight = lax.all_gather(down_rotated, "y", axis=0)
    grad_factor = jnp.exp2(grad_exponent.astype(F32))[:, None]
    grad_local = jnp.clip(out_gradient.astype(F32) / grad_factor, -127.0, 127.0).astype(BF)

    spread = jax.ShapeDtypeStruct((parts, lines, BLK), BF)
    signed = call(spread_kernel, spread, (hidden, down_rotated, sign_bits[None, :], act_exponent[:, None]), 1_000_000)
    arrived = exchange(signed)
    arrived, grad_local = lax.optimization_barrier((arrived, grad_local))
    turned_grad = turned(grad_local)
    whole = call(
        functools.partial(hadamard_kernel, half, 127.0),
        spread,
        (jnp.asarray(sylvester(BLK), BF), arrived),
        2 * arrived.size * BLK,
        [pltpu.VMEM((parts, lines, BLK), F32)],
    )
    home = exchange(whole)
    rotated_weight = lax.all_gather(home[:used, half:], "y", axis=0)
    own = home[:used, :half]
    own, turned_grad = lax.optimization_barrier((own, turned_grad))
    grads = exchange(jnp.broadcast_to(turned_grad[None], (parts // 2, rows, cols)), ("x", "zl"))
    cross_grads = to_other_core(grads)
    prev, following = shifted(own, "zh", 1), shifted(own, "zh", -1)
    first, second = shifted(prev[: used // 2], "zh", 1), shifted(following[used // 2 :], "zh", -1)

    place = jnp.stack([lax.axis_index("zh"), lax.axis_index("core")]).astype(jnp.int32)
    dots = 2 * rows * width * 4096
    shares = jax.ShapeDtypeStruct((parts // 2, rows, cols), BF)
    keep, give = call(
        forward_kernel,
        (shares, shares),
        (place, weight, own, prev, following, first, second),
        dots,
        [pltpu.VMEM((4, rows, width), BF)],
    )
    both = (keep.astype(F32) + to_other_core(give).astype(F32)).astype(BF)
    sums = exchange(both, ("x", "zl"))
    block = jax.ShapeDtypeStruct((rows, width), BF)
    far, upper, lower, kept = call(
        back_kernel,
        (block, block, block, jax.ShapeDtypeStruct((rows, width), F32)),
        (place, grads, cross_grads, rotated_weight),
        dots,
        [pltpu.VMEM((4 * cols, width), BF)],
    )
    one, two = shifted(far[:half], "zh", 1), shifted(far[half:], "zh", -1)
    upper = jnp.concatenate([(upper[:half].astype(F32) + one.astype(F32)).astype(BF), upper[half:]])
    lower = jnp.concatenate([lower[:half], (lower[half:].astype(F32) + two.astype(F32)).astype(BF)])
    one, two = shifted(upper, "zh", 1), shifted(lower, "zh", -1)
    flips = (1 - 2 * sign_bits).astype(F32)
    grad_hidden = (kept + one.astype(F32) + two.astype(F32)) * grad_factor * flips[None, :]

    summed = turned(jnp.sum(sums.astype(F32), 0).astype(BF))
    mixed = summed.astype(F32) * jnp.exp2(act_exponent.astype(F32))[:, None]
    return mixed.astype(BF), grad_hidden.astype(BF)


def solution(mesh):
    fine = Mesh(mesh.devices.reshape(4, 8, 4, 2, 2), DP + TENSOR)
    in_specs = (P(DP, TENSOR), P(TENSOR, DP), P(DP, TENSOR), P(TENSOR), P(DP), P(DP))
    out_specs = (P(DP, TENSOR), P(DP, TENSOR))
    return jax.shard_map(local, mesh=fine, in_specs=in_specs, out_specs=out_specs, check_vma=False)
```

time: 364 us -> 179 us (0.49)
  the two profiles are of different devices: /device:TPU:8 before, /device:TPU:47 now
where the time goes in v3:
time: 179 us; the launch traced here: 178 us
  starting transfers between devices  78.8 us (44%)
  waiting for transfers between devices  48 us (27%)
  blocking collectives  15.7 us (9%)
  between operations  14.4 us (8%)
  local copies, waits for them, and re-layouts  8.18 us (5%)
  Pallas kernels  7.29 us (4%)
  other arithmetic  5.41 us (3%)
    ppermute x8, starting transfers between devices, shifted(): lax.ppermute(value, axis, [(i, (i + step) % size) for i in range(size)])  33.3 us
    ppermute x8, waiting for transfers between devices, shifted(): lax.ppermute(value, axis, [(i, (i + step) % size) for i in range(size)])  30.3 us
    all_to_all x3, starting transfers between devices, exchange(): return lax.all_to_all(value, axes, 0, 0)  21.5 us
    ppermute x2, starting transfers between devices, turned(): lax.ppermute(value, ('zh', 'x'), [(a * 4 + b, b * 4 + a) for a in range(4...  18.1 us
    all_to_all x1, blocking collectives, exchange(): return lax.all_to_all(value, axes, 0, 0)  15.7 us
    all_to_all x3, waiting for transfers between devices, exchange(): return lax.all_to_all(value, axes, 0, 0)  10.6 us
    pallas_call x4, Pallas kernels, call(): pl.pallas_call(kernel, out_shape=out, in_specs=[smem if a.ndim == 1 else...  7.29 us
    ppermute x2, waiting for transfers between devices, turned(): lax.ppermute(value, ('zh', 'x'), [(a * 4 + b, b * 4 + a) for a in range(4...  6.09 us
  transfers between devices with their start and end apart: 17, of which 8 were waited for; matrix products, arithmetic and copies ran while one was open for 4% of the time, Pallas kernels for 4%

profile of v3, /device:TPU:47, one launch (start us, length us, event | category | flops | bytes accessed | tf_op | source)
XLA Modules:
  0.0 177.7 jit_solution(12859509505062080930)
XLA Ops:
  10.4 1.0 copy-done.1
  11.3 1.1 shard_map.86
  12.4 6.9 %all-to-all-start = ((bf16[16,160,128]{2,1,0:T(8,128)(2,1)}), bf16[16,160,128]{2,1,0:T(8,128)(2,1)S(1)}, u32[]{:S(2)}, u32[]{:S(2)}) async-start(bf16[16,160,128]{2,1,0:T(8,128)(2,1)} %shard_map.86), calls=%async_computation | async-start | bytes 1310720 | tf_op jit(solution)/shard_map/all_to_all | solution.py:37
  19.5 9.0 %all-to-all-done.x_ref = bf16[16,160,128]{2,1,0:T(8,128)(2,1)S(1)} async-done(((bf16[16,160,128]{2,1,0:T(8,128)(2,1)}), bf16[16,160,128]{2,1,0:T(8,128)(2,1)S(1)}, u32[]{:S(2)}, u32[]{:S(2)}) %all-to-all-start) | async-done | bytes 655392 | tf_op jit(solution)/shard_map/all_to_all | solution.py:37
  29.0 15.7 %all_to_all.20 = bf16[16,160,128]{2,1,0:T(8,128)(2,1)S(1)} all-to-all(bf16[16,160,128]{2,1,0:T(8,128)(2,1)S(1)} %shard_map.87), channel_id=1, replica_groups=mesh['zh'=4,'y'=8,'x'=4,'zl'=2,'core'=2] {'x','zl','core'}, dimensions={0} | all-to-all | bytes 1310720 | tf_op jit(solution)/shard_map/all_to_all | solution.py:37
  45.4 11.4 %collective-permute-start = (bf16[192,256]{1,0:T(8,128)(2,1)S(1)}, bf16[192,256]{1,0:T(8,128)(2,1)S(1)}, u32[]{:S(2)}, u32[]{:S(2)}) collective-permute-start(bf16[192,256]{1,0:T(8,128)(2,1)S(1)} %clamp_convert_fusion), channel_id=1, source_target_pairs={{0,0},{4,128},{8,256},{12,384},{128,4},{132,132},{136,260},{140,38... | collective-permute-start | bytes 294920 | tf_op jit(solution)/shard_map/ppermute | solution.py:33
  56.8 6.1 %collective-permute-done = bf16[192,256]{1,0:T(8,128)(2,1)S(1)} collective-permute-done((bf16[192,256]{1,0:T(8,128)(2,1)S(1)}, bf16[192,256]{1,0:T(8,128)(2,1)S(1)}, u32[]{:S(2)}, u32[]{:S(2)}) %collective-permute-start) | collective-permute-done | bytes 98336 | tf_op jit(solution)/shard_map/ppermute | solution.py:33
  62.9 1.9 %collective-permute-start.1 = (bf16[14,96,128]{2,1,0:T(8,128)(2,1)S(1)}, bf16[14,96,128]{2,1,0:T(8,128)(2,1)S(1)}, u32[]{:S(2)}, u32[]{:S(2)}) collective-permute-start(bf16[14,96,128]{2,1,0:T(8,128)(2,1)S(1)} %slice.40.own_ref), channel_id=1, source_target_pairs={{0,128},{128,256},{256,384},{384,0},{1,129},{129,257},{257,385},{3... | collective-permute-start | bytes 1032200 | tf_op jit(solution)/shard_map/ppermute | solution.py:29
  64.8 5.5 %collective-permute-start.2 = (bf16[14,96,128]{2,1,0:T(8,128)(2,1)S(1)}, bf16[14,96,128]{2,1,0:T(8,128)(2,1)S(1)}, u32[]{:S(2)}, u32[]{:S(2)}) collective-permute-start(bf16[14,96,128]{2,1,0:T(8,128)(2,1)S(1)} %slice.40.own_ref), channel_id=1, source_target_pairs={{0,384},{128,0},{256,128},{384,256},{1,385},{129,1},{257,129},{385... | collective-permute-start | bytes 1032200 | tf_op jit(solution)/shard_map/ppermute | solution.py:29
  70.3 0.9 broadcast_in_dim.8
  71.2 6.8 %all-to-all-start.3 = ((bf16[8,192,256]{2,1,0:T(8,128)(2,1)}), bf16[8,192,256]{2,1,0:T(8,128)(2,1)S(1)}, u32[]{:S(2)}, u32[]{:S(2)}) async-start(bf16[8,192,256]{2,1,0:T(8,128)(2,1)} %broadcast_in_dim.8), calls=%async_computation.3 | async-start | bytes 1572864 | tf_op jit(solution)/shard_map/all_to_all | solution.py:37
  78.0 2.3 %collective-permute-done.1.prev_ref = bf16[14,96,128]{2,1,0:T(8,128)(2,1)S(1)} collective-permute-done((bf16[14,96,128]{2,1,0:T(8,128)(2,1)S(1)}, bf16[14,96,128]{2,1,0:T(8,128)(2,1)S(1)}, u32[]{:S(2)}, u32[]{:S(2)}) %collective-permute-start.1) | collective-permute-done | bytes 344096 | tf_op jit(solution)/shard_map/ppermute | solution.py:29
  80.3 1.9 %collective-permute-start.3 = (bf16[7,96,128]{2,1,0:T(8,128)(2,1)S(1)}, bf16[7,96,128]{2,1,0:T(8,128)(2,1)S(1)}, u32[]{:S(2)}, u32[]{:S(2)}) collective-permute-start(bf16[7,96,128]{2,1,0:T(8,128)(2,1)S(1)} %slice.41), channel_id=1, source_target_pairs={{0,128},{128,256},{256,384},{384,0},{1,129},{129,257},{257,385},{3... | collective-permute-start | bytes 516104 | tf_op jit(solution)/shard_map/ppermute | solution.py:29
  82.2 5.5 %collective-permute-start.4 = (bf16[7,96,128]{2,1,0:T(8,128)(2,1)S(1)}, bf16[7,96,128]{2,1,0:T(8,128)(2,1)S(1)}, u32[]{:S(2)}, u32[]{:S(2)}) collective-permute-start(bf16[7,96,128]{2,1,0:T(8,128)(2,1)S(1)} %slice.42), channel_id=1, source_target_pairs={{0,384},{128,0},{256,128},{384,256},{1,385},{129,1},{257,129},{385... | collective-permute-start | bytes 516104 | tf_op jit(solution)/shard_map/ppermute | solution.py:29
  87.8 9.0 %collective-permute-done.3.first_ref = bf16[7,96,128]{2,1,0:T(8,128)(2,1)S(1)} collective-permute-done((bf16[7,96,128]{2,1,0:T(8,128)(2,1)S(1)}, bf16[7,96,128]{2,1,0:T(8,128)(2,1)S(1)}, u32[]{:S(2)}, u32[]{:S(2)}) %collective-permute-start.3) | collective-permute-done | bytes 172064 | tf_op jit(solution)/shard_map/ppermute | solution.py:29
  96.8 1.5 copy-done.4
  98.3 3.1 %shard_map.88 = (bf16[8,192,256]{2,1,0:T(8,128)(2,1)S(1)}, bf16[8,192,256]{2,1,0:T(8,128)(2,1)}) custom-call(s32[2]{0:T(128)S(1)} %pad_add_fusion.place_ref, bf16[8,896,128]{2,1,0:T(8,128)(2,1)S(1)} %bitcast.6, bf16[14,96,128]{2,1,0:T(8,128)(2,1)S(1)} %slice.40.own_ref, bf16[14,96,128]{2,1,0:T(8,128)(2,1)S(1)} %collective-permute-done.1.prev_ref, ...), custom_call_target="tpu_custom_call" | custom-call | flops 1409286144 | bytes 2000000 | tf_op jit(solution)/shard_map/pallas_call | solution.py:59
  101.4 3.9 %collective-permute-start.5 = (bf16[8,192,256]{2,1,0:T(8,128)(2,1)}, bf16[8,192,256]{2,1,0:T(8,128)(2,1)}, u32[]{:S(2)}, u32[]{:S(2)}) collective-permute-start(bf16[8,192,256]{2,1,0:T(8,128)(2,1)} %get-tuple-element.16), channel_id=1, source_target_pairs={{0,1},{1,0},{2,3},{3,2},{4,5},{5,4},{6,7},{7,6},{8,9},{9,8},{10,11... | collective-permute-start | bytes 2359304 | tf_op jit(solution)/shard_map/ppermute | solution.py:41
  105.3 1.9 %collective-permute-start.7 = (bf16[8,192,256]{2,1,0:T(8,128)(2,1)S(1)}, bf16[8,192,256]{2,1,0:T(8,128)(2,1)S(1)}, u32[]{:S(2)}, u32[]{:S(2)}) collective-permute-start(bf16[8,192,256]{2,1,0:T(8,128)(2,1)S(1)} %all-to-all-done.3.grad_ref), channel_id=1, source_target_pairs={{0,1},{1,0},{2,3},{3,2},{4,5},{5,4},{6,7},{7,6},{8,9},{9,8},{10,11... | collective-permute-start | bytes 2359304 | tf_op jit(solution)/shard_map/ppermute | solution.py:41
  107.5 2.2 %add_convert_fusion = bf16[8,192,256]{2,1,0:T(8,128)(2,1)} fusion(bf16[8,192,256]{2,1,0:T(8,128)(2,1)} %collective-permute-done.5, bf16[8,192,256]{2,1,0:T(8,128)(2,1)S(1)} %get-tuple-element.15), kind=kLoop, calls=%fused_computation | loop fusion | flops 1572864 | bytes 2359296 | tf_op jit(solution)/shard_map/convert_element_type | solution.py:187
  109.7 7.8 %all-to-all-start.2 = ((bf16[8,192,256]{2,1,0:T(8,128)(2,1)}), bf16[8,192,256]{2,1,0:T(8,128)(2,1)}, u32[]{:S(2)}, u32[]{:S(2)}) async-start(bf16[8,192,256]{2,1,0:T(8,128)(2,1)} %add_convert_fusion), calls=%async_computation.2 | async-start | bytes 1572864 | tf_op jit(solution)/shard_map/all_to_all | solution.py:37
  117.5 1.5 copy-done.3
  119.0 2.7 %shard_map.89 = (bf16[192,896]{1,0:T(8,128)(2,1)S(1)}, bf16[192,896]{1,0:T(8,128)(2,1)S(1)}, bf16[192,896]{1,0:T(8,128)(2,1)S(1)}, f32[192,896]{1,0:T(8,128)S(1)}) custom-call(s32[2]{0:T(128)S(1)} %pad_add_fusion.place_ref, bf16[8,192,256]{2,1,0:T(8,128)(2,1)S(1)} %all-to-all-done.3.grad_ref, bf16[8,192,256]{2,1,0:T(8,128)(2,1)S(1)} %collective-permute-done.7.cross_ref, ...), custom_call_target="tpu_custom_call" | custom-call | flops 1409286144 | bytes 2000000 | tf_op jit(solution)/shard_map/pallas_call | solution.py:59
  121.7 4.5 %collective-permute-start.8 = (bf16[96,896]{1,0:T(8,128)(2,1)S(1)}, bf16[96,896]{1,0:T(8,128)(2,1)S(1)}, u32[]{:S(2)}, u32[]{:S(2)}) collective-permute-start(bf16[96,896]{1,0:T(8,128)(2,1)S(1)} %get-tuple-element.22), channel_id=1, source_target_pairs={{0,128},{128,256},{256,384},{384,0},{1,129},{129,257},{257,385},{3... | collective-permute-start | bytes 516104 | tf_op jit(solution)/shard_map/ppermute | solution.py:29
  126.2 1.6 all-to-all-done.2
  127.8 1.2 reduce_sum.12
  129.1 6.8 %collective-permute-start.6 = (bf16[192,256]{1,0:T(8,128)(2,1)S(1)}, bf16[192,256]{1,0:T(8,128)(2,1)S(1)}, u32[]{:S(2)}, u32[]{:S(2)}) collective-permute-start(bf16[192,256]{1,0:T(8,128)(2,1)S(1)} %reduce_sum.12), channel_id=1, source_target_pairs={{0,0},{4,128},{8,256},{12,384},{128,4},{132,132},{136,260},{140,38... | collective-permute-start | bytes 294920 | tf_op jit(solution)/shard_map/ppermute | solution.py:33
  135.9 1.9 %collective-permute-start.10 = (bf16[96,896]{1,0:T(8,128)(2,1)S(1)}, bf16[96,896]{1,0:T(8,128)(2,1)S(1)}, u32[]{:S(2)}, u32[]{:S(2)}) collective-permute-start(bf16[96,896]{1,0:T(8,128)(2,1)S(1)} %get-tuple-element.23), channel_id=1, source_target_pairs={{0,384},{128,0},{256,128},{384,256},{1,385},{129,1},{257,129},{385... | collective-permute-start | bytes 516104 | tf_op jit(solution)/shard_map/ppermute | solution.py:29
  137.9 4.3 %collective-permute-start.9 = (bf16[192,896]{1,0:T(8,128)(2,1)S(1)}, bf16[192,896]{1,0:T(8,128)(2,1)S(1)}, u32[]{:S(2)}, u32[]{:S(2)}) collective-permute-start(bf16[192,896]{1,0:T(8,128)(2,1)S(1)} %pad_maximum_fusion), channel_id=1, source_target_pairs={{0,128},{128,256},{256,384},{384,0},{1,129},{129,257},{257,385},{3... | collective-permute-start | bytes 1032200 | tf_op jit(solution)/shard_map/ppermute | solution.py:29
  142.2 4.8 %collective-permute-done.10 = bf16[96,896]{1,0:T(8,128)(2,1)S(1)} collective-permute-done((bf16[96,896]{1,0:T(8,128)(2,1)S(1)}, bf16[96,896]{1,0:T(8,128)(2,1)S(1)}, u32[]{:S(2)}, u32[]{:S(2)}) %collective-permute-start.10) | collective-permute-done | bytes 172064 | tf_op jit(solution)/shard_map/ppermute | solution.py:29
  147.1 7.9 %collective-permute-start.11 = (bf16[192,896]{1,0:T(8,128)(2,1)S(1)}, bf16[192,896]{1,0:T(8,128)(2,1)S(1)}, u32[]{:S(2)}, u32[]{:S(2)}) collective-permute-start(bf16[192,896]{1,0:T(8,128)(2,1)S(1)} %pad_maximum_fusion.1), channel_id=1, source_target_pairs={{0,384},{128,0},{256,128},{384,256},{1,385},{129,1},{257,129},{385... | collective-permute-start | bytes 1032200 | tf_op jit(solution)/shard_map/ppermute | solution.py:29
  155.8 14.2 %collective-permute-done.11 = bf16[192,896]{1,0:T(8,128)(2,1)S(1)} collective-permute-done((bf16[192,896]{1,0:T(8,128)(2,1)S(1)}, bf16[192,896]{1,0:T(8,128)(2,1)S(1)}, u32[]{:S(2)}, u32[]{:S(2)}) %collective-permute-start.11) | collective-permute-done | bytes 344096 | tf_op jit(solution)/shard_map/ppermute | solution.py:29
  (50 shorter events, 6.8 us)
Async XLA Ops:
  7.2 21.3 %copy-start.2 = (bf16[128,128]{1,0:T(8,128)(2,1)S(1)}, bf16[128,128]{1,0:T(8,128)(2,1)}, u32[]{:S(2)}) copy-start(bf16[128,128]{1,0:T(8,128)(2,1)} %constant.25.clone.table_ref) | copy-start | bytes 98308
  7.2 12.2 %copy-start.8 = (s32[192]{0:T(256)S(1)}, s32[192]{0:T(256)}, u32[]{:S(2)}) copy-start(s32[192]{0:T(256)} %param.12) | copy-start | bytes 2308
  7.2 12.2 %copy-start.5 = (bf16[192,256]{1,0:T(8,128)(2,1)S(1)}, bf16[192,256]{1,0:T(8,128)(2,1)}, u32[]{:S(2)}) copy-start(bf16[192,256]{1,0:T(8,128)(2,1)} %param.9) | copy-start | bytes 294916
  7.2 89.6 %all-gather.5.cloned.1.call-start = ((), (), s32[]{:S(2)}) async-start(), calls=%async_computation.4 | async-start | bytes 2064384 | tf_op jit(solution)/shard_map/all_gather | solution.py:152
  9.4 0.9 copy-start
  10.4 1.0 copy-start.1
  12.4 16.1 %all-to-all-start = ((bf16[16,160,128]{2,1,0:T(8,128)(2,1)}), bf16[16,160,128]{2,1,0:T(8,128)(2,1)S(1)}, u32[]{:S(2)}, u32[]{:S(2)}) async-start(bf16[16,160,128]{2,1,0:T(8,128)(2,1)} %shard_map.86), calls=%async_computation | async-start | bytes 1310720 | tf_op jit(solution)/shard_map/all_to_all | solution.py:37
  19.3 98.2 %all-gather.7.cloned.1.call-start = ((), (), s32[]{:S(2)}) async-start(), calls=%async_computation.5 | async-start | bytes 2064384 | tf_op jit(solution)/shard_map/all_gather | solution.py:169
  45.4 17.5 %collective-permute-start = (bf16[192,256]{1,0:T(8,128)(2,1)S(1)}, bf16[192,256]{1,0:T(8,128)(2,1)S(1)}, u32[]{:S(2)}, u32[]{:S(2)}) collective-permute-start(bf16[192,256]{1,0:T(8,128)(2,1)S(1)} %clamp_convert_fusion), channel_id=1, source_target_pairs={{0,0},{4,128},{8,256},{12,384},{128,4},{132,132},{136,260},{140,38... | collective-permute-start | bytes 294920 | tf_op jit(solution)/shard_map/ppermute | solution.py:33
  62.9 17.4 %collective-permute-start.1 = (bf16[14,96,128]{2,1,0:T(8,128)(2,1)S(1)}, bf16[14,96,128]{2,1,0:T(8,128)(2,1)S(1)}, u32[]{:S(2)}, u32[]{:S(2)}) collective-permute-start(bf16[14,96,128]{2,1,0:T(8,128)(2,1)S(1)} %slice.40.own_ref), channel_id=1, source_target_pairs={{0,128},{128,256},{256,384},{384,0},{1,129},{129,257},{257,385},{3... | collective-permute-start | bytes 1032200 | tf_op jit(solution)/shard_map/ppermute | solution.py:29
  64.8 17.4 %collective-permute-start.2 = (bf16[14,96,128]{2,1,0:T(8,128)(2,1)S(1)}, bf16[14,96,128]{2,1,0:T(8,128)(2,1)S(1)}, u32[]{:S(2)}, u32[]{:S(2)}) collective-permute-start(bf16[14,96,128]{2,1,0:T(8,128)(2,1)S(1)} %slice.40.own_ref), channel_id=1, source_target_pairs={{0,384},{128,0},{256,128},{384,256},{1,385},{129,1},{257,129},{385... | collective-permute-start | bytes 1032200 | tf_op jit(solution)/shard_map/ppermute | solution.py:29
  71.2 34.1 %all-to-all-start.3 = ((bf16[8,192,256]{2,1,0:T(8,128)(2,1)}), bf16[8,192,256]{2,1,0:T(8,128)(2,1)S(1)}, u32[]{:S(2)}, u32[]{:S(2)}) async-start(bf16[8,192,256]{2,1,0:T(8,128)(2,1)} %broadcast_in_dim.8), calls=%async_computation.3 | async-start | bytes 1572864 | tf_op jit(solution)/shard_map/all_to_all | solution.py:37
  80.3 16.5 %collective-permute-start.3 = (bf16[7,96,128]{2,1,0:T(8,128)(2,1)S(1)}, bf16[7,96,128]{2,1,0:T(8,128)(2,1)S(1)}, u32[]{:S(2)}, u32[]{:S(2)}) collective-permute-start(bf16[7,96,128]{2,1,0:T(8,128)(2,1)S(1)} %slice.41), channel_id=1, source_target_pairs={{0,128},{128,256},{256,384},{384,0},{1,129},{129,257},{257,385},{3... | collective-permute-start | bytes 516104 | tf_op jit(solution)/shard_map/ppermute | solution.py:29
  82.2 14.6 %collective-permute-start.4 = (bf16[7,96,128]{2,1,0:T(8,128)(2,1)S(1)}, bf16[7,96,128]{2,1,0:T(8,128)(2,1)S(1)}, u32[]{:S(2)}, u32[]{:S(2)}) collective-permute-start(bf16[7,96,128]{2,1,0:T(8,128)(2,1)S(1)} %slice.42), channel_id=1, source_target_pairs={{0,384},{128,0},{256,128},{384,256},{1,385},{129,1},{257,129},{385... | collective-permute-start | bytes 516104 | tf_op jit(solution)/shard_map/ppermute | solution.py:29
  96.8 1.5 copy-start.4
  101.4 6.2 %collective-permute-start.5 = (bf16[8,192,256]{2,1,0:T(8,128)(2,1)}, bf16[8,192,256]{2,1,0:T(8,128)(2,1)}, u32[]{:S(2)}, u32[]{:S(2)}) collective-permute-start(bf16[8,192,256]{2,1,0:T(8,128)(2,1)} %get-tuple-element.16), channel_id=1, source_target_pairs={{0,1},{1,0},{2,3},{3,2},{4,5},{5,4},{6,7},{7,6},{8,9},{9,8},{10,11... | collective-permute-start | bytes 2359304 | tf_op jit(solution)/shard_map/ppermute | solution.py:41
  105.3 12.2 %collective-permute-start.7 = (bf16[8,192,256]{2,1,0:T(8,128)(2,1)S(1)}, bf16[8,192,256]{2,1,0:T(8,128)(2,1)S(1)}, u32[]{:S(2)}, u32[]{:S(2)}) collective-permute-start(bf16[8,192,256]{2,1,0:T(8,128)(2,1)S(1)} %all-to-all-done.3.grad_ref), channel_id=1, source_target_pairs={{0,1},{1,0},{2,3},{3,2},{4,5},{5,4},{6,7},{7,6},{8,9},{9,8},{10,11... | collective-permute-start | bytes 2359304 | tf_op jit(solution)/shard_map/ppermute | solution.py:41
  109.7 18.1 %all-to-all-start.2 = ((bf16[8,192,256]{2,1,0:T(8,128)(2,1)}), bf16[8,192,256]{2,1,0:T(8,128)(2,1)}, u32[]{:S(2)}, u32[]{:S(2)}) async-start(bf16[8,192,256]{2,1,0:T(8,128)(2,1)} %add_convert_fusion), calls=%async_computation.2 | async-start | bytes 1572864 | tf_op jit(solution)/shard_map/all_to_all | solution.py:37
  117.5 1.5 copy-start.3
  119.0 7.2 %copy-start.6 = (s32[896]{0:T(1024)S(1)}, s32[896]{0:T(1024)}, u32[]{:S(2)}) copy-start(s32[896]{0:T(1024)} %param.10) | copy-start | bytes 10756
  121.7 16.1 %collective-permute-start.8 = (bf16[96,896]{1,0:T(8,128)(2,1)S(1)}, bf16[96,896]{1,0:T(8,128)(2,1)S(1)}, u32[]{:S(2)}, u32[]{:S(2)}) collective-permute-start(bf16[96,896]{1,0:T(8,128)(2,1)S(1)} %get-tuple-element.22), channel_id=1, source_target_pairs={{0,128},{128,256},{256,384},{384,0},{1,129},{129,257},{257,385},{3... | collective-permute-start | bytes 516104 | tf_op jit(solution)/shard_map/ppermute | solution.py:29
  129.1 26.0 %copy-start.7 = (s32[192]{0:T(256)S(1)}, s32[192]{0:T(256)}, u32[]{:S(2)}) copy-start(s32[192]{0:T(256)} %param.11) | copy-start | bytes 2308
  129.1 26.0 %collective-permute-start.6 = (bf16[192,256]{1,0:T(8,128)(2,1)S(1)}, bf16[192,256]{1,0:T(8,128)(2,1)S(1)}, u32[]{:S(2)}, u32[]{:S(2)}) collective-permute-start(bf16[192,256]{1,0:T(8,128)(2,1)S(1)} %reduce_sum.12), channel_id=1, source_target_pairs={{0,0},{4,128},{8,256},{12,384},{128,4},{132,132},{136,260},{140,38... | collective-permute-start | bytes 294920 | tf_op jit(solution)/shard_map/ppermute | solution.py:33
  135.9 11.2 %collective-permute-start.10 = (bf16[96,896]{1,0:T(8,128)(2,1)S(1)}, bf16[96,896]{1,0:T(8,128)(2,1)S(1)}, u32[]{:S(2)}, u32[]{:S(2)}) collective-permute-start(bf16[96,896]{1,0:T(8,128)(2,1)S(1)} %get-tuple-element.23), channel_id=1, source_target_pairs={{0,384},{128,0},{256,128},{384,256},{1,385},{129,1},{257,129},{385... | collective-permute-start | bytes 516104 | tf_op jit(solution)/shard_map/ppermute | solution.py:29
  137.9 17.9 %collective-permute-start.9 = (bf16[192,896]{1,0:T(8,128)(2,1)S(1)}, bf16[192,896]{1,0:T(8,128)(2,1)S(1)}, u32[]{:S(2)}, u32[]{:S(2)}) collective-permute-start(bf16[192,896]{1,0:T(8,128)(2,1)S(1)} %pad_maximum_fusion), channel_id=1, source_target_pairs={{0,128},{128,256},{256,384},{384,0},{1,129},{129,257},{257,385},{3... | collective-permute-start | bytes 1032200 | tf_op jit(solution)/shard_map/ppermute | solution.py:29
  147.1 22.9 %collective-permute-start.11 = (bf16[192,896]{1,0:T(8,128)(2,1)S(1)}, bf16[192,896]{1,0:T(8,128)(2,1)S(1)}, u32[]{:S(2)}, u32[]{:S(2)}) collective-permute-start(bf16[192,896]{1,0:T(8,128)(2,1)S(1)} %pad_maximum_fusion.1), channel_id=1, source_target_pairs={{0,384},{128,0},{256,128},{384,256},{1,385},{129,1},{257,129},{385... | collective-permute-start | bytes 1032200 | tf_op jit(solution)/shard_map/ppermute | solution.py:29
Sparse Core Ops, SparseCore 0:
  10.1 40.9 all-gather.4
  53.7 41.9 all-gather.6

commit v4 on v3

--- a/solution.py
+++ b/solution.py
@@ -195,6 +195,7 @@
         [pltpu.VMEM((4 * cols, width), BF)],
     )
     one, two = shifted(far[:half], "zh", 1), shifted(far[half:], "zh", -1)
+    one, two, sums = lax.optimization_barrier((one, two, sums))
     upper = jnp.concatenate([(upper[:half].astype(F32) + one.astype(F32)).astype(BF), upper[half:]])
     lower = jnp.concatenate([lower[:half], (lower[half:].astype(F32) + two.astype(F32)).astype(BF)])
     one, two = shifted(upper, "zh", 1), shifted(lower, "zh", -1)

time: 179 us -> 176 us (0.983)
  the two profiles are of different devices: /device:TPU:47 before, /device:TPU:2 now
where the time goes in v4:
time: 176 us; the launch traced here: 175 us
  starting transfers between devices  70.1 us (40%)
  waiting for transfers between devices  54.4 us (31%)
  blocking collectives  15.8 us (9%)
  between operations  14.4 us (8%)
  local copies, waits for them, and re-layouts  8.18 us (5%)
  Pallas kernels  7.29 us (4%)
  other arithmetic  5.4 us (3%)
    ppermute x8, starting transfers between devices, shifted(): lax.ppermute(value, axis, [(i, (i + step) % size) for i in range(size)])  35.6 us
    ppermute x2, waiting for transfers between devices, turned(): lax.ppermute(value, ('zh', 'x'), [(a * 4 + b, b * 4 + a) for a in range(4...  23.8 us
    all_to_all x3, starting transfers between devices, exchange(): return lax.all_to_all(value, axes, 0, 0)  23.4 us
    ppermute x8, waiting for transfers between devices, shifted(): lax.ppermute(value, axis, [(i, (i + step) % size) for i in range(size)])  20.2 us
    all_to_all x1, blocking collectives, exchange(): return lax.all_to_all(value, axes, 0, 0)  15.8 us
    all_to_all x3, waiting for transfers between devices, exchange(): return lax.all_to_all(value, axes, 0, 0)  9.49 us
    pallas_call x4, Pallas kernels, call(): pl.pallas_call(kernel, out_shape=out, in_specs=[smem if a.ndim == 1 else...  7.29 us
    ppermute x2, starting transfers between devices, turned(): lax.ppermute(value, ('zh', 'x'), [(a * 4 + b, b * 4 + a) for a in range(4...  6.72 us
  transfers between devices with their start and end apart: 17, of which 7 were waited for; matrix products, arithmetic and copies ran while one was open for 4% of the time, Pallas kernels for 4%

profile of v4, /device:TPU:2, one launch (start us, length us, event | category | flops | bytes accessed | tf_op | source)
XLA Modules:
  0.0 175.5 jit_solution(7844221760533667252)
XLA Ops:
  9.4 0.9 copy-done
  10.4 1.0 copy-done.1
  11.3 1.1 shard_map.86
  12.4 9.3 %all-to-all-start = ((bf16[16,160,128]{2,1,0:T(8,128)(2,1)}), bf16[16,160,128]{2,1,0:T(8,128)(2,1)S(1)}, u32[]{:S(2)}, u32[]{:S(2)}) async-start(bf16[16,160,128]{2,1,0:T(8,128)(2,1)} %shard_map.86), calls=%async_computation | async-start | bytes 1310720 | tf_op jit(solution)/shard_map/all_to_all | solution.py:37
  21.9 9.5 %all-to-all-done.x_ref = bf16[16,160,128]{2,1,0:T(8,128)(2,1)S(1)} async-done(((bf16[16,160,128]{2,1,0:T(8,128)(2,1)}), bf16[16,160,128]{2,1,0:T(8,128)(2,1)S(1)}, u32[]{:S(2)}, u32[]{:S(2)}) %all-to-all-start) | async-done | bytes 655392 | tf_op jit(solution)/shard_map/all_to_all | solution.py:37
  31.9 15.8 %all_to_all.20 = bf16[16,160,128]{2,1,0:T(8,128)(2,1)S(1)} all-to-all(bf16[16,160,128]{2,1,0:T(8,128)(2,1)S(1)} %shard_map.87), channel_id=1, replica_groups=mesh['zh'=4,'y'=8,'x'=4,'zl'=2,'core'=2] {'x','zl','core'}, dimensions={0} | all-to-all | bytes 1310720 | tf_op jit(solution)/shard_map/all_to_all | solution.py:37
  48.4 4.8 %collective-permute-start = (bf16[192,256]{1,0:T(8,128)(2,1)S(1)}, bf16[192,256]{1,0:T(8,128)(2,1)S(1)}, u32[]{:S(2)}, u32[]{:S(2)}) collective-permute-start(bf16[192,256]{1,0:T(8,128)(2,1)S(1)} %clamp_convert_fusion), channel_id=1, source_target_pairs={{0,0},{4,128},{8,256},{12,384},{128,4},{132,132},{136,260},{140,38... | collective-permute-start | bytes 294920 | tf_op jit(solution)/shard_map/ppermute | solution.py:33
  53.2 6.0 %collective-permute-done = bf16[192,256]{1,0:T(8,128)(2,1)S(1)} collective-permute-done((bf16[192,256]{1,0:T(8,128)(2,1)S(1)}, bf16[192,256]{1,0:T(8,128)(2,1)S(1)}, u32[]{:S(2)}, u32[]{:S(2)}) %collective-permute-start) | collective-permute-done | bytes 98336 | tf_op jit(solution)/shard_map/ppermute | solution.py:33
  59.2 1.9 %collective-permute-start.4 = (bf16[14,96,128]{2,1,0:T(8,128)(2,1)S(1)}, bf16[14,96,128]{2,1,0:T(8,128)(2,1)S(1)}, u32[]{:S(2)}, u32[]{:S(2)}) collective-permute-start(bf16[14,96,128]{2,1,0:T(8,128)(2,1)S(1)} %slice.40.own_ref), channel_id=1, source_target_pairs={{0,128},{128,256},{256,384},{384,0},{1,129},{129,257},{257,385},{3... | collective-permute-start | bytes 1032200 | tf_op jit(solution)/shard_map/ppermute | solution.py:29
  61.1 9.8 %collective-permute-start.5 = (bf16[14,96,128]{2,1,0:T(8,128)(2,1)S(1)}, bf16[14,96,128]{2,1,0:T(8,128)(2,1)S(1)}, u32[]{:S(2)}, u32[]{:S(2)}) collective-permute-start(bf16[14,96,128]{2,1,0:T(8,128)(2,1)S(1)} %slice.40.own_ref), channel_id=1, source_target_pairs={{0,384},{128,0},{256,128},{384,256},{1,385},{129,1},{257,129},{385... | collective-permute-start | bytes 1032200 | tf_op jit(solution)/shard_map/ppermute | solution.py:29
  70.9 0.9 broadcast_in_dim.8
  71.8 7.0 %all-to-all-start.2 = ((bf16[8,192,256]{2,1,0:T(8,128)(2,1)}), bf16[8,192,256]{2,1,0:T(8,128)(2,1)S(1)}, u32[]{:S(2)}, u32[]{:S(2)}) async-start(bf16[8,192,256]{2,1,0:T(8,128)(2,1)} %broadcast_in_dim.8), calls=%async_computation.2 | async-start | bytes 1572864 | tf_op jit(solution)/shard_map/all_to_all | solution.py:37
  78.8 6.0 %collective-permute-done.4.prev_ref = bf16[14,96,128]{2,1,0:T(8,128)(2,1)S(1)} collective-permute-done((bf16[14,96,128]{2,1,0:T(8,128)(2,1)S(1)}, bf16[14,96,128]{2,1,0:T(8,128)(2,1)S(1)}, u32[]{:S(2)}, u32[]{:S(2)}) %collective-permute-start.4) | collective-permute-done | bytes 344096 | tf_op jit(solution)/shard_map/ppermute | solution.py:29
  84.9 1.9 %collective-permute-start.6 = (bf16[7,96,128]{2,1,0:T(8,128)(2,1)S(1)}, bf16[7,96,128]{2,1,0:T(8,128)(2,1)S(1)}, u32[]{:S(2)}, u32[]{:S(2)}) collective-permute-start(bf16[7,96,128]{2,1,0:T(8,128)(2,1)S(1)} %slice.42), channel_id=1, source_target_pairs={{0,128},{128,256},{256,384},{384,0},{1,129},{129,257},{257,385},{3... | collective-permute-start | bytes 516104 | tf_op jit(solution)/shard_map/ppermute | solution.py:29
  86.9 6.0 %collective-permute-start.7 = (bf16[7,96,128]{2,1,0:T(8,128)(2,1)S(1)}, bf16[7,96,128]{2,1,0:T(8,128)(2,1)S(1)}, u32[]{:S(2)}, u32[]{:S(2)}) collective-permute-start(bf16[7,96,128]{2,1,0:T(8,128)(2,1)S(1)} %slice.43), channel_id=1, source_target_pairs={{0,384},{128,0},{256,128},{384,256},{1,385},{129,1},{257,129},{385... | collective-permute-start | bytes 516104 | tf_op jit(solution)/shard_map/ppermute | solution.py:29
  93.0 6.9 %collective-permute-done.6.first_ref = bf16[7,96,128]{2,1,0:T(8,128)(2,1)S(1)} collective-permute-done((bf16[7,96,128]{2,1,0:T(8,128)(2,1)S(1)}, bf16[7,96,128]{2,1,0:T(8,128)(2,1)S(1)}, u32[]{:S(2)}, u32[]{:S(2)}) %collective-permute-start.6) | collective-permute-done | bytes 172064 | tf_op jit(solution)/shard_map/ppermute | solution.py:29
  99.9 1.5 copy-done.4
  101.4 3.1 %shard_map.89 = (bf16[8,192,256]{2,1,0:T(8,128)(2,1)S(1)}, bf16[8,192,256]{2,1,0:T(8,128)(2,1)}) custom-call(s32[2]{0:T(128)S(1)} %pad_add_fusion.place_ref, bf16[8,896,128]{2,1,0:T(8,128)(2,1)S(1)} %bitcast.6, bf16[14,96,128]{2,1,0:T(8,128)(2,1)S(1)} %slice.40.own_ref, bf16[14,96,128]{2,1,0:T(8,128)(2,1)S(1)} %collective-permute-done.4.prev_ref, ...), custom_call_target="tpu_custom_call" | custom-call | flops 1409286144 | bytes 2000000 | tf_op jit(solution)/shard_map/pallas_call | solution.py:59
  104.5 1.9 %collective-permute-start.8 = (bf16[8,192,256]{2,1,0:T(8,128)(2,1)}, bf16[8,192,256]{2,1,0:T(8,128)(2,1)}, u32[]{:S(2)}, u32[]{:S(2)}) collective-permute-start(bf16[8,192,256]{2,1,0:T(8,128)(2,1)} %get-tuple-element.21), channel_id=1, source_target_pairs={{0,1},{1,0},{2,3},{3,2},{4,5},{5,4},{6,7},{7,6},{8,9},{9,8},{10,11... | collective-permute-start | bytes 2359304 | tf_op jit(solution)/shard_map/ppermute | solution.py:41
  106.4 2.4 %collective-permute-start.1 = (bf16[8,192,256]{2,1,0:T(8,128)(2,1)S(1)}, bf16[8,192,256]{2,1,0:T(8,128)(2,1)S(1)}, u32[]{:S(2)}, u32[]{:S(2)}) collective-permute-start(bf16[8,192,256]{2,1,0:T(8,128)(2,1)S(1)} %all-to-all-done.2.grad_ref), channel_id=1, source_target_pairs={{0,1},{1,0},{2,3},{3,2},{4,5},{5,4},{6,7},{7,6},{8,9},{9,8},{10,11... | collective-permute-start | bytes 2359304 | tf_op jit(solution)/shard_map/ppermute | solution.py:41
  109.0 2.2 %add_convert_fusion = bf16[8,192,256]{2,1,0:T(8,128)(2,1)} fusion(bf16[8,192,256]{2,1,0:T(8,128)(2,1)} %collective-permute-done.8, bf16[8,192,256]{2,1,0:T(8,128)(2,1)S(1)} %get-tuple-element.20), kind=kLoop, calls=%fused_computation | loop fusion | flops 1572864 | bytes 2359296 | tf_op jit(solution)/shard_map/convert_element_type | solution.py:187
  111.2 7.2 %all-to-all-start.3 = ((bf16[8,192,256]{2,1,0:T(8,128)(2,1)}), bf16[8,192,256]{2,1,0:T(8,128)(2,1)}, u32[]{:S(2)}, u32[]{:S(2)}) async-start(bf16[8,192,256]{2,1,0:T(8,128)(2,1)} %add_convert_fusion), calls=%async_computation.3 | async-start | bytes 1572864 | tf_op jit(solution)/shard_map/all_to_all | solution.py:37
  118.3 1.5 copy-done.3
  119.8 2.7 %shard_map.88 = (bf16[192,896]{1,0:T(8,128)(2,1)S(1)}, bf16[192,896]{1,0:T(8,128)(2,1)S(1)}, bf16[192,896]{1,0:T(8,128)(2,1)S(1)}, f32[192,896]{1,0:T(8,128)S(1)}) custom-call(s32[2]{0:T(128)S(1)} %pad_add_fusion.place_ref, bf16[8,192,256]{2,1,0:T(8,128)(2,1)S(1)} %all-to-all-done.2.grad_ref, bf16[8,192,256]{2,1,0:T(8,128)(2,1)S(1)} %collective-permute-done.1.cross_ref, ...), custom_call_target="tpu_custom_call" | custom-call | flops 1409286144 | bytes 2000000 | tf_op jit(solution)/shard_map/pallas_call | solution.py:59
  122.5 4.8 %collective-permute-start.2 = (bf16[96,896]{1,0:T(8,128)(2,1)S(1)}, bf16[96,896]{1,0:T(8,128)(2,1)S(1)}, u32[]{:S(2)}, u32[]{:S(2)}) collective-permute-start(bf16[96,896]{1,0:T(8,128)(2,1)S(1)} %get-tuple-element.29), channel_id=1, source_target_pairs={{0,128},{128,256},{256,384},{384,0},{1,129},{129,257},{257,385},{3... | collective-permute-start | bytes 516104 | tf_op jit(solution)/shard_map/ppermute | solution.py:29
  127.4 3.1 %collective-permute-start.3 = (bf16[96,896]{1,0:T(8,128)(2,1)S(1)}, bf16[96,896]{1,0:T(8,128)(2,1)S(1)}, u32[]{:S(2)}, u32[]{:S(2)}) collective-permute-start(bf16[96,896]{1,0:T(8,128)(2,1)S(1)} %get-tuple-element.28), channel_id=1, source_target_pairs={{0,384},{128,0},{256,128},{384,256},{1,385},{129,1},{257,129},{385... | collective-permute-start | bytes 516104 | tf_op jit(solution)/shard_map/ppermute | solution.py:29
  130.6 7.2 %collective-permute-done.2 = bf16[96,896]{1,0:T(8,128)(2,1)S(1)} collective-permute-done((bf16[96,896]{1,0:T(8,128)(2,1)S(1)}, bf16[96,896]{1,0:T(8,128)(2,1)S(1)}, u32[]{:S(2)}, u32[]{:S(2)}) %collective-permute-start.2) | collective-permute-done | bytes 172064 | tf_op jit(solution)/shard_map/ppermute | solution.py:29
  137.9 3.0 %collective-permute-start.10 = (bf16[192,896]{1,0:T(8,128)(2,1)S(1)}, bf16[192,896]{1,0:T(8,128)(2,1)S(1)}, u32[]{:S(2)}, u32[]{:S(2)}) collective-permute-start(bf16[192,896]{1,0:T(8,128)(2,1)S(1)} %pad_maximum_fusion), channel_id=1, source_target_pairs={{0,128},{128,256},{256,384},{384,0},{1,129},{129,257},{257,385},{3... | collective-permute-start | bytes 1032200 | tf_op jit(solution)/shard_map/ppermute | solution.py:29
  141.0 5.0 %collective-permute-start.11 = (bf16[192,896]{1,0:T(8,128)(2,1)S(1)}, bf16[192,896]{1,0:T(8,128)(2,1)S(1)}, u32[]{:S(2)}, u32[]{:S(2)}) collective-permute-start(bf16[192,896]{1,0:T(8,128)(2,1)S(1)} %pad_maximum_fusion.1), channel_id=1, source_target_pairs={{0,384},{128,0},{256,128},{384,256},{1,385},{129,1},{257,129},{385... | collective-permute-start | bytes 1032200 | tf_op jit(solution)/shard_map/ppermute | solution.py:29
  146.0 1.2 reduce_sum.12
  147.2 1.9 %collective-permute-start.9 = (bf16[192,256]{1,0:T(8,128)(2,1)S(1)}, bf16[192,256]{1,0:T(8,128)(2,1)S(1)}, u32[]{:S(2)}, u32[]{:S(2)}) collective-permute-start(bf16[192,256]{1,0:T(8,128)(2,1)S(1)} %reduce_sum.12), channel_id=1, source_target_pairs={{0,0},{4,128},{8,256},{12,384},{128,4},{132,132},{136,260},{140,38... | collective-permute-start | bytes 294920 | tf_op jit(solution)/shard_map/ppermute | solution.py:33
  149.2 17.8 %collective-permute-done.9 = bf16[192,256]{1,0:T(8,128)(2,1)S(1)} collective-permute-done((bf16[192,256]{1,0:T(8,128)(2,1)S(1)}, bf16[192,256]{1,0:T(8,128)(2,1)S(1)}, u32[]{:S(2)}, u32[]{:S(2)}) %collective-permute-start.9) | collective-permute-done | bytes 98336 | tf_op jit(solution)/shard_map/ppermute | solution.py:33
  (50 shorter events, 5.7 us)
Async XLA Ops:
  7.2 24.2 %copy-start.2 = (bf16[128,128]{1,0:T(8,128)(2,1)S(1)}, bf16[128,128]{1,0:T(8,128)(2,1)}, u32[]{:S(2)}) copy-start(bf16[128,128]{1,0:T(8,128)(2,1)} %constant.25.clone.table_ref) | copy-start | bytes 98308
  7.2 14.6 %copy-start.8 = (s32[192]{0:T(256)S(1)}, s32[192]{0:T(256)}, u32[]{:S(2)}) copy-start(s32[192]{0:T(256)} %param.12) | copy-start | bytes 2308
  7.2 14.6 %copy-start.5 = (bf16[192,256]{1,0:T(8,128)(2,1)S(1)}, bf16[192,256]{1,0:T(8,128)(2,1)}, u32[]{:S(2)}) copy-start(bf16[192,256]{1,0:T(8,128)(2,1)} %param.9) | copy-start | bytes 294916
  7.2 92.7 %all-gather.7.cloned.1.call-start = ((), (), s32[]{:S(2)}) async-start(), calls=%async_computation.5 | async-start | bytes 2064384 | tf_op jit(solution)/shard_map/all_gather | solution.py:152
  9.4 0.9 copy-start
  10.4 1.0 copy-start.1
  12.4 19.0 %all-to-all-start = ((bf16[16,160,128]{2,1,0:T(8,128)(2,1)}), bf16[16,160,128]{2,1,0:T(8,128)(2,1)S(1)}, u32[]{:S(2)}, u32[]{:S(2)}) async-start(bf16[16,160,128]{2,1,0:T(8,128)(2,1)} %shard_map.86), calls=%async_computation | async-start | bytes 1310720 | tf_op jit(solution)/shard_map/all_to_all | solution.py:37
  21.7 96.6 %all-gather.5.cloned.1.call-start = ((), (), s32[]{:S(2)}) async-start(), calls=%async_computation.4 | async-start | bytes 2064384 | tf_op jit(solution)/shard_map/all_gather | solution.py:169
  48.4 10.8 %collective-permute-start = (bf16[192,256]{1,0:T(8,128)(2,1)S(1)}, bf16[192,256]{1,0:T(8,128)(2,1)S(1)}, u32[]{:S(2)}, u32[]{:S(2)}) collective-permute-start(bf16[192,256]{1,0:T(8,128)(2,1)S(1)} %clamp_convert_fusion), channel_id=1, source_target_pairs={{0,0},{4,128},{8,256},{12,384},{128,4},{132,132},{136,260},{140,38... | collective-permute-start | bytes 294920 | tf_op jit(solution)/shard_map/ppermute | solution.py:33
  59.2 25.7 %collective-permute-start.4 = (bf16[14,96,128]{2,1,0:T(8,128)(2,1)S(1)}, bf16[14,96,128]{2,1,0:T(8,128)(2,1)S(1)}, u32[]{:S(2)}, u32[]{:S(2)}) collective-permute-start(bf16[14,96,128]{2,1,0:T(8,128)(2,1)S(1)} %slice.40.own_ref), channel_id=1, source_target_pairs={{0,128},{128,256},{256,384},{384,0},{1,129},{129,257},{257,385},{3... | collective-permute-start | bytes 1032200 | tf_op jit(solution)/shard_map/ppermute | solution.py:29
  61.1 25.7 %collective-permute-start.5 = (bf16[14,96,128]{2,1,0:T(8,128)(2,1)S(1)}, bf16[14,96,128]{2,1,0:T(8,128)(2,1)S(1)}, u32[]{:S(2)}, u32[]{:S(2)}) collective-permute-start(bf16[14,96,128]{2,1,0:T(8,128)(2,1)S(1)} %slice.40.own_ref), channel_id=1, source_target_pairs={{0,384},{128,0},{256,128},{384,256},{1,385},{129,1},{257,129},{385... | collective-permute-start | bytes 1032200 | tf_op jit(solution)/shard_map/ppermute | solution.py:29
  71.8 34.5 %all-to-all-start.2 = ((bf16[8,192,256]{2,1,0:T(8,128)(2,1)}), bf16[8,192,256]{2,1,0:T(8,128)(2,1)S(1)}, u32[]{:S(2)}, u32[]{:S(2)}) async-start(bf16[8,192,256]{2,1,0:T(8,128)(2,1)} %broadcast_in_dim.8), calls=%async_computation.2 | async-start | bytes 1572864 | tf_op jit(solution)/shard_map/all_to_all | solution.py:37
  84.9 15.0 %collective-permute-start.6 = (bf16[7,96,128]{2,1,0:T(8,128)(2,1)S(1)}, bf16[7,96,128]{2,1,0:T(8,128)(2,1)S(1)}, u32[]{:S(2)}, u32[]{:S(2)}) collective-permute-start(bf16[7,96,128]{2,1,0:T(8,128)(2,1)S(1)} %slice.42), channel_id=1, source_target_pairs={{0,128},{128,256},{256,384},{384,0},{1,129},{129,257},{257,385},{3... | collective-permute-start | bytes 516104 | tf_op jit(solution)/shard_map/ppermute | solution.py:29
  86.9 13.0 %collective-permute-start.7 = (bf16[7,96,128]{2,1,0:T(8,128)(2,1)S(1)}, bf16[7,96,128]{2,1,0:T(8,128)(2,1)S(1)}, u32[]{:S(2)}, u32[]{:S(2)}) collective-permute-start(bf16[7,96,128]{2,1,0:T(8,128)(2,1)S(1)} %slice.43), channel_id=1, source_target_pairs={{0,384},{128,0},{256,128},{384,256},{1,385},{129,1},{257,129},{385... | collective-permute-start | bytes 516104 | tf_op jit(solution)/shard_map/ppermute | solution.py:29
  99.9 1.5 copy-start.4
  104.5 4.5 %collective-permute-start.8 = (bf16[8,192,256]{2,1,0:T(8,128)(2,1)}, bf16[8,192,256]{2,1,0:T(8,128)(2,1)}, u32[]{:S(2)}, u32[]{:S(2)}) collective-permute-start(bf16[8,192,256]{2,1,0:T(8,128)(2,1)} %get-tuple-element.21), channel_id=1, source_target_pairs={{0,1},{1,0},{2,3},{3,2},{4,5},{5,4},{6,7},{7,6},{8,9},{9,8},{10,11... | collective-permute-start | bytes 2359304 | tf_op jit(solution)/shard_map/ppermute | solution.py:41
  106.4 11.9 %collective-permute-start.1 = (bf16[8,192,256]{2,1,0:T(8,128)(2,1)S(1)}, bf16[8,192,256]{2,1,0:T(8,128)(2,1)S(1)}, u32[]{:S(2)}, u32[]{:S(2)}) collective-permute-start(bf16[8,192,256]{2,1,0:T(8,128)(2,1)S(1)} %all-to-all-done.2.grad_ref), channel_id=1, source_target_pairs={{0,1},{1,0},{2,3},{3,2},{4,5},{5,4},{6,7},{7,6},{8,9},{9,8},{10,11... | collective-permute-start | bytes 2359304 | tf_op jit(solution)/shard_map/ppermute | solution.py:41
  111.2 19.4 %all-to-all-start.3 = ((bf16[8,192,256]{2,1,0:T(8,128)(2,1)}), bf16[8,192,256]{2,1,0:T(8,128)(2,1)}, u32[]{:S(2)}, u32[]{:S(2)}) async-start(bf16[8,192,256]{2,1,0:T(8,128)(2,1)} %add_convert_fusion), calls=%async_computation.3 | async-start | bytes 1572864 | tf_op jit(solution)/shard_map/all_to_all | solution.py:37
  118.3 1.5 copy-start.3
  119.8 10.7 %copy-start.6 = (s32[896]{0:T(1024)S(1)}, s32[896]{0:T(1024)}, u32[]{:S(2)}) copy-start(s32[896]{0:T(1024)} %param.10) | copy-start | bytes 10756
  122.5 15.3 %collective-permute-start.2 = (bf16[96,896]{1,0:T(8,128)(2,1)S(1)}, bf16[96,896]{1,0:T(8,128)(2,1)S(1)}, u32[]{:S(2)}, u32[]{:S(2)}) collective-permute-start(bf16[96,896]{1,0:T(8,128)(2,1)S(1)} %get-tuple-element.29), channel_id=1, source_target_pairs={{0,128},{128,256},{256,384},{384,0},{1,129},{129,257},{257,385},{3... | collective-permute-start | bytes 516104 | tf_op jit(solution)/shard_map/ppermute | solution.py:29
  127.4 10.5 %collective-permute-start.3 = (bf16[96,896]{1,0:T(8,128)(2,1)S(1)}, bf16[96,896]{1,0:T(8,128)(2,1)S(1)}, u32[]{:S(2)}, u32[]{:S(2)}) collective-permute-start(bf16[96,896]{1,0:T(8,128)(2,1)S(1)} %get-tuple-element.28), channel_id=1, source_target_pairs={{0,384},{128,0},{256,128},{384,256},{1,385},{129,1},{257,129},{385... | collective-permute-start | bytes 516104 | tf_op jit(solution)/shard_map/ppermute | solution.py:29
  130.6 18.6 %copy-start.7 = (s32[192]{0:T(256)S(1)}, s32[192]{0:T(256)}, u32[]{:S(2)}) copy-start(s32[192]{0:T(256)} %param.11) | copy-start | bytes 2308
  137.9 29.8 %collective-permute-start.10 = (bf16[192,896]{1,0:T(8,128)(2,1)S(1)}, bf16[192,896]{1,0:T(8,128)(2,1)S(1)}, u32[]{:S(2)}, u32[]{:S(2)}) collective-permute-start(bf16[192,896]{1,0:T(8,128)(2,1)S(1)} %pad_maximum_fusion), channel_id=1, source_target_pairs={{0,128},{128,256},{256,384},{384,0},{1,129},{129,257},{257,385},{3... | collective-permute-start | bytes 1032200 | tf_op jit(solution)/shard_map/ppermute | solution.py:29
  141.0 26.8 %collective-permute-start.11 = (bf16[192,896]{1,0:T(8,128)(2,1)S(1)}, bf16[192,896]{1,0:T(8,128)(2,1)S(1)}, u32[]{:S(2)}, u32[]{:S(2)}) collective-permute-start(bf16[192,896]{1,0:T(8,128)(2,1)S(1)} %pad_maximum_fusion.1), channel_id=1, source_target_pairs={{0,384},{128,0},{256,128},{384,256},{1,385},{129,1},{257,129},{385... | collective-permute-start | bytes 1032200 | tf_op jit(solution)/shard_map/ppermute | solution.py:29
  147.2 19.8 %collective-permute-start.9 = (bf16[192,256]{1,0:T(8,128)(2,1)S(1)}, bf16[192,256]{1,0:T(8,128)(2,1)S(1)}, u32[]{:S(2)}, u32[]{:S(2)}) collective-permute-start(bf16[192,256]{1,0:T(8,128)(2,1)S(1)} %reduce_sum.12), channel_id=1, source_target_pairs={{0,0},{4,128},{8,256},{12,384},{128,4},{132,132},{136,260},{140,38... | collective-permute-start | bytes 294920 | tf_op jit(solution)/shard_map/ppermute | solution.py:33
Sparse Core Ops, SparseCore 0:
  10.1 47.6 all-gather.6
  60.5 41.9 all-gather.4

commit v5 on v3

--- a/solution.py
+++ b/solution.py
@@ -195,13 +195,15 @@
         [pltpu.VMEM((4 * cols, width), BF)],
     )
     one, two = shifted(far[:half], "zh", 1), shifted(far[half:], "zh", -1)
+    summed = jnp.sum(sums.astype(F32), 0).astype(BF)
+    one, two, summed = lax.optimization_barrier((one, two, summed))
+    summed = turned(summed)
     upper = jnp.concatenate([(upper[:half].astype(F32) + one.astype(F32)).astype(BF), upper[half:]])
     lower = jnp.concatenate([lower[:half], (lower[half:].astype(F32) + two.astype(F32)).astype(BF)])
     one, two = shifted(upper, "zh", 1), shifted(lower, "zh", -1)
     flips = (1 - 2 * sign_bits).astype(F32)
     grad_hidden = (kept + one.astype(F32) + two.astype(F32)) * grad_factor * flips[None, :]
 
-    summed = turned(jnp.sum(sums.astype(F32), 0).astype(BF))
     mixed = summed.astype(F32) * jnp.exp2(act_exponent.astype(F32))[:, None]
     return mixed.astype(BF), grad_hidden.astype(BF)
 

time: 179 us -> 176 us (0.983)
  the two profiles are of different devices: /device:TPU:47 before, /device:TPU:123 now
where the time goes in v5:
time: 176 us; the launch traced here: 175 us
  starting transfers between devices  62.4 us (35%)
  waiting for transfers between devices  62 us (35%)
  blocking collectives  15.7 us (9%)
  between operations  14.4 us (8%)
  local copies, waits for them, and re-layouts  8.18 us (5%)
  Pallas kernels  7.29 us (4%)
  other arithmetic  5.4 us (3%)
    ppermute x8, starting transfers between devices, shifted(): lax.ppermute(value, axis, [(i, (i + step) % size) for i in range(size)])  31.5 us
    ppermute x8, waiting for transfers between devices, shifted(): lax.ppermute(value, axis, [(i, (i + step) % size) for i in range(size)])  29.8 us
    ppermute x2, waiting for transfers between devices, turned(): lax.ppermute(value, ('zh', 'x'), [(a * 4 + b, b * 4 + a) for a in range(4...  21.9 us
    all_to_all x3, starting transfers between devices, exchange(): return lax.all_to_all(value, axes, 0, 0)  17.9 us
    all_to_all x1, blocking collectives, exchange(): return lax.all_to_all(value, axes, 0, 0)  15.7 us
    all_to_all x3, waiting for transfers between devices, exchange(): return lax.all_to_all(value, axes, 0, 0)  9.31 us
    ppermute x2, starting transfers between devices, turned(): lax.ppermute(value, ('zh', 'x'), [(a * 4 + b, b * 4 + a) for a in range(4...  8.52 us
    pallas_call x4, Pallas kernels, call(): pl.pallas_call(kernel, out_shape=out, in_specs=[smem if a.ndim == 1 else...  7.29 us
  transfers between devices with their start and end apart: 17, of which 9 were waited for; matrix products, arithmetic and copies ran while one was open for 4% of the time, Pallas kernels for 4%

profile of v5, /device:TPU:123, one launch (start us, length us, event | category | flops | bytes accessed | tf_op | source)
XLA Modules:
  0.0 175.3 jit_solution(8723662313552332138)
XLA Ops:
  10.4 1.0 copy-done.1
  11.3 1.1 shard_map.86
  12.4 6.1 %all-to-all-start = ((bf16[16,160,128]{2,1,0:T(8,128)(2,1)}), bf16[16,160,128]{2,1,0:T(8,128)(2,1)S(1)}, u32[]{:S(2)}, u32[]{:S(2)}) async-start(bf16[16,160,128]{2,1,0:T(8,128)(2,1)} %shard_map.86), calls=%async_computation | async-start | bytes 1310720 | tf_op jit(solution)/shard_map/all_to_all | solution.py:37
  18.7 9.3 %all-to-all-done.x_ref = bf16[16,160,128]{2,1,0:T(8,128)(2,1)S(1)} async-done(((bf16[16,160,128]{2,1,0:T(8,128)(2,1)}), bf16[16,160,128]{2,1,0:T(8,128)(2,1)S(1)}, u32[]{:S(2)}, u32[]{:S(2)}) %all-to-all-start) | async-done | bytes 655392 | tf_op jit(solution)/shard_map/all_to_all | solution.py:37
  28.4 15.7 %all_to_all.20 = bf16[16,160,128]{2,1,0:T(8,128)(2,1)S(1)} all-to-all(bf16[16,160,128]{2,1,0:T(8,128)(2,1)S(1)} %shard_map.87), channel_id=1, replica_groups=mesh['zh'=4,'y'=8,'x'=4,'zl'=2,'core'=2] {'x','zl','core'}, dimensions={0} | all-to-all | bytes 1310720 | tf_op jit(solution)/shard_map/all_to_all | solution.py:37
  44.9 6.6 %collective-permute-start = (bf16[192,256]{1,0:T(8,128)(2,1)S(1)}, bf16[192,256]{1,0:T(8,128)(2,1)S(1)}, u32[]{:S(2)}, u32[]{:S(2)}) collective-permute-start(bf16[192,256]{1,0:T(8,128)(2,1)S(1)} %clamp_convert_fusion), channel_id=1, source_target_pairs={{0,0},{4,128},{8,256},{12,384},{128,4},{132,132},{136,260},{140,38... | collective-permute-start | bytes 294920 | tf_op jit(solution)/shard_map/ppermute | solution.py:33
  51.5 4.1 %collective-permute-done = bf16[192,256]{1,0:T(8,128)(2,1)S(1)} collective-permute-done((bf16[192,256]{1,0:T(8,128)(2,1)S(1)}, bf16[192,256]{1,0:T(8,128)(2,1)S(1)}, u32[]{:S(2)}, u32[]{:S(2)}) %collective-permute-start) | collective-permute-done | bytes 98336 | tf_op jit(solution)/shard_map/ppermute | solution.py:33
  55.6 1.9 %collective-permute-start.4 = (bf16[14,96,128]{2,1,0:T(8,128)(2,1)S(1)}, bf16[14,96,128]{2,1,0:T(8,128)(2,1)S(1)}, u32[]{:S(2)}, u32[]{:S(2)}) collective-permute-start(bf16[14,96,128]{2,1,0:T(8,128)(2,1)S(1)} %slice.40.own_ref), channel_id=1, source_target_pairs={{0,128},{128,256},{256,384},{384,0},{1,129},{129,257},{257,385},{3... | collective-permute-start | bytes 1032200 | tf_op jit(solution)/shard_map/ppermute | solution.py:29
  57.5 11.0 %collective-permute-start.5 = (bf16[14,96,128]{2,1,0:T(8,128)(2,1)S(1)}, bf16[14,96,128]{2,1,0:T(8,128)(2,1)S(1)}, u32[]{:S(2)}, u32[]{:S(2)}) collective-permute-start(bf16[14,96,128]{2,1,0:T(8,128)(2,1)S(1)} %slice.40.own_ref), channel_id=1, source_target_pairs={{0,384},{128,0},{256,128},{384,256},{1,385},{129,1},{257,129},{385... | collective-permute-start | bytes 1032200 | tf_op jit(solution)/shard_map/ppermute | solution.py:29
  68.5 0.9 broadcast_in_dim.8
  69.4 7.7 %all-to-all-start.2 = ((bf16[8,192,256]{2,1,0:T(8,128)(2,1)}), bf16[8,192,256]{2,1,0:T(8,128)(2,1)S(1)}, u32[]{:S(2)}, u32[]{:S(2)}) async-start(bf16[8,192,256]{2,1,0:T(8,128)(2,1)} %broadcast_in_dim.8), calls=%async_computation.2 | async-start | bytes 1572864 | tf_op jit(solution)/shard_map/all_to_all | solution.py:37
  77.6 1.9 %collective-permute-start.6 = (bf16[7,96,128]{2,1,0:T(8,128)(2,1)S(1)}, bf16[7,96,128]{2,1,0:T(8,128)(2,1)S(1)}, u32[]{:S(2)}, u32[]{:S(2)}) collective-permute-start(bf16[7,96,128]{2,1,0:T(8,128)(2,1)S(1)} %slice.42), channel_id=1, source_target_pairs={{0,128},{128,256},{256,384},{384,0},{1,129},{129,257},{257,385},{3... | collective-permute-start | bytes 516104 | tf_op jit(solution)/shard_map/ppermute | solution.py:29
  79.5 6.7 %collective-permute-done.5.next_ref = bf16[14,96,128]{2,1,0:T(8,128)(2,1)S(1)} collective-permute-done((bf16[14,96,128]{2,1,0:T(8,128)(2,1)S(1)}, bf16[14,96,128]{2,1,0:T(8,128)(2,1)S(1)}, u32[]{:S(2)}, u32[]{:S(2)}) %collective-permute-start.5) | collective-permute-done | bytes 344096 | tf_op jit(solution)/shard_map/ppermute | solution.py:29
  86.2 1.9 %collective-permute-start.7 = (bf16[7,96,128]{2,1,0:T(8,128)(2,1)S(1)}, bf16[7,96,128]{2,1,0:T(8,128)(2,1)S(1)}, u32[]{:S(2)}, u32[]{:S(2)}) collective-permute-start(bf16[7,96,128]{2,1,0:T(8,128)(2,1)S(1)} %slice.43), channel_id=1, source_target_pairs={{0,384},{128,0},{256,128},{384,256},{1,385},{129,1},{257,129},{385... | collective-permute-start | bytes 516104 | tf_op jit(solution)/shard_map/ppermute | solution.py:29
  88.2 13.9 %collective-permute-done.7.second_ref = bf16[7,96,128]{2,1,0:T(8,128)(2,1)S(1)} collective-permute-done((bf16[7,96,128]{2,1,0:T(8,128)(2,1)S(1)}, bf16[7,96,128]{2,1,0:T(8,128)(2,1)S(1)}, u32[]{:S(2)}, u32[]{:S(2)}) %collective-permute-start.7) | collective-permute-done | bytes 172064 | tf_op jit(solution)/shard_map/ppermute | solution.py:29
  102.1 1.5 copy-done.4
  103.6 3.1 %shard_map.89 = (bf16[8,192,256]{2,1,0:T(8,128)(2,1)S(1)}, bf16[8,192,256]{2,1,0:T(8,128)(2,1)}) custom-call(s32[2]{0:T(128)S(1)} %pad_add_fusion.place_ref, bf16[8,896,128]{2,1,0:T(8,128)(2,1)S(1)} %bitcast.6, bf16[14,96,128]{2,1,0:T(8,128)(2,1)S(1)} %slice.40.own_ref, bf16[14,96,128]{2,1,0:T(8,128)(2,1)S(1)} %collective-permute-done.4.prev_ref, ...), custom_call_target="tpu_custom_call" | custom-call | flops 1409286144 | bytes 2000000 | tf_op jit(solution)/shard_map/pallas_call | solution.py:59
  106.7 2.5 %collective-permute-start.8 = (bf16[8,192,256]{2,1,0:T(8,128)(2,1)}, bf16[8,192,256]{2,1,0:T(8,128)(2,1)}, u32[]{:S(2)}, u32[]{:S(2)}) collective-permute-start(bf16[8,192,256]{2,1,0:T(8,128)(2,1)} %get-tuple-element.21), channel_id=1, source_target_pairs={{0,1},{1,0},{2,3},{3,2},{4,5},{5,4},{6,7},{7,6},{8,9},{9,8},{10,11... | collective-permute-start | bytes 2359304 | tf_op jit(solution)/shard_map/ppermute | solution.py:41
  109.2 1.9 %collective-permute-start.1 = (bf16[8,192,256]{2,1,0:T(8,128)(2,1)S(1)}, bf16[8,192,256]{2,1,0:T(8,128)(2,1)S(1)}, u32[]{:S(2)}, u32[]{:S(2)}) collective-permute-start(bf16[8,192,256]{2,1,0:T(8,128)(2,1)S(1)} %all-to-all-done.2.grad_ref), channel_id=1, source_target_pairs={{0,1},{1,0},{2,3},{3,2},{4,5},{5,4},{6,7},{7,6},{8,9},{9,8},{10,11... | collective-permute-start | bytes 2359304 | tf_op jit(solution)/shard_map/ppermute | solution.py:41
  111.4 2.2 %add_convert_fusion = bf16[8,192,256]{2,1,0:T(8,128)(2,1)} fusion(bf16[8,192,256]{2,1,0:T(8,128)(2,1)} %collective-permute-done.8, bf16[8,192,256]{2,1,0:T(8,128)(2,1)S(1)} %get-tuple-element.20), kind=kLoop, calls=%fused_computation | loop fusion | flops 1572864 | bytes 2359296 | tf_op jit(solution)/shard_map/convert_element_type | solution.py:187
  113.6 4.2 %all-to-all-start.3 = ((bf16[8,192,256]{2,1,0:T(8,128)(2,1)}), bf16[8,192,256]{2,1,0:T(8,128)(2,1)}, u32[]{:S(2)}, u32[]{:S(2)}) async-start(bf16[8,192,256]{2,1,0:T(8,128)(2,1)} %add_convert_fusion), calls=%async_computation.3 | async-start | bytes 1572864 | tf_op jit(solution)/shard_map/all_to_all | solution.py:37
  117.8 1.5 copy-done.3
  119.3 2.7 %shard_map.88 = (bf16[192,896]{1,0:T(8,128)(2,1)S(1)}, bf16[192,896]{1,0:T(8,128)(2,1)S(1)}, bf16[192,896]{1,0:T(8,128)(2,1)S(1)}, f32[192,896]{1,0:T(8,128)S(1)}) custom-call(s32[2]{0:T(128)S(1)} %pad_add_fusion.place_ref, bf16[8,192,256]{2,1,0:T(8,128)(2,1)S(1)} %all-to-all-done.2.grad_ref, bf16[8,192,256]{2,1,0:T(8,128)(2,1)S(1)} %collective-permute-done.1.cross_ref, ...), custom_call_target="tpu_custom_call" | custom-call | flops 1409286144 | bytes 2000000 | tf_op jit(solution)/shard_map/pallas_call | solution.py:59
  122.0 5.2 %collective-permute-start.2 = (bf16[96,896]{1,0:T(8,128)(2,1)S(1)}, bf16[96,896]{1,0:T(8,128)(2,1)S(1)}, u32[]{:S(2)}, u32[]{:S(2)}) collective-permute-start(bf16[96,896]{1,0:T(8,128)(2,1)S(1)} %get-tuple-element.29), channel_id=1, source_target_pairs={{0,128},{128,256},{256,384},{384,0},{1,129},{129,257},{257,385},{3... | collective-permute-start | bytes 516104 | tf_op jit(solution)/shard_map/ppermute | solution.py:29
  127.2 2.2 %collective-permute-start.3 = (bf16[96,896]{1,0:T(8,128)(2,1)S(1)}, bf16[96,896]{1,0:T(8,128)(2,1)S(1)}, u32[]{:S(2)}, u32[]{:S(2)}) collective-permute-start(bf16[96,896]{1,0:T(8,128)(2,1)S(1)} %get-tuple-element.28), channel_id=1, source_target_pairs={{0,384},{128,0},{256,128},{384,256},{1,385},{129,1},{257,129},{385... | collective-permute-start | bytes 516104 | tf_op jit(solution)/shard_map/ppermute | solution.py:29
  129.5 1.2 reduce_sum.12
  130.8 3.1 %collective-permute-done.2 = bf16[96,896]{1,0:T(8,128)(2,1)S(1)} collective-permute-done((bf16[96,896]{1,0:T(8,128)(2,1)S(1)}, bf16[96,896]{1,0:T(8,128)(2,1)S(1)}, u32[]{:S(2)}, u32[]{:S(2)}) %collective-permute-start.2) | collective-permute-done | bytes 172064 | tf_op jit(solution)/shard_map/ppermute | solution.py:29
  133.9 5.6 %collective-permute-done.3 = bf16[96,896]{1,0:T(8,128)(2,1)S(1)} collective-permute-done((bf16[96,896]{1,0:T(8,128)(2,1)S(1)}, bf16[96,896]{1,0:T(8,128)(2,1)S(1)}, u32[]{:S(2)}, u32[]{:S(2)}) %collective-permute-start.3) | collective-permute-done | bytes 172064 | tf_op jit(solution)/shard_map/ppermute | solution.py:29
  139.6 1.9 %collective-permute-start.10 = (bf16[192,896]{1,0:T(8,128)(2,1)S(1)}, bf16[192,896]{1,0:T(8,128)(2,1)S(1)}, u32[]{:S(2)}, u32[]{:S(2)}) collective-permute-start(bf16[192,896]{1,0:T(8,128)(2,1)S(1)} %pad_maximum_fusion), channel_id=1, source_target_pairs={{0,128},{128,256},{256,384},{384,0},{1,129},{129,257},{257,385},{3... | collective-permute-start | bytes 1032200 | tf_op jit(solution)/shard_map/ppermute | solution.py:29
  141.6 5.5 %collective-permute-start.11 = (bf16[192,896]{1,0:T(8,128)(2,1)S(1)}, bf16[192,896]{1,0:T(8,128)(2,1)S(1)}, u32[]{:S(2)}, u32[]{:S(2)}) collective-permute-start(bf16[192,896]{1,0:T(8,128)(2,1)S(1)} %pad_maximum_fusion.1), channel_id=1, source_target_pairs={{0,384},{128,0},{256,128},{384,256},{1,385},{129,1},{257,129},{385... | collective-permute-start | bytes 1032200 | tf_op jit(solution)/shard_map/ppermute | solution.py:29
  147.1 1.9 %collective-permute-start.9 = (bf16[192,256]{1,0:T(8,128)(2,1)S(1)}, bf16[192,256]{1,0:T(8,128)(2,1)S(1)}, u32[]{:S(2)}, u32[]{:S(2)}) collective-permute-start(bf16[192,256]{1,0:T(8,128)(2,1)S(1)} %reduce_sum.12), channel_id=1, source_target_pairs={{0,0},{4,128},{8,256},{12,384},{128,4},{132,132},{136,260},{140,38... | collective-permute-start | bytes 294920 | tf_op jit(solution)/shard_map/ppermute | solution.py:33
  149.0 17.8 %collective-permute-done.9 = bf16[192,256]{1,0:T(8,128)(2,1)S(1)} collective-permute-done((bf16[192,256]{1,0:T(8,128)(2,1)S(1)}, bf16[192,256]{1,0:T(8,128)(2,1)S(1)}, u32[]{:S(2)}, u32[]{:S(2)}) %collective-permute-start.9) | collective-permute-done | bytes 98336 | tf_op jit(solution)/shard_map/ppermute | solution.py:33
  (50 shorter events, 7.3 us)
Async XLA Ops:
  7.2 20.8 %copy-start.2 = (bf16[128,128]{1,0:T(8,128)(2,1)S(1)}, bf16[128,128]{1,0:T(8,128)(2,1)}, u32[]{:S(2)}) copy-start(bf16[128,128]{1,0:T(8,128)(2,1)} %constant.25.clone.table_ref) | copy-start | bytes 98308
  7.2 11.3 %copy-start.8 = (s32[192]{0:T(256)S(1)}, s32[192]{0:T(256)}, u32[]{:S(2)}) copy-start(s32[192]{0:T(256)} %param.12) | copy-start | bytes 2308
  7.2 11.3 %copy-start.5 = (bf16[192,256]{1,0:T(8,128)(2,1)S(1)}, bf16[192,256]{1,0:T(8,128)(2,1)}, u32[]{:S(2)}) copy-start(bf16[192,256]{1,0:T(8,128)(2,1)} %param.9) | copy-start | bytes 294916
  7.2 94.9 %all-gather.7.cloned.1.call-start = ((), (), s32[]{:S(2)}) async-start(), calls=%async_computation.5 | async-start | bytes 2064384 | tf_op jit(solution)/shard_map/all_gather | solution.py:152
  9.4 0.9 copy-start
  10.4 1.0 copy-start.1
  12.4 15.6 %all-to-all-start = ((bf16[16,160,128]{2,1,0:T(8,128)(2,1)}), bf16[16,160,128]{2,1,0:T(8,128)(2,1)S(1)}, u32[]{:S(2)}, u32[]{:S(2)}) async-start(bf16[16,160,128]{2,1,0:T(8,128)(2,1)} %shard_map.86), calls=%async_computation | async-start | bytes 1310720 | tf_op jit(solution)/shard_map/all_to_all | solution.py:37
  18.5 99.3 %all-gather.5.cloned.1.call-start = ((), (), s32[]{:S(2)}) async-start(), calls=%async_computation.4 | async-start | bytes 2064384 | tf_op jit(solution)/shard_map/all_gather | solution.py:169
  44.9 10.7 %collective-permute-start = (bf16[192,256]{1,0:T(8,128)(2,1)S(1)}, bf16[192,256]{1,0:T(8,128)(2,1)S(1)}, u32[]{:S(2)}, u32[]{:S(2)}) collective-permute-start(bf16[192,256]{1,0:T(8,128)(2,1)S(1)} %clamp_convert_fusion), channel_id=1, source_target_pairs={{0,0},{4,128},{8,256},{12,384},{128,4},{132,132},{136,260},{140,38... | collective-permute-start | bytes 294920 | tf_op jit(solution)/shard_map/ppermute | solution.py:33
  55.6 22.0 %collective-permute-start.4 = (bf16[14,96,128]{2,1,0:T(8,128)(2,1)S(1)}, bf16[14,96,128]{2,1,0:T(8,128)(2,1)S(1)}, u32[]{:S(2)}, u32[]{:S(2)}) collective-permute-start(bf16[14,96,128]{2,1,0:T(8,128)(2,1)S(1)} %slice.40.own_ref), channel_id=1, source_target_pairs={{0,128},{128,256},{256,384},{384,0},{1,129},{129,257},{257,385},{3... | collective-permute-start | bytes 1032200 | tf_op jit(solution)/shard_map/ppermute | solution.py:29
  57.5 28.7 %collective-permute-start.5 = (bf16[14,96,128]{2,1,0:T(8,128)(2,1)S(1)}, bf16[14,96,128]{2,1,0:T(8,128)(2,1)S(1)}, u32[]{:S(2)}, u32[]{:S(2)}) collective-permute-start(bf16[14,96,128]{2,1,0:T(8,128)(2,1)S(1)} %slice.40.own_ref), channel_id=1, source_target_pairs={{0,384},{128,0},{256,128},{384,256},{1,385},{129,1},{257,129},{385... | collective-permute-start | bytes 1032200 | tf_op jit(solution)/shard_map/ppermute | solution.py:29
  69.4 39.8 %all-to-all-start.2 = ((bf16[8,192,256]{2,1,0:T(8,128)(2,1)}), bf16[8,192,256]{2,1,0:T(8,128)(2,1)S(1)}, u32[]{:S(2)}, u32[]{:S(2)}) async-start(bf16[8,192,256]{2,1,0:T(8,128)(2,1)} %broadcast_in_dim.8), calls=%async_computation.2 | async-start | bytes 1572864 | tf_op jit(solution)/shard_map/all_to_all | solution.py:37
  77.6 10.7 %collective-permute-start.6 = (bf16[7,96,128]{2,1,0:T(8,128)(2,1)S(1)}, bf16[7,96,128]{2,1,0:T(8,128)(2,1)S(1)}, u32[]{:S(2)}, u32[]{:S(2)}) collective-permute-start(bf16[7,96,128]{2,1,0:T(8,128)(2,1)S(1)} %slice.42), channel_id=1, source_target_pairs={{0,128},{128,256},{256,384},{384,0},{1,129},{129,257},{257,385},{3... | collective-permute-start | bytes 516104 | tf_op jit(solution)/shard_map/ppermute | solution.py:29
  86.2 15.9 %collective-permute-start.7 = (bf16[7,96,128]{2,1,0:T(8,128)(2,1)S(1)}, bf16[7,96,128]{2,1,0:T(8,128)(2,1)S(1)}, u32[]{:S(2)}, u32[]{:S(2)}) collective-permute-start(bf16[7,96,128]{2,1,0:T(8,128)(2,1)S(1)} %slice.43), channel_id=1, source_target_pairs={{0,384},{128,0},{256,128},{384,256},{1,385},{129,1},{257,129},{385... | collective-permute-start | bytes 516104 | tf_op jit(solution)/shard_map/ppermute | solution.py:29
  102.1 1.5 copy-start.4
  106.7 4.7 %collective-permute-start.8 = (bf16[8,192,256]{2,1,0:T(8,128)(2,1)}, bf16[8,192,256]{2,1,0:T(8,128)(2,1)}, u32[]{:S(2)}, u32[]{:S(2)}) collective-permute-start(bf16[8,192,256]{2,1,0:T(8,128)(2,1)} %get-tuple-element.21), channel_id=1, source_target_pairs={{0,1},{1,0},{2,3},{3,2},{4,5},{5,4},{6,7},{7,6},{8,9},{9,8},{10,11... | collective-permute-start | bytes 2359304 | tf_op jit(solution)/shard_map/ppermute | solution.py:41
  109.2 8.6 %collective-permute-start.1 = (bf16[8,192,256]{2,1,0:T(8,128)(2,1)S(1)}, bf16[8,192,256]{2,1,0:T(8,128)(2,1)S(1)}, u32[]{:S(2)}, u32[]{:S(2)}) collective-permute-start(bf16[8,192,256]{2,1,0:T(8,128)(2,1)S(1)} %all-to-all-done.2.grad_ref), channel_id=1, source_target_pairs={{0,1},{1,0},{2,3},{3,2},{4,5},{5,4},{6,7},{7,6},{8,9},{9,8},{10,11... | collective-permute-start | bytes 2359304 | tf_op jit(solution)/shard_map/ppermute | solution.py:41
  113.6 15.8 %all-to-all-start.3 = ((bf16[8,192,256]{2,1,0:T(8,128)(2,1)}), bf16[8,192,256]{2,1,0:T(8,128)(2,1)}, u32[]{:S(2)}, u32[]{:S(2)}) async-start(bf16[8,192,256]{2,1,0:T(8,128)(2,1)} %add_convert_fusion), calls=%async_computation.3 | async-start | bytes 1572864 | tf_op jit(solution)/shard_map/all_to_all | solution.py:37
  117.8 1.5 copy-start.3
  119.3 10.1 %copy-start.6 = (s32[896]{0:T(1024)S(1)}, s32[896]{0:T(1024)}, u32[]{:S(2)}) copy-start(s32[896]{0:T(1024)} %param.10) | copy-start | bytes 10756
  122.0 11.8 %collective-permute-start.2 = (bf16[96,896]{1,0:T(8,128)(2,1)S(1)}, bf16[96,896]{1,0:T(8,128)(2,1)S(1)}, u32[]{:S(2)}, u32[]{:S(2)}) collective-permute-start(bf16[96,896]{1,0:T(8,128)(2,1)S(1)} %get-tuple-element.29), channel_id=1, source_target_pairs={{0,128},{128,256},{256,384},{384,0},{1,129},{129,257},{257,385},{3... | collective-permute-start | bytes 516104 | tf_op jit(solution)/shard_map/ppermute | solution.py:29
  127.2 12.3 %collective-permute-start.3 = (bf16[96,896]{1,0:T(8,128)(2,1)S(1)}, bf16[96,896]{1,0:T(8,128)(2,1)S(1)}, u32[]{:S(2)}, u32[]{:S(2)}) collective-permute-start(bf16[96,896]{1,0:T(8,128)(2,1)S(1)} %get-tuple-element.28), channel_id=1, source_target_pairs={{0,384},{128,0},{256,128},{384,256},{1,385},{129,1},{257,129},{385... | collective-permute-start | bytes 516104 | tf_op jit(solution)/shard_map/ppermute | solution.py:29
  130.7 18.3 %copy-start.7 = (s32[192]{0:T(256)S(1)}, s32[192]{0:T(256)}, u32[]{:S(2)}) copy-start(s32[192]{0:T(256)} %param.11) | copy-start | bytes 2308
  139.6 28.0 %collective-permute-start.10 = (bf16[192,896]{1,0:T(8,128)(2,1)S(1)}, bf16[192,896]{1,0:T(8,128)(2,1)S(1)}, u32[]{:S(2)}, u32[]{:S(2)}) collective-permute-start(bf16[192,896]{1,0:T(8,128)(2,1)S(1)} %pad_maximum_fusion), channel_id=1, source_target_pairs={{0,128},{128,256},{256,384},{384,0},{1,129},{129,257},{257,385},{3... | collective-permute-start | bytes 1032200 | tf_op jit(solution)/shard_map/ppermute | solution.py:29
  141.6 26.0 %collective-permute-start.11 = (bf16[192,896]{1,0:T(8,128)(2,1)S(1)}, bf16[192,896]{1,0:T(8,128)(2,1)S(1)}, u32[]{:S(2)}, u32[]{:S(2)}) collective-permute-start(bf16[192,896]{1,0:T(8,128)(2,1)S(1)} %pad_maximum_fusion.1), channel_id=1, source_target_pairs={{0,384},{128,0},{256,128},{384,256},{1,385},{129,1},{257,129},{385... | collective-permute-start | bytes 1032200 | tf_op jit(solution)/shard_map/ppermute | solution.py:29
  147.1 19.8 %collective-permute-start.9 = (bf16[192,256]{1,0:T(8,128)(2,1)S(1)}, bf16[192,256]{1,0:T(8,128)(2,1)S(1)}, u32[]{:S(2)}, u32[]{:S(2)}) collective-permute-start(bf16[192,256]{1,0:T(8,128)(2,1)S(1)} %reduce_sum.12), channel_id=1, source_target_pairs={{0,0},{4,128},{8,256},{12,384},{128,4},{132,132},{136,260},{140,38... | collective-permute-start | bytes 294920 | tf_op jit(solution)/shard_map/ppermute | solution.py:33
Sparse Core Ops, SparseCore 0:
  10.1 41.4 all-gather.6
  54.3 41.8 all-gather.4

commit v6 on v4

--- a/solution.py
+++ b/solution.py
@@ -59,7 +59,7 @@
     return pl.pallas_call(
         kernel,
         out_shape=out,
-        in_specs=[smem if a.ndim == 1 else vmem for a in arguments],
+        in_specs=[smem if a.shape == (2,) else vmem for a in arguments],
         out_specs=jax.tree.map(lambda _: vmem, out),
         scratch_shapes=list(scratch),
         compiler_params=pltpu.CompilerParams(vmem_limit_bytes=limit * 2**20),
@@ -69,8 +69,10 @@
 
 def spread_kernel(hidden_ref, weight_ref, sign_ref, exponent_ref, out_ref):
     rows, width = hidden_ref.shape
-    flips = (1 - 2 * sign_ref[...]).astype(F32)
-    scale = two_to(-exponent_ref[...])
+    flips = (1 - 2 * sign_ref[...]).astype(F32).reshape(1, width)
+    line = two_to(-exponent_ref[...]).reshape(1, rows)
+    place = [lax.broadcasted_iota(jnp.int32, (rows, rows), d) for d in range(2)]
+    scale = jnp.sum(jnp.where(place[0] == place[1], line, 0.0), 1, keepdims=True)
     for g, at, units in groups_of(width, rows):
         signed = hidden_ref[at, units].astype(F32) * flips[:, units] * scale[at, :]
         out_ref[g, : rows // 2, :] = signed.astype(BF)
@@ -154,7 +156,7 @@
     grad_local = jnp.clip(out_gradient.astype(F32) / grad_factor, -127.0, 127.0).astype(BF)
 
     spread = jax.ShapeDtypeStruct((parts, lines, BLK), BF)
-    signed = call(spread_kernel, spread, (hidden, down_rotated, sign_bits[None, :], act_exponent[:, None]), 1_000_000)
+    signed = call(spread_kernel, spread, (hidden, down_rotated, sign_bits, act_exponent), 1_000_000)
     arrived = exchange(signed)
     arrived, grad_local = lax.optimization_barrier((arrived, grad_local))
     turned_grad = turned(grad_local)

time: 176 us -> 176 us (level)
  the two profiles are of different devices: /device:TPU:2 before, /device:TPU:123 now
where the time goes in v6:
time: 176 us; the launch traced here: 175 us
  starting transfers between devices  62.8 us (36%)
  waiting for transfers between devices  61.7 us (35%)
  blocking collectives  15.7 us (9%)
  between operations  14.4 us (8%)
  local copies, waits for them, and re-layouts  8.04 us (5%)
  Pallas kernels  7.27 us (4%)
  other arithmetic  5.43 us (3%)
    ppermute x8, starting transfers between devices, shifted(): lax.ppermute(value, axis, [(i, (i + step) % size) for i in range(size)])  31.8 us
    ppermute x8, waiting for transfers between devices, shifted(): lax.ppermute(value, axis, [(i, (i + step) % size) for i in range(size)])  30.7 us
    ppermute x2, waiting for transfers between devices, turned(): lax.ppermute(value, ('zh', 'x'), [(a * 4 + b, b * 4 + a) for a in range(4...  20.6 us
    all_to_all x3, starting transfers between devices, exchange(): return lax.all_to_all(value, axes, 0, 0)  17.6 us
    all_to_all x1, blocking collectives, exchange(): return lax.all_to_all(value, axes, 0, 0)  15.7 us
    all_to_all x3, waiting for transfers between devices, exchange(): return lax.all_to_all(value, axes, 0, 0)  9.31 us
    ppermute x2, starting transfers between devices, turned(): lax.ppermute(value, ('zh', 'x'), [(a * 4 + b, b * 4 + a) for a in range(4...  8.53 us
    pallas_call x4, Pallas kernels, call(): pl.pallas_call(kernel, out_shape=out, in_specs=[smem if a.shape == (2,) e...  7.27 us
  transfers between devices with their start and end apart: 17, of which 9 were waited for; matrix products, arithmetic and copies ran while one was open for 4% of the time, Pallas kernels for 4%

profile of v6, /device:TPU:123, one launch (start us, length us, event | category | flops | bytes accessed | tf_op | source)
XLA Modules:
  0.0 175.3 jit_solution(13506464595052198743)
XLA Ops:
  7.9 0.9 copy-done
  8.9 1.0 copy-done.1
  11.2 1.0 shard_map.86
  12.3 6.1 %all-to-all-start = ((bf16[16,160,128]{2,1,0:T(8,128)(2,1)}), bf16[16,160,128]{2,1,0:T(8,128)(2,1)S(1)}, u32[]{:S(2)}, u32[]{:S(2)}) async-start(bf16[16,160,128]{2,1,0:T(8,128)(2,1)} %shard_map.86), calls=%async_computation | async-start | bytes 1310720 | tf_op jit(solution)/shard_map/all_to_all | solution.py:37
  18.5 9.3 %all-to-all-done.x_ref = bf16[16,160,128]{2,1,0:T(8,128)(2,1)S(1)} async-done(((bf16[16,160,128]{2,1,0:T(8,128)(2,1)}), bf16[16,160,128]{2,1,0:T(8,128)(2,1)S(1)}, u32[]{:S(2)}, u32[]{:S(2)}) %all-to-all-start) | async-done | bytes 655392 | tf_op jit(solution)/shard_map/all_to_all | solution.py:37
  28.3 15.7 %all_to_all.20 = bf16[16,160,128]{2,1,0:T(8,128)(2,1)S(1)} all-to-all(bf16[16,160,128]{2,1,0:T(8,128)(2,1)S(1)} %shard_map.87), channel_id=1, replica_groups=mesh['zh'=4,'y'=8,'x'=4,'zl'=2,'core'=2] {'x','zl','core'}, dimensions={0} | all-to-all | bytes 1310720 | tf_op jit(solution)/shard_map/all_to_all | solution.py:37
  44.7 6.6 %collective-permute-start = (bf16[192,256]{1,0:T(8,128)(2,1)S(1)}, bf16[192,256]{1,0:T(8,128)(2,1)S(1)}, u32[]{:S(2)}, u32[]{:S(2)}) collective-permute-start(bf16[192,256]{1,0:T(8,128)(2,1)S(1)} %clamp_convert_fusion), channel_id=1, source_target_pairs={{0,0},{4,128},{8,256},{12,384},{128,4},{132,132},{136,260},{140,38... | collective-permute-start | bytes 294920 | tf_op jit(solution)/shard_map/ppermute | solution.py:33
  51.4 4.1 %collective-permute-done = bf16[192,256]{1,0:T(8,128)(2,1)S(1)} collective-permute-done((bf16[192,256]{1,0:T(8,128)(2,1)S(1)}, bf16[192,256]{1,0:T(8,128)(2,1)S(1)}, u32[]{:S(2)}, u32[]{:S(2)}) %collective-permute-start) | collective-permute-done | bytes 98336 | tf_op jit(solution)/shard_map/ppermute | solution.py:33
  55.4 1.9 %collective-permute-start.4 = (bf16[14,96,128]{2,1,0:T(8,128)(2,1)S(1)}, bf16[14,96,128]{2,1,0:T(8,128)(2,1)S(1)}, u32[]{:S(2)}, u32[]{:S(2)}) collective-permute-start(bf16[14,96,128]{2,1,0:T(8,128)(2,1)S(1)} %slice.40.own_ref), channel_id=1, source_target_pairs={{0,128},{128,256},{256,384},{384,0},{1,129},{129,257},{257,385},{3... | collective-permute-start | bytes 1032200 | tf_op jit(solution)/shard_map/ppermute | solution.py:29
  57.3 11.3 %collective-permute-start.5 = (bf16[14,96,128]{2,1,0:T(8,128)(2,1)S(1)}, bf16[14,96,128]{2,1,0:T(8,128)(2,1)S(1)}, u32[]{:S(2)}, u32[]{:S(2)}) collective-permute-start(bf16[14,96,128]{2,1,0:T(8,128)(2,1)S(1)} %slice.40.own_ref), channel_id=1, source_target_pairs={{0,384},{128,0},{256,128},{384,256},{1,385},{129,1},{257,129},{385... | collective-permute-start | bytes 1032200 | tf_op jit(solution)/shard_map/ppermute | solution.py:29
  69.6 7.4 %all-to-all-start.2 = ((bf16[8,192,256]{2,1,0:T(8,128)(2,1)}), bf16[8,192,256]{2,1,0:T(8,128)(2,1)S(1)}, u32[]{:S(2)}, u32[]{:S(2)}) async-start(bf16[8,192,256]{2,1,0:T(8,128)(2,1)} %broadcast_in_dim.2), calls=%async_computation.2 | async-start | bytes 1572864 | tf_op jit(solution)/shard_map/all_to_all | solution.py:37
  77.4 1.9 %collective-permute-start.6 = (bf16[7,96,128]{2,1,0:T(8,128)(2,1)S(1)}, bf16[7,96,128]{2,1,0:T(8,128)(2,1)S(1)}, u32[]{:S(2)}, u32[]{:S(2)}) collective-permute-start(bf16[7,96,128]{2,1,0:T(8,128)(2,1)S(1)} %slice.42), channel_id=1, source_target_pairs={{0,128},{128,256},{256,384},{384,0},{1,129},{129,257},{257,385},{3... | collective-permute-start | bytes 516104 | tf_op jit(solution)/shard_map/ppermute | solution.py:29
  79.3 6.4 %collective-permute-done.5.next_ref = bf16[14,96,128]{2,1,0:T(8,128)(2,1)S(1)} collective-permute-done((bf16[14,96,128]{2,1,0:T(8,128)(2,1)S(1)}, bf16[14,96,128]{2,1,0:T(8,128)(2,1)S(1)}, u32[]{:S(2)}, u32[]{:S(2)}) %collective-permute-start.5) | collective-permute-done | bytes 344096 | tf_op jit(solution)/shard_map/ppermute | solution.py:29
  85.7 1.9 %collective-permute-start.7 = (bf16[7,96,128]{2,1,0:T(8,128)(2,1)S(1)}, bf16[7,96,128]{2,1,0:T(8,128)(2,1)S(1)}, u32[]{:S(2)}, u32[]{:S(2)}) collective-permute-start(bf16[7,96,128]{2,1,0:T(8,128)(2,1)S(1)} %slice.43), channel_id=1, source_target_pairs={{0,384},{128,0},{256,128},{384,256},{1,385},{129,1},{257,129},{385... | collective-permute-start | bytes 516104 | tf_op jit(solution)/shard_map/ppermute | solution.py:29
  87.8 13.8 %collective-permute-done.7.second_ref = bf16[7,96,128]{2,1,0:T(8,128)(2,1)S(1)} collective-permute-done((bf16[7,96,128]{2,1,0:T(8,128)(2,1)S(1)}, bf16[7,96,128]{2,1,0:T(8,128)(2,1)S(1)}, u32[]{:S(2)}, u32[]{:S(2)}) %collective-permute-start.7) | collective-permute-done | bytes 172064 | tf_op jit(solution)/shard_map/ppermute | solution.py:29
  101.5 1.5 copy-done.8
  103.0 3.1 %shard_map.89 = (bf16[8,192,256]{2,1,0:T(8,128)(2,1)S(1)}, bf16[8,192,256]{2,1,0:T(8,128)(2,1)}) custom-call(s32[2]{0:T(128)S(1)} %pad_add_fusion.place_ref, bf16[8,896,128]{2,1,0:T(8,128)(2,1)S(1)} %bitcast.5, bf16[14,96,128]{2,1,0:T(8,128)(2,1)S(1)} %slice.40.own_ref, bf16[14,96,128]{2,1,0:T(8,128)(2,1)S(1)} %collective-permute-done.4.prev_ref, ...), custom_call_target="tpu_custom_call" | custom-call | flops 1409286144 | bytes 2000000 | tf_op jit(solution)/shard_map/pallas_call | solution.py:59
  106.1 2.8 %collective-permute-start.8 = (bf16[8,192,256]{2,1,0:T(8,128)(2,1)}, bf16[8,192,256]{2,1,0:T(8,128)(2,1)}, u32[]{:S(2)}, u32[]{:S(2)}) collective-permute-start(bf16[8,192,256]{2,1,0:T(8,128)(2,1)} %get-tuple-element.21), channel_id=1, source_target_pairs={{0,1},{1,0},{2,3},{3,2},{4,5},{5,4},{6,7},{7,6},{8,9},{9,8},{10,11... | collective-permute-start | bytes 2359304 | tf_op jit(solution)/shard_map/ppermute | solution.py:41
  109.0 1.9 %collective-permute-start.1 = (bf16[8,192,256]{2,1,0:T(8,128)(2,1)S(1)}, bf16[8,192,256]{2,1,0:T(8,128)(2,1)S(1)}, u32[]{:S(2)}, u32[]{:S(2)}) collective-permute-start(bf16[8,192,256]{2,1,0:T(8,128)(2,1)S(1)} %all-to-all-done.2.grad_ref), channel_id=1, source_target_pairs={{0,1},{1,0},{2,3},{3,2},{4,5},{5,4},{6,7},{7,6},{8,9},{9,8},{10,11... | collective-permute-start | bytes 2359304 | tf_op jit(solution)/shard_map/ppermute | solution.py:41
  111.2 2.2 %add_convert_fusion = bf16[8,192,256]{2,1,0:T(8,128)(2,1)} fusion(bf16[8,192,256]{2,1,0:T(8,128)(2,1)} %collective-permute-done.8, bf16[8,192,256]{2,1,0:T(8,128)(2,1)S(1)} %get-tuple-element.20), kind=kLoop, calls=%fused_computation | loop fusion | flops 1572864 | bytes 2359296 | tf_op jit(solution)/shard_map/convert_element_type | solution.py:189
  113.4 4.2 %all-to-all-start.3 = ((bf16[8,192,256]{2,1,0:T(8,128)(2,1)}), bf16[8,192,256]{2,1,0:T(8,128)(2,1)}, u32[]{:S(2)}, u32[]{:S(2)}) async-start(bf16[8,192,256]{2,1,0:T(8,128)(2,1)} %add_convert_fusion), calls=%async_computation.3 | async-start | bytes 1572864 | tf_op jit(solution)/shard_map/all_to_all | solution.py:37
  117.6 1.5 copy-done.7
  119.1 2.7 %shard_map.88 = (bf16[192,896]{1,0:T(8,128)(2,1)S(1)}, bf16[192,896]{1,0:T(8,128)(2,1)S(1)}, bf16[192,896]{1,0:T(8,128)(2,1)S(1)}, f32[192,896]{1,0:T(8,128)S(1)}) custom-call(s32[2]{0:T(128)S(1)} %pad_add_fusion.place_ref, bf16[8,192,256]{2,1,0:T(8,128)(2,1)S(1)} %all-to-all-done.2.grad_ref, bf16[8,192,256]{2,1,0:T(8,128)(2,1)S(1)} %collective-permute-done.1.cross_ref, ...), custom_call_target="tpu_custom_call" | custom-call | flops 1409286144 | bytes 2000000 | tf_op jit(solution)/shard_map/pallas_call | solution.py:59
  121.8 5.3 %collective-permute-start.2 = (bf16[96,896]{1,0:T(8,128)(2,1)S(1)}, bf16[96,896]{1,0:T(8,128)(2,1)S(1)}, u32[]{:S(2)}, u32[]{:S(2)}) collective-permute-start(bf16[96,896]{1,0:T(8,128)(2,1)S(1)} %get-tuple-element.29), channel_id=1, source_target_pairs={{0,128},{128,256},{256,384},{384,0},{1,129},{129,257},{257,385},{3... | collective-permute-start | bytes 516104 | tf_op jit(solution)/shard_map/ppermute | solution.py:29
  127.1 2.1 %collective-permute-start.3 = (bf16[96,896]{1,0:T(8,128)(2,1)S(1)}, bf16[96,896]{1,0:T(8,128)(2,1)S(1)}, u32[]{:S(2)}, u32[]{:S(2)}) collective-permute-start(bf16[96,896]{1,0:T(8,128)(2,1)S(1)} %get-tuple-element.28), channel_id=1, source_target_pairs={{0,384},{128,0},{256,128},{384,256},{1,385},{129,1},{257,129},{385... | collective-permute-start | bytes 516104 | tf_op jit(solution)/shard_map/ppermute | solution.py:29
  129.3 4.4 %collective-permute-done.2 = bf16[96,896]{1,0:T(8,128)(2,1)S(1)} collective-permute-done((bf16[96,896]{1,0:T(8,128)(2,1)S(1)}, bf16[96,896]{1,0:T(8,128)(2,1)S(1)}, u32[]{:S(2)}, u32[]{:S(2)}) %collective-permute-start.2) | collective-permute-done | bytes 172064 | tf_op jit(solution)/shard_map/ppermute | solution.py:29
  133.7 5.7 %collective-permute-done.3 = bf16[96,896]{1,0:T(8,128)(2,1)S(1)} collective-permute-done((bf16[96,896]{1,0:T(8,128)(2,1)S(1)}, bf16[96,896]{1,0:T(8,128)(2,1)S(1)}, u32[]{:S(2)}, u32[]{:S(2)}) %collective-permute-start.3) | collective-permute-done | bytes 172064 | tf_op jit(solution)/shard_map/ppermute | solution.py:29
  139.5 2.0 %collective-permute-start.10 = (bf16[192,896]{1,0:T(8,128)(2,1)S(1)}, bf16[192,896]{1,0:T(8,128)(2,1)S(1)}, u32[]{:S(2)}, u32[]{:S(2)}) collective-permute-start(bf16[192,896]{1,0:T(8,128)(2,1)S(1)} %pad_maximum_fusion), channel_id=1, source_target_pairs={{0,128},{128,256},{256,384},{384,0},{1,129},{129,257},{257,385},{3... | collective-permute-start | bytes 1032200 | tf_op jit(solution)/shard_map/ppermute | solution.py:29
  141.6 5.4 %collective-permute-start.11 = (bf16[192,896]{1,0:T(8,128)(2,1)S(1)}, bf16[192,896]{1,0:T(8,128)(2,1)S(1)}, u32[]{:S(2)}, u32[]{:S(2)}) collective-permute-start(bf16[192,896]{1,0:T(8,128)(2,1)S(1)} %pad_maximum_fusion.1), channel_id=1, source_target_pairs={{0,384},{128,0},{256,128},{384,256},{1,385},{129,1},{257,129},{385... | collective-permute-start | bytes 1032200 | tf_op jit(solution)/shard_map/ppermute | solution.py:29
  147.0 1.2 reduce_sum.12
  148.2 1.9 %collective-permute-start.9 = (bf16[192,256]{1,0:T(8,128)(2,1)S(1)}, bf16[192,256]{1,0:T(8,128)(2,1)S(1)}, u32[]{:S(2)}, u32[]{:S(2)}) collective-permute-start(bf16[192,256]{1,0:T(8,128)(2,1)S(1)} %reduce_sum.12), channel_id=1, source_target_pairs={{0,0},{4,128},{8,256},{12,384},{128,4},{132,132},{136,260},{140,38... | collective-permute-start | bytes 294920 | tf_op jit(solution)/shard_map/ppermute | solution.py:33
  150.2 16.6 %collective-permute-done.9 = bf16[192,256]{1,0:T(8,128)(2,1)S(1)} collective-permute-done((bf16[192,256]{1,0:T(8,128)(2,1)S(1)}, bf16[192,256]{1,0:T(8,128)(2,1)S(1)}, u32[]{:S(2)}, u32[]{:S(2)}) %collective-permute-start.9) | collective-permute-done | bytes 98336 | tf_op jit(solution)/shard_map/ppermute | solution.py:33
  (52 shorter events, 7.1 us)
Async XLA Ops:
  7.2 20.6 %copy-start.2 = (bf16[128,128]{1,0:T(8,128)(2,1)S(1)}, bf16[128,128]{1,0:T(8,128)(2,1)}, u32[]{:S(2)}) copy-start(bf16[128,128]{1,0:T(8,128)(2,1)} %constant.25.clone.table_ref) | copy-start | bytes 98308
  7.2 11.2 %copy-start.10 = (s32[192]{0:T(256)S(1)}, s32[192]{0:T(256)}, u32[]{:S(2)}) copy-start(s32[192]{0:T(256)} %param.12) | copy-start | bytes 2308
  7.2 11.2 %copy-start.9 = (bf16[192,256]{1,0:T(8,128)(2,1)S(1)}, bf16[192,256]{1,0:T(8,128)(2,1)}, u32[]{:S(2)}) copy-start(bf16[192,256]{1,0:T(8,128)(2,1)} %param.9) | copy-start | bytes 294916
  7.2 94.3 %all-gather.7.cloned.1.call-start = ((), (), s32[]{:S(2)}) async-start(), calls=%async_computation.5 | async-start | bytes 2064384 | tf_op jit(solution)/shard_map/all_gather | solution.py:154
  7.9 0.9 copy-start
  8.9 1.0 copy-start.1
  9.8 0.7 copy-start.3
  10.5 0.7 copy-start.5
  12.3 15.6 %all-to-all-start = ((bf16[16,160,128]{2,1,0:T(8,128)(2,1)}), bf16[16,160,128]{2,1,0:T(8,128)(2,1)S(1)}, u32[]{:S(2)}, u32[]{:S(2)}) async-start(bf16[16,160,128]{2,1,0:T(8,128)(2,1)} %shard_map.86), calls=%async_computation | async-start | bytes 1310720 | tf_op jit(solution)/shard_map/all_to_all | solution.py:37
  18.3 99.3 %all-gather.5.cloned.1.call-start = ((), (), s32[]{:S(2)}) async-start(), calls=%async_computation.4 | async-start | bytes 2064384 | tf_op jit(solution)/shard_map/all_gather | solution.py:171
  44.7 10.7 %collective-permute-start = (bf16[192,256]{1,0:T(8,128)(2,1)S(1)}, bf16[192,256]{1,0:T(8,128)(2,1)S(1)}, u32[]{:S(2)}, u32[]{:S(2)}) collective-permute-start(bf16[192,256]{1,0:T(8,128)(2,1)S(1)} %clamp_convert_fusion), channel_id=1, source_target_pairs={{0,0},{4,128},{8,256},{12,384},{128,4},{132,132},{136,260},{140,38... | collective-permute-start | bytes 294920 | tf_op jit(solution)/shard_map/ppermute | solution.py:33
  55.4 21.9 %collective-permute-start.4 = (bf16[14,96,128]{2,1,0:T(8,128)(2,1)S(1)}, bf16[14,96,128]{2,1,0:T(8,128)(2,1)S(1)}, u32[]{:S(2)}, u32[]{:S(2)}) collective-permute-start(bf16[14,96,128]{2,1,0:T(8,128)(2,1)S(1)} %slice.40.own_ref), channel_id=1, source_target_pairs={{0,128},{128,256},{256,384},{384,0},{1,129},{129,257},{257,385},{3... | collective-permute-start | bytes 1032200 | tf_op jit(solution)/shard_map/ppermute | solution.py:29
  57.3 28.4 %collective-permute-start.5 = (bf16[14,96,128]{2,1,0:T(8,128)(2,1)S(1)}, bf16[14,96,128]{2,1,0:T(8,128)(2,1)S(1)}, u32[]{:S(2)}, u32[]{:S(2)}) collective-permute-start(bf16[14,96,128]{2,1,0:T(8,128)(2,1)S(1)} %slice.40.own_ref), channel_id=1, source_target_pairs={{0,384},{128,0},{256,128},{384,256},{1,385},{129,1},{257,129},{385... | collective-permute-start | bytes 1032200 | tf_op jit(solution)/shard_map/ppermute | solution.py:29
  69.6 39.4 %all-to-all-start.2 = ((bf16[8,192,256]{2,1,0:T(8,128)(2,1)}), bf16[8,192,256]{2,1,0:T(8,128)(2,1)S(1)}, u32[]{:S(2)}, u32[]{:S(2)}) async-start(bf16[8,192,256]{2,1,0:T(8,128)(2,1)} %broadcast_in_dim.2), calls=%async_computation.2 | async-start | bytes 1572864 | tf_op jit(solution)/shard_map/all_to_all | solution.py:37
  77.4 10.4 %collective-permute-start.6 = (bf16[7,96,128]{2,1,0:T(8,128)(2,1)S(1)}, bf16[7,96,128]{2,1,0:T(8,128)(2,1)S(1)}, u32[]{:S(2)}, u32[]{:S(2)}) collective-permute-start(bf16[7,96,128]{2,1,0:T(8,128)(2,1)S(1)} %slice.42), channel_id=1, source_target_pairs={{0,128},{128,256},{256,384},{384,0},{1,129},{129,257},{257,385},{3... | collective-permute-start | bytes 516104 | tf_op jit(solution)/shard_map/ppermute | solution.py:29
  85.7 15.8 %collective-permute-start.7 = (bf16[7,96,128]{2,1,0:T(8,128)(2,1)S(1)}, bf16[7,96,128]{2,1,0:T(8,128)(2,1)S(1)}, u32[]{:S(2)}, u32[]{:S(2)}) collective-permute-start(bf16[7,96,128]{2,1,0:T(8,128)(2,1)S(1)} %slice.43), channel_id=1, source_target_pairs={{0,384},{128,0},{256,128},{384,256},{1,385},{129,1},{257,129},{385... | collective-permute-start | bytes 516104 | tf_op jit(solution)/shard_map/ppermute | solution.py:29
  101.5 1.5 copy-start.8
  106.1 5.1 %collective-permute-start.8 = (bf16[8,192,256]{2,1,0:T(8,128)(2,1)}, bf16[8,192,256]{2,1,0:T(8,128)(2,1)}, u32[]{:S(2)}, u32[]{:S(2)}) collective-permute-start(bf16[8,192,256]{2,1,0:T(8,128)(2,1)} %get-tuple-element.21), channel_id=1, source_target_pairs={{0,1},{1,0},{2,3},{3,2},{4,5},{5,4},{6,7},{7,6},{8,9},{9,8},{10,11... | collective-permute-start | bytes 2359304 | tf_op jit(solution)/shard_map/ppermute | solution.py:41
  109.0 8.6 %collective-permute-start.1 = (bf16[8,192,256]{2,1,0:T(8,128)(2,1)S(1)}, bf16[8,192,256]{2,1,0:T(8,128)(2,1)S(1)}, u32[]{:S(2)}, u32[]{:S(2)}) collective-permute-start(bf16[8,192,256]{2,1,0:T(8,128)(2,1)S(1)} %all-to-all-done.2.grad_ref), channel_id=1, source_target_pairs={{0,1},{1,0},{2,3},{3,2},{4,5},{5,4},{6,7},{7,6},{8,9},{9,8},{10,11... | collective-permute-start | bytes 2359304 | tf_op jit(solution)/shard_map/ppermute | solution.py:41
  113.4 15.9 %all-to-all-start.3 = ((bf16[8,192,256]{2,1,0:T(8,128)(2,1)}), bf16[8,192,256]{2,1,0:T(8,128)(2,1)}, u32[]{:S(2)}, u32[]{:S(2)}) async-start(bf16[8,192,256]{2,1,0:T(8,128)(2,1)} %add_convert_fusion), calls=%async_computation.3 | async-start | bytes 1572864 | tf_op jit(solution)/shard_map/all_to_all | solution.py:37
  117.6 1.5 copy-start.7
  119.1 10.1 %copy-start.4 = (s32[896]{0:T(1024)S(1)}, s32[896]{0:T(1024)}, u32[]{:S(2)}) copy-start(s32[896]{0:T(1024)} %sign_ref.1) | copy-start | bytes 10756
  121.8 11.9 %collective-permute-start.2 = (bf16[96,896]{1,0:T(8,128)(2,1)S(1)}, bf16[96,896]{1,0:T(8,128)(2,1)S(1)}, u32[]{:S(2)}, u32[]{:S(2)}) collective-permute-start(bf16[96,896]{1,0:T(8,128)(2,1)S(1)} %get-tuple-element.29), channel_id=1, source_target_pairs={{0,128},{128,256},{256,384},{384,0},{1,129},{129,257},{257,385},{3... | collective-permute-start | bytes 516104 | tf_op jit(solution)/shard_map/ppermute | solution.py:29
  127.1 12.3 %collective-permute-start.3 = (bf16[96,896]{1,0:T(8,128)(2,1)S(1)}, bf16[96,896]{1,0:T(8,128)(2,1)S(1)}, u32[]{:S(2)}, u32[]{:S(2)}) collective-permute-start(bf16[96,896]{1,0:T(8,128)(2,1)S(1)} %get-tuple-element.28), channel_id=1, source_target_pairs={{0,384},{128,0},{256,128},{384,256},{1,385},{129,1},{257,129},{385... | collective-permute-start | bytes 516104 | tf_op jit(solution)/shard_map/ppermute | solution.py:29
  129.3 20.9 %copy-start.6 = (s32[192]{0:T(256)S(1)}, s32[192]{0:T(256)}, u32[]{:S(2)}) copy-start(s32[192]{0:T(256)} %exponent_ref.1) | copy-start | bytes 2308
  139.5 28.0 %collective-permute-start.10 = (bf16[192,896]{1,0:T(8,128)(2,1)S(1)}, bf16[192,896]{1,0:T(8,128)(2,1)S(1)}, u32[]{:S(2)}, u32[]{:S(2)}) collective-permute-start(bf16[192,896]{1,0:T(8,128)(2,1)S(1)} %pad_maximum_fusion), channel_id=1, source_target_pairs={{0,128},{128,256},{256,384},{384,0},{1,129},{129,257},{257,385},{3... | collective-permute-start | bytes 1032200 | tf_op jit(solution)/shard_map/ppermute | solution.py:29
  141.6 25.9 %collective-permute-start.11 = (bf16[192,896]{1,0:T(8,128)(2,1)S(1)}, bf16[192,896]{1,0:T(8,128)(2,1)S(1)}, u32[]{:S(2)}, u32[]{:S(2)}) collective-permute-start(bf16[192,896]{1,0:T(8,128)(2,1)S(1)} %pad_maximum_fusion.1), channel_id=1, source_target_pairs={{0,384},{128,0},{256,128},{384,256},{1,385},{129,1},{257,129},{385... | collective-permute-start | bytes 1032200 | tf_op jit(solution)/shard_map/ppermute | solution.py:29
  148.2 18.5 %collective-permute-start.9 = (bf16[192,256]{1,0:T(8,128)(2,1)S(1)}, bf16[192,256]{1,0:T(8,128)(2,1)S(1)}, u32[]{:S(2)}, u32[]{:S(2)}) collective-permute-start(bf16[192,256]{1,0:T(8,128)(2,1)S(1)} %reduce_sum.12), channel_id=1, source_target_pairs={{0,0},{4,128},{8,256},{12,384},{128,4},{132,132},{136,260},{140,38... | collective-permute-start | bytes 294920 | tf_op jit(solution)/shard_map/ppermute | solution.py:33
Sparse Core Ops, SparseCore 0:
  10.1 41.4 all-gather.6
  54.3 41.9 all-gather.4
